TPU v7x, 256 devices: a whole 4x4x8 slice. The times are simulated.
256 devices in a mesh: gz: 8 (over z), gy: 8 (over x, y_hi), gx: 4 (over y_lo, core).
Axes of the slice: x: 4, y: 4 (y_hi: 2, y_lo: 2; y = y_hi * 2 + y_lo), z: 8, core: 2. Of those that a mesh axis runs over, the one named last changes fastest.
Arguments:
- recorded: bfloat16 [6, 3072, 2, 8, 512], P(None, ('gz', 'gy'), None, None, 'gx'), may hold values from 0.19921875 to 2
- tile_place: int32 [6, 3072], replicated, may hold values from 0 to 1023, as said below
- psf: float32 [6, 3, 31], replicated, may hold values from 0.009 to 1
- estimate: float32 [128, 128, 512], P('gz', 'gy', 'gx'), may hold values from 0.34 to 2.81
Outputs:
- restored: float32 [128, 128, 512], P('gz', 'gy', 'gx')
Inputs may be any that keep to these rules, and one draw needn't show every extreme that they name: `tile_place`: tile j belongs to index j // 48 of gz+gy (gz slowest). For each view, the 48 tiles of one index name any block at most 2 times, and one block of each view is named exactly 2 times by the tiles of every index. Positions are below 16.
All inputs are finite; a program needn't handle non-finite values.
Results may differ from a plain program's by a relative error of at most 0.0009.
Values may be sent and summed in bfloat16 or wider, within the bound.
No kernel may reach another device: no remote copies, remote signals or barrier semaphores. Data moves between devices by JAX's collectives and lax.ppermute only.
A program may use at most 128 MiB of HBM per device.

v0:
```python
import functools

import jax
import jax.numpy as jnp
from jax import lax
from jax.experimental import pallas as pl
from jax.experimental.pallas import tpu as pltpu
from jax.sharding import PartitionSpec as P

background_level = 0.1
highest = lax.Precision.HIGHEST
capacity = 2
usual_slots = 56
smem = pl.BlockSpec(memory_space=pltpu.SMEM)
vmem = pl.BlockSpec(memory_space=pltpu.VMEM)


def neighbours(upward, downward, axis):
    devices = lax.axis_size(axis)
    even = lax.axis_index(axis) % 2 == 0
    first = jnp.where(even, upward, downward)
    second = jnp.where(even, downward, upward)
    bonds = [(i, i + 1) for i in range(devices - 1)]
    pairs = [[p for i, j in bonds[odd::2] for p in ((i, j), (j, i))] for odd in (0, 1)]
    return lax.ppermute(first, axis, pairs[0]), lax.ppermute(second, axis, pairs[1])


def from_sides(upward, downward, axis):
    even = lax.axis_index(axis) % 2 == 0
    first, second = neighbours(upward, downward, axis)
    return jnp.where(even, second, first), jnp.where(even, first, second)


def edges_kernel(value, last, first):
    rows, cols = last.shape
    groups = value.shape[0] // rows
    side = cols // groups
    group_of = lax.broadcasted_iota(jnp.int32, (rows, cols), 1) // side
    lasts = firsts = jnp.zeros((rows, cols), jnp.float32)
    for g in range(groups):
        block = value[g * rows : (g + 1) * rows].astype(jnp.float32)
        lasts = jnp.where(group_of == g, pltpu.roll(block, (g + 1) * side % cols, 1), lasts)
        firsts = jnp.where(group_of == g, pltpu.roll(block, g * side, 1), firsts)
    last[...] = lasts.astype(last.dtype)
    first[...] = firsts.astype(first.dtype)


def widen_kernel(value, before, after, wide):
    rows, cols = before.shape
    groups = value.shape[0] // rows
    side = cols // groups
    lane = lax.broadcasted_iota(jnp.int32, (rows, cols), 1)
    befores, afters = before[...].astype(jnp.float32), after[...].astype(jnp.float32)
    for g in range(groups):
        part = slice(g * rows, (g + 1) * rows)
        left = pltpu.roll(befores, (cols - g * side) % cols, 1)
        right = pltpu.roll(afters, (cols + side - g * side) % cols, 1)
        halo = jnp.where(lane < side, left, jnp.where(lane < 2 * side, right, 0.0))
        wide[part, :cols] = value[part]
        wide[part, cols:] = halo.astype(wide.dtype)


def with_columns(value, side):
    rows, cols = value.shape
    groups = cols // side
    packed = jax.ShapeDtypeStruct((rows // groups, cols), value.dtype)
    last, first = pl.pallas_call(
        edges_kernel,
        out_shape=[packed, packed],
        in_specs=[vmem],
        out_specs=[vmem, vmem],
        compiler_params=pltpu.CompilerParams(vmem_limit_bytes=32 << 20),
        name="edges",
    )(value)
    before, after = from_sides(last, first, "gx")
    return pl.pallas_call(
        widen_kernel,
        out_shape=jax.ShapeDtypeStruct((rows, 2 * cols), value.dtype),
        in_specs=[vmem] * 3,
        out_specs=vmem,
        compiler_params=pltpu.CompilerParams(vmem_limit_bytes=32 << 20),
        name="widen",
    )(value, before, after)


def taps_table(kernel_set, offset):
    taps = kernel_set.shape[-1]
    table = (offset[:, :, None] == jnp.arange(taps)[None, None, :]).astype(jnp.float32)
    return jnp.einsum("eim,vm->vei", table, kernel_set, precision=highest)


def slot_tables(tile_place, positions, chunks, usual):
    view_count = tile_place.shape[0]
    gz_count, gy_count = lax.axis_size("gz"), lax.axis_size("gy")
    my_gz, my_gy = lax.axis_index("gz"), lax.axis_index("gy")
    chunk = view_count // chunks
    placed = tile_place.reshape(view_count, gz_count, gy_count, -1)
    slot_count = placed.shape[-1]
    entries = view_count * slot_count
    group = lax.dynamic_index_in_dim(placed, my_gz, 1, keepdims=False)
    group = group.transpose(1, 0, 2).reshape(gy_count, entries)
    destination = group // positions
    dest_gy = destination % gy_count
    ahead = (destination // gy_count - my_gz) % gz_count
    view = jnp.arange(entries) // slot_count % chunk
    cell = (ahead * chunk + view) * positions + group % positions
    own_dest = lax.dynamic_index_in_dim(dest_gy, my_gy, 0, keepdims=True)
    sends = own_dest == jnp.arange(gy_count)[:, None]
    takes = dest_gy == my_gy
    number = jnp.broadcast_to(jnp.arange(entries)[None, :], takes.shape)
    chosen = jnp.stack([sends, takes])
    value = jnp.stack([number, cell])
    upto = (jnp.arange(entries)[:, None] <= jnp.arange(entries)[None, :]).astype(jnp.bfloat16)
    rank = jnp.dot(chosen.astype(jnp.bfloat16), upto, preferred_element_type=jnp.float32)
    rank = jnp.where(chosen, rank.astype(jnp.int32) - 1, -1)

    def table(first, lanes):
        hit = rank[..., None, :] == first + jnp.arange(lanes)[:, None]
        return jnp.sum(jnp.where(hit, value[..., None, :], 0), axis=-1).astype(jnp.int32)

    ends = [
        jnp.sum(takes[:, : c * chunk * slot_count], axis=-1).astype(jnp.int32)
        for c in range(chunks + 1)
    ]
    return table, jnp.stack(ends)


def most_slots(tile_place, positions):
    gy_count = lax.axis_size("gy")
    route_count = lax.axis_size(("gz", "gy"))
    dest_gy = (tile_place // positions) % gy_count
    dest_gy = dest_gy.reshape(tile_place.shape[0], route_count, 1, -1)
    return jnp.max(jnp.sum(dest_gy == jnp.arange(gy_count)[:, None], axis=(0, 3)))


def pack_kernel(source, tiles, outgoing):
    partners, lanes = outgoing.shape[:2]

    def one(partner, carry):
        for lane in range(lanes):
            outgoing[partner, lane] = tiles[source[partner, lane]]
        return carry

    lax.fori_loop(0, partners, one, 0)


def join_kernel(chunk, ends, cell, late_cell, arrived, late, *blocks_and_total):
    blocks, total = blocks_and_total[:-1], blocks_and_total[-1]
    partners, usual = arrived.shape[:2]
    step = 16

    def clear(index, carry):
        total[pl.ds(index * step, step)] = jnp.zeros((step,) + total.shape[1:], total.dtype)
        return carry

    lax.fori_loop(0, total.shape[0] // step, clear, 0)

    def add(cells, tiles, partner, lane):
        place = cells[partner, lane]
        total[place] = add_rounded(total[place], tiles[partner, lane])

    for partner in range(partners):
        first, last = ends[chunk, partner], ends[chunk + 1, partner]

        def add_usual(lane, carry):
            add(cell, arrived, partner, lane)
            return carry

        def add_late(lane, carry):
            add(late_cell, late, partner, lane - usual)
            return carry

        lax.fori_loop(jnp.minimum(first, usual), jnp.minimum(last, usual), add_usual, 0)
        lax.fori_loop(jnp.maximum(first, usual), jnp.maximum(last, usual), add_late, 0)
    start = 0
    for block in blocks:
        block[...] = total[start : start + block.shape[0]]
        start += block.shape[0]


def pack(source, tiles):
    return pl.pallas_call(
        pack_kernel,
        out_shape=jax.ShapeDtypeStruct(source.shape + tiles.shape[1:], tiles.dtype),
        in_specs=[smem, vmem],
        out_specs=vmem,
        compiler_params=pltpu.CompilerParams(vmem_limit_bytes=32 << 20),
        name="pack",
    )(source, tiles)


def join(chunk, ends, cell, late_cell, arrived, late, devices, cells):
    tile = arrived.shape[2:]
    half = devices // 2
    sizes = [cells] * half + [cells // 2] * 2 + [cells] * (half - 1)
    return pl.pallas_call(
        functools.partial(join_kernel, chunk),
        out_shape=[jax.ShapeDtypeStruct((size,) + tile, arrived.dtype) for size in sizes],
        in_specs=[smem, smem, smem, vmem, vmem],
        out_specs=[vmem] * len(sizes),
        scratch_shapes=[pltpu.VMEM((devices * cells,) + tile, arrived.dtype)],
        compiler_params=pltpu.CompilerParams(vmem_limit_bytes=32 << 20),
        name="join",
    )(ends, cell, late_cell, arrived, late)


def unwritten(shape, dtype):
    return pl.pallas_call(
        lambda out: None,
        out_shape=jax.ShapeDtypeStruct(shape, dtype),
        out_specs=pl.BlockSpec(memory_space=pl.ANY),
        name="unwritten",
    )()


def exchange(value):
    return lax.all_to_all(value, "gy", split_axis=0, concat_axis=0, tiled=True)


def add_rounded(left, right):
    return (left.astype(jnp.float32) + right.astype(jnp.float32)).astype(left.dtype)


def ring_step(upward, downward):
    devices = lax.axis_size("gz")
    up = [(i, (i + 1) % devices) for i in range(devices)]
    down = [(j, i) for i, j in up]
    return lax.ppermute(upward, "gz", up), lax.ppermute(downward, "gz", down)


def ring_sum(blocks, from_below, from_above):
    devices = len(blocks) - 1
    half = devices // 2
    middle = blocks[half].shape[0]
    for ahead in range(half - 1, 0, -1):
        upward, downward = blocks[ahead], blocks[devices - ahead + 1]
        if ahead == half - 1:
            upward = jnp.concatenate([add_rounded(upward[:middle], from_below), upward[middle:]])
            downward = jnp.concatenate(
                [downward[:middle], add_rounded(downward[middle:], from_above)]
            )
        else:
            upward = add_rounded(upward, from_below)
            downward = add_rounded(downward, from_above)
        from_below, from_above = ring_step(upward, downward)
    return (
        blocks[0].astype(jnp.float32)
        + from_below.astype(jnp.float32)
        + from_above.astype(jnp.float32)
    )


def on_device(recorded, tile_place, psf, estimate):
    view_count = recorded.shape[0]
    tile_depth, tile_rows = recorded.shape[2:4]
    depth, rows, cols = estimate.shape
    per_row = rows // tile_rows
    positions = depth // tile_depth * per_row
    area = depth * rows
    radius = (psf.shape[2] - 1) // 2
    side = 16
    tall, wide = depth + 2 * side, rows + 2 * side
    chunks = 2
    chunk = view_count // chunks
    gz_count, gy_count = lax.axis_size("gz"), lax.axis_size("gy")
    tiles = recorded.reshape(-1, tile_depth * tile_rows, cols)
    lanes = gz_count * capacity * view_count
    usual = min(usual_slots, lanes)
    table, ends = slot_tables(tile_place, positions, chunks, usual)
    usual_table = table(0, usual)

    def late_exchange():
        late_table = table(usual, lanes - usual)
        return exchange(pack(late_table[0], tiles)), late_table[1]

    def no_exchange():
        shape = (gy_count, lanes - usual)
        return unwritten(shape + tiles.shape[1:], tiles.dtype), jnp.zeros(shape, jnp.int32)

    late, late_cell = lax.cond(
        most_slots(tile_place, positions) > usual, late_exchange, no_exchange
    )
    usual_table, late_cell = lax.optimization_barrier((usual_table, late_cell))
    outgoing, psf = lax.optimization_barrier((pack(usual_table[0], tiles), psf))
    arrived = exchange(outgoing)
    own = estimate.astype(jnp.bfloat16)

    kernels = psf / jnp.sum(psf, axis=-1, keepdims=True)
    line = jnp.arange(area)
    place, inside = line // (tile_depth * tile_rows), line % (tile_depth * tile_rows)
    line_depth = place // per_row * tile_depth + inside // tile_rows
    line_row = place % per_row * tile_rows + inside % tile_rows
    reach = radius - side
    depth_taps = taps_table(kernels[:, 0], jnp.arange(tall)[:, None] - line_depth[None, :] + reach)
    row_taps = taps_table(kernels[:, 1], jnp.arange(wide)[:, None] - line_row[None, :] + reach)
    sheets = []
    for v in range(0, view_count, chunk):
        down = depth_taps[v : v + chunk].transpose(1, 0, 2).reshape(tall, 1, chunk * area)
        across = row_taps[v : v + chunk].transpose(1, 0, 2).reshape(1, wide, chunk * area)
        sheet = (down * across).astype(jnp.bfloat16)
        sheets.append(sheet.reshape(tall * wide, chunk * area))
    own, _ = lax.optimization_barrier((own, sheets))
    above, below = from_sides(own, own, "gz")
    own = jnp.concatenate([above, own, below], axis=0)
    blocks, near = [], []
    for c in range(chunks):
        blocks.append(
            join(c, ends, usual_table[1], late_cell, arrived, late, gz_count, chunk * positions)
        )
        near.append(ring_step(blocks[c][gz_count // 2], blocks[c][gz_count // 2 + 1]))
        near[c], arrived = lax.optimization_barrier((near[c], arrived))
    joined = [ring_sum(blocks[c], *near[c]) for c in range(chunks)]
    own, column_kernels, _ = lax.optimization_barrier((own, kernels[:, 2], blocks[-1][0]))
    above, below = from_sides(own, own, "gy")
    own = jnp.concatenate([above, own, below], axis=1)
    own = own.reshape(tall * wide, cols)
    column = jnp.concatenate(
        [jnp.arange(cols), jnp.arange(-side, 0), jnp.arange(cols, cols + side)]
        + [jnp.full(cols - 2 * side, -cols)]
    )
    offset = column[:, None] - jnp.arange(cols)[None, :]
    col_taps = taps_table(column_kernels, radius + offset).astype(jnp.bfloat16)
    col_taps_back = taps_table(column_kernels, radius - offset).astype(jnp.bfloat16)
    field = with_columns(own, side)
    total = jnp.zeros((tall * wide, cols), jnp.float32)
    for c in range(chunks):
        views = slice(c * chunk, (c + 1) * chunk)
        swept = lax.dot_general(
            sheets[c], field, (((0,), (0,)), ((), ())), preferred_element_type=jnp.float32
        )
        swept = swept.astype(jnp.bfloat16).reshape(chunk, area, -1)
        blurred = jnp.einsum(
            "vac,vck->vak", swept, col_taps[views], preferred_element_type=jnp.float32
        )
        ratio = joined[c].reshape(chunk, area, cols) / (blurred + background_level)
        ratio = ratio.astype(jnp.bfloat16).reshape(chunk * area, cols)
        ratio = with_columns(ratio, side).reshape(chunk, area, -1)
        spread = jnp.einsum(
            "vac,vck->vak", ratio, col_taps_back[views], preferred_element_type=jnp.float32
        )
        spread = spread.astype(jnp.bfloat16).reshape(chunk * area, cols)
        total = total + jnp.dot(sheets[c], spread, preferred_element_type=jnp.float32)
    total = total.reshape(tall, wide, cols)
    first, second = neighbours(
        total[side + depth :].astype(jnp.float16), total[:side].astype(jnp.float16), "gz"
    )
    total = total[side : side + depth] + first.astype(jnp.float32) + second.astype(jnp.float32)
    first, second = neighbours(
        total[:, side + rows :].astype(jnp.float16), total[:, :side].astype(jnp.float16), "gy"
    )
    result = total[:, side : side + rows] + first.astype(jnp.float32) + second.astype(jnp.float32)
    return estimate * result / view_count


def solution(mesh):
    placed = (P(None, ("gz", "gy"), None, None, "gx"), P(), P(), P("gz", "gy", "gx"))
    return jax.shard_map(
        on_device, mesh=mesh, in_specs=placed, out_specs=P("gz", "gy", "gx"), check_vma=False
    )
```

profile of v0, /device:TPU:106, one launch (start us, length us, event | category | flops | bytes accessed | tf_op | source)
XLA Modules:
  0.0 133.0 jit_solution(14661572325587364227)
XLA Ops:
  0.0 1.1 add_select_fusion
  1.1 1.0 reshape.561
  2.7 0.6 reduce_max.9
  4.1 0.5 copy-done.8
  4.8 0.4 select_reduce_fusion.1
  5.2 1.1 pack.3
  6.4 1.3 copy-done
  7.7 6.7 %all-to-all-start.1 = ((bf16[8,56,16,128]{3,2,1,0:T(8,128)(2,1)}), bf16[8,56,16,128]{3,2,1,0:T(8,128)(2,1)S(1)}, u32[]{:S(2)}, u32[]{:S(2)}) async-start(bf16[8,56,16,128]{3,2,1,0:T(8,128)(2,1)} %copy-done), calls=%async_computation.1 | async-start | bytes 3670016 | tf_op jit(solution)/shard_map/all_to_all | solution.py:217
  14.7 0.6 fusion.5
  15.5 0.6 fusion.4
  16.2 2.7 %multiply_convert_fusion.1 = bf16[48,48,768]{2,1,0:T(8,128)(2,1)} fusion(f32[48,768]{1,0:T(8,128)S(1)} %bitcast.109, f32[48,768]{1,0:T(8,128)S(1)} %bitcast.111), kind=kLoop, calls=%fused_computation.5 | loop fusion | flops 3538944 | bytes 3833856 | tf_op jit(solution)/shard_map/convert_element_type | solution.py:300
  18.9 2.7 %multiply_convert_fusion = bf16[48,48,768]{2,1,0:T(8,128)(2,1)} fusion(f32[48,768]{1,0:T(8,128)S(1)} %bitcast.108, f32[48,768]{1,0:T(8,128)S(1)} %bitcast.110), kind=kLoop, calls=%fused_computation.4 | loop fusion | flops 3538944 | bytes 3833856 | tf_op jit(solution)/shard_map/convert_element_type | solution.py:300
  21.7 5.9 %collective-permute-start.8 = (bf16[16,16,128]{2,1,0:T(8,128)(2,1)S(1)}, bf16[16,16,128]{2,1,0:T(8,128)(2,1)}, u32[]{:S(2)}, u32[]{:S(2)}) collective-permute-start(bf16[16,16,128]{2,1,0:T(8,128)(2,1)S(1)} %convert_element_type.249), channel_id=1, source_target_pairs={{32,64},{64,32},{96,128},{128,96},{160,192},{192,160},{33,65},{65,... | collective-permute-start | bytes 196616 | tf_op jit(solution)/shard_map/ppermute | solution.py:25
  27.9 0.3 convert_reduce_fusion.1
  28.1 0.8 fusion.23
  29.0 1.0 collective-permute-done.8
  30.0 0.9 broadcast_select_fusion.11
  30.8 8.4 %all-to-all-done.1.arrived = bf16[8,56,16,128]{3,2,1,0:T(8,128)(2,1)S(1)} async-done(((bf16[8,56,16,128]{3,2,1,0:T(8,128)(2,1)}), bf16[8,56,16,128]{3,2,1,0:T(8,128)(2,1)S(1)}, u32[]{:S(2)}, u32[]{:S(2)}) %all-to-all-start.1) | async-done | bytes 1835040 | tf_op jit(solution)/shard_map/all_to_all | solution.py:217
  39.3 2.8 %join.2 = (bf16[48,16,128]{2,1,0:T(8,128)(2,1)S(1)}, bf16[48,16,128]{2,1,0:T(8,128)(2,1)S(1)}, bf16[48,16,128]{2,1,0:T(8,128)(2,1)S(1)}, bf16[48,16,128]{2,1,0:T...) custom-call(s32[3,8]{1,0:T(4,128)S(1)} %pad_add_fusion.1.ends, ...), custom_call_target="tpu_custom_call" | custom-call | tf_op jit(solution)/shard_map/join/pallas_call | solution.py:196
  42.1 3.2 %collective-permute-start = (bf16[24,16,128]{2,1,0:T(8,128)(2,1)S(1)}, bf16[24,16,128]{2,1,0:T(8,128)(2,1)S(1)}, u32[]{:S(2)}, u32[]{:S(2)}) collective-permute-start(bf16[24,16,128]{2,1,0:T(8,128)(2,1)S(1)} %get-tuple-element.62), channel_id=1, source_target_pairs={{0,32},{32,64},{64,96},{96,128},{128,160},{160,192},{192,224},{224... | collective-permute-start | bytes 294920 | tf_op jit(solution)/shard_map/ppermute | solution.py:228
  45.3 2.1 %collective-permute-done = bf16[24,16,128]{2,1,0:T(8,128)(2,1)S(1)} collective-permute-done((bf16[24,16,128]{2,1,0:T(8,128)(2,1)S(1)}, bf16[24,16,128]{2,1,0:T(8,128)(2,1)S(1)}, u32[]{:S(2)}, u32[]{:S(2)}) %collective-permute-start) | collective-permute-done | bytes 98336 | tf_op jit(solution)/shard_map/ppermute | solution.py:228
  47.5 3.6 %collective-permute-done.1 = bf16[24,16,128]{2,1,0:T(8,128)(2,1)S(1)} collective-permute-done((bf16[24,16,128]{2,1,0:T(8,128)(2,1)S(1)}, bf16[24,16,128]{2,1,0:T(8,128)(2,1)S(1)}, u32[]{:S(2)}, u32[]{:S(2)}) %collective-permute-start.1) | collective-permute-done | bytes 98336 | tf_op jit(solution)/shard_map/ppermute | solution.py:228
  51.1 2.6 %join.3 = (bf16[48,16,128]{2,1,0:T(8,128)(2,1)S(1)}, bf16[48,16,128]{2,1,0:T(8,128)(2,1)S(1)}, bf16[48,16,128]{2,1,0:T(8,128)(2,1)S(1)}, bf16[48,16,128]{2,1,0:T...) custom-call(s32[3,8]{1,0:T(4,128)S(1)} %pad_add_fusion.1.ends, ...), custom_call_target="tpu_custom_call" | custom-call | tf_op jit(solution)/shard_map/join/pallas_call | solution.py:196
  53.7 1.8 %collective-permute-start.11 = (bf16[48,16,128]{2,1,0:T(8,128)(2,1)S(1)}, bf16[48,16,128]{2,1,0:T(8,128)(2,1)S(1)}, u32[]{:S(2)}, u32[]{:S(2)}) collective-permute-start(bf16[48,16,128]{2,1,0:T(8,128)(2,1)S(1)} %pad_maximum_fusion.3), channel_id=1, source_target_pairs={{0,4},{4,0},{8,12},{12,8},{16,20},{20,16},{24,28},{28,24},{1,5},{5... | collective-permute-start | bytes 589832 | tf_op jit(solution)/shard_map/ppermute | solution.py:25
  55.5 5.5 %collective-permute-start.10 = (bf16[48,16,128]{2,1,0:T(8,128)(2,1)S(1)}, bf16[48,16,128]{2,1,0:T(8,128)(2,1)S(1)}, u32[]{:S(2)}, u32[]{:S(2)}) collective-permute-start(bf16[48,16,128]{2,1,0:T(8,128)(2,1)S(1)} %pad_maximum_fusion.3), channel_id=1, source_target_pairs={{4,8},{8,4},{12,16},{16,12},{20,24},{24,20},{5,9},{9,5},{13,17},{1... | collective-permute-start | bytes 589832 | tf_op jit(solution)/shard_map/ppermute | solution.py:25
  61.2 3.3 %collective-permute-start.16 = (bf16[24,16,128]{2,1,0:T(8,128)(2,1)S(1)}, bf16[24,16,128]{2,1,0:T(8,128)(2,1)S(1)}, u32[]{:S(2)}, u32[]{:S(2)}) collective-permute-start(bf16[24,16,128]{2,1,0:T(8,128)(2,1)S(1)} %get-tuple-element.81), channel_id=1, source_target_pairs={{0,32},{32,64},{64,96},{96,128},{128,160},{160,192},{192,224},{224... | collective-permute-start | bytes 294920 | tf_op jit(solution)/shard_map/ppermute | solution.py:228
  64.5 1.4 %fusion.6 = bf16[6,256,128]{2,0,1:T(8,128)(2,1)S(1)} fusion(s32[256,128]{1,0:T(8,128)S(1)} %copy-done.6, f32[6,31]{1,0:T(8,128)S(1)} %slice_bitcast_fusion.2), kind=kOutput, calls=%fused_computation.19 | convolution fusion | flops 74350592 | bytes 525032 | tf_op jit(solution)/shard_map/eim,vm->vei/dot_general | solution.py:89
  65.9 0.2 fusion.62
  66.1 1.4 %fusion.7 = bf16[6,256,128]{2,0,1:T(8,128)(2,1)S(1)} fusion(s32[256,128]{1,0:T(8,128)S(1)} %copy-done.5, f32[6,31]{1,0:T(8,128)S(1)} %slice_bitcast_fusion.2), kind=kOutput, calls=%fused_computation.20 | convolution fusion | flops 74350592 | bytes 525032 | tf_op jit(solution)/shard_map/eim,vm->vei/dot_general | solution.py:89
  67.5 0.2 fusion.63
  67.7 3.3 %collective-permute-start.2 = (bf16[48,16,128]{2,1,0:T(8,128)(2,1)S(1)}, bf16[48,16,128]{2,1,0:T(8,128)(2,1)S(1)}, u32[]{:S(2)}, u32[]{:S(2)}) collective-permute-start(bf16[48,16,128]{2,1,0:T(8,128)(2,1)S(1)} %pad_maximum_fusion.1), channel_id=1, source_target_pairs={{0,32},{32,64},{64,96},{96,128},{128,160},{160,192},{192,224},{224... | collective-permute-start | bytes 589832 | tf_op jit(solution)/shard_map/ppermute | solution.py:228
  71.3 2.1 %collective-permute-start.21 = (bf16[48,16,128]{2,1,0:T(8,128)(2,1)S(1)}, bf16[48,16,128]{2,1,0:T(8,128)(2,1)S(1)}, u32[]{:S(2)}, u32[]{:S(2)}) collective-permute-start(bf16[48,16,128]{2,1,0:T(8,128)(2,1)S(1)} %pad_maximum_fusion.5), channel_id=1, source_target_pairs={{32,0},{64,32},{96,64},{128,96},{160,128},{192,160},{224,192},{0,2... | collective-permute-start | bytes 589832 | tf_op jit(solution)/shard_map/ppermute | solution.py:228
  73.6 0.3 edges.3
  74.2 3.2 %collective-permute-start.12 = (bf16[288,128]{1,0:T(8,128)(2,1)S(1)}, bf16[288,128]{1,0:T(8,128)(2,1)S(1)}, u32[]{:S(2)}, u32[]{:S(2)}) collective-permute-start(bf16[288,128]{1,0:T(8,128)(2,1)S(1)} %get-tuple-element.111), channel_id=1, source_target_pairs={{1,2},{2,1},{5,6},{6,5},{9,10},{10,9},{13,14},{14,13},{17,18},{18,... | collective-permute-start | bytes 221192 | tf_op jit(solution)/shard_map/ppermute | solution.py:25
  77.5 3.3 %collective-permute-start.3 = (bf16[48,16,128]{2,1,0:T(8,128)(2,1)S(1)}, bf16[48,16,128]{2,1,0:T(8,128)(2,1)S(1)}, u32[]{:S(2)}, u32[]{:S(2)}) collective-permute-start(bf16[48,16,128]{2,1,0:T(8,128)(2,1)S(1)} %add_convert_fusion.7), channel_id=1, source_target_pairs={{0,32},{32,64},{64,96},{96,128},{128,160},{160,192},{192,224},{224... | collective-permute-start | bytes 589832 | tf_op jit(solution)/shard_map/ppermute | solution.py:228
  80.8 0.4 widen.3
  81.3 1.1 convolution_convert_fusion
  82.4 0.9 copy-done.2
  83.3 1.1 convolution_convert_fusion.1
  84.4 0.2 convolution_add_fusion.2
  84.6 0.2 convolution_add_fusion.1
  85.0 2.8 %collective-permute-start.19 = (bf16[48,16,128]{2,1,0:T(8,128)(2,1)S(1)}, bf16[48,16,128]{2,1,0:T(8,128)(2,1)S(1)}, u32[]{:S(2)}, u32[]{:S(2)}) collective-permute-start(bf16[48,16,128]{2,1,0:T(8,128)(2,1)S(1)} %add_convert_fusion.3), channel_id=1, source_target_pairs={{0,32},{32,64},{64,96},{96,128},{128,160},{160,192},{192,224},{224... | collective-permute-start | bytes 589832 | tf_op jit(solution)/shard_map/ppermute | solution.py:228
  87.9 0.3 collective-permute-start.22
  88.4 3.3 %collective-permute-start.4 = (bf16[48,16,128]{2,1,0:T(8,128)(2,1)S(1)}, bf16[48,16,128]{2,1,0:T(8,128)(2,1)S(1)}, u32[]{:S(2)}, u32[]{:S(2)}) collective-permute-start(bf16[48,16,128]{2,1,0:T(8,128)(2,1)S(1)} %add_convert_fusion.6), channel_id=1, source_target_pairs={{0,32},{32,64},{64,96},{96,128},{128,160},{160,192},{192,224},{224... | collective-permute-start | bytes 589832 | tf_op jit(solution)/shard_map/ppermute | solution.py:228
  91.7 1.4 %collective-permute-done.19 = bf16[48,16,128]{2,1,0:T(8,128)(2,1)S(1)} collective-permute-done((bf16[48,16,128]{2,1,0:T(8,128)(2,1)S(1)}, bf16[48,16,128]{2,1,0:T(8,128)(2,1)S(1)}, u32[]{:S(2)}, u32[]{:S(2)}) %collective-permute-start.19) | collective-permute-done | bytes 196640 | tf_op jit(solution)/shard_map/ppermute | solution.py:228
  93.2 3.8 %collective-permute-start.20 = (bf16[48,16,128]{2,1,0:T(8,128)(2,1)S(1)}, bf16[48,16,128]{2,1,0:T(8,128)(2,1)S(1)}, u32[]{:S(2)}, u32[]{:S(2)}) collective-permute-start(bf16[48,16,128]{2,1,0:T(8,128)(2,1)S(1)} %add_convert_fusion.2), channel_id=1, source_target_pairs={{0,32},{32,64},{64,96},{96,128},{128,160},{160,192},{192,224},{224... | collective-permute-start | bytes 589832 | tf_op jit(solution)/shard_map/ppermute | solution.py:228
  96.9 0.2 collective-permute-done.7
  97.6 2.1 %collective-permute-start.14 = (bf16[96,128]{1,0:T(8,128)(2,1)S(1)}, bf16[96,128]{1,0:T(8,128)(2,1)S(1)}, u32[]{:S(2)}, u32[]{:S(2)}) collective-permute-start(bf16[96,128]{1,0:T(8,128)(2,1)S(1)} %get-tuple-element.121), channel_id=1, source_target_pairs={{1,2},{2,1},{5,6},{6,5},{9,10},{10,9},{13,14},{14,13},{17,18},{18,... | collective-permute-start | bytes 73736 | tf_op jit(solution)/shard_map/ppermute | solution.py:25
  99.8 1.1 collective-permute-start.23
  100.9 1.8 %collective-permute-done.14 = bf16[96,128]{1,0:T(8,128)(2,1)S(1)} collective-permute-done((bf16[96,128]{1,0:T(8,128)(2,1)S(1)}, bf16[96,128]{1,0:T(8,128)(2,1)S(1)}, u32[]{:S(2)}, u32[]{:S(2)}) %collective-permute-start.14) | collective-permute-done | bytes 24608 | tf_op jit(solution)/shard_map/ppermute | solution.py:25
  102.9 0.2 convolution_convert_fusion.3
  103.2 3.7 %collective-permute-done.23 = bf16[48,16,128]{2,1,0:T(8,128)(2,1)S(1)} collective-permute-done((bf16[48,16,128]{2,1,0:T(8,128)(2,1)S(1)}, bf16[48,16,128]{2,1,0:T(8,128)(2,1)S(1)}, u32[]{:S(2)}, u32[]{:S(2)}) %collective-permute-start.23) | collective-permute-done | bytes 196640 | tf_op jit(solution)/shard_map/ppermute | solution.py:228
  107.3 2.4 %collective-permute-start.24 = (bf16[96,128]{1,0:T(8,128)(2,1)S(1)}, bf16[96,128]{1,0:T(8,128)(2,1)S(1)}, u32[]{:S(2)}, u32[]{:S(2)}) collective-permute-start(bf16[96,128]{1,0:T(8,128)(2,1)S(1)} %get-tuple-element.117), channel_id=1, source_target_pairs={{1,2},{2,1},{5,6},{6,5},{9,10},{10,9},{13,14},{14,13},{17,18},{18,... | collective-permute-start | bytes 73736 | tf_op jit(solution)/shard_map/ppermute | solution.py:25
  109.7 1.1 fusion.67
  110.8 1.6 %collective-permute-done.24 = bf16[96,128]{1,0:T(8,128)(2,1)S(1)} collective-permute-done((bf16[96,128]{1,0:T(8,128)(2,1)S(1)}, bf16[96,128]{1,0:T(8,128)(2,1)S(1)}, u32[]{:S(2)}, u32[]{:S(2)}) %collective-permute-start.24) | collective-permute-done | bytes 24608 | tf_op jit(solution)/shard_map/ppermute | solution.py:25
  112.6 0.2 convolution_convert_fusion.2
  112.9 1.1 fusion.66
  114.1 3.7 %collective-permute-start.27 = (f16[16,48,128]{2,1,0:T(8,128)(2,1)S(1)}, f16[16,48,128]{2,1,0:T(8,128)(2,1)S(1)}, u32[]{:S(2)}, u32[]{:S(2)}) collective-permute-start(f16[16,48,128]{2,1,0:T(8,128)(2,1)S(1)} %bitcast.117), channel_id=1, source_target_pairs={{32,64},{64,32},{96,128},{128,96},{160,192},{192,160},{33,65},{65,... | collective-permute-start | bytes 589832 | tf_op jit(solution)/shard_map/ppermute | solution.py:25
  117.9 5.0 %collective-permute-done.27 = f16[16,48,128]{2,1,0:T(8,128)(2,1)S(1)} collective-permute-done((f16[16,48,128]{2,1,0:T(8,128)(2,1)S(1)}, f16[16,48,128]{2,1,0:T(8,128)(2,1)S(1)}, u32[]{:S(2)}, u32[]{:S(2)}) %collective-permute-start.27) | collective-permute-done | bytes 196640 | tf_op jit(solution)/shard_map/ppermute | solution.py:25
  122.9 0.6 collective-permute-done.26
  123.8 2.6 %collective-permute-start.29 = (f16[16,16,128]{2,1,0:T(8,128)(2,1)S(1)}, f16[16,16,128]{2,1,0:T(8,128)(2,1)S(1)}, u32[]{:S(2)}, u32[]{:S(2)}) collective-permute-start(f16[16,16,128]{2,1,0:T(8,128)(2,1)S(1)} %get-tuple-element.107), channel_id=1, source_target_pairs={{4,8},{8,4},{12,16},{16,12},{20,24},{24,20},{5,9},{9,5},{13,17},{1... | collective-permute-start | bytes 196616 | tf_op jit(solution)/shard_map/ppermute | solution.py:25
  126.4 3.1 %collective-permute-done.28 = f16[16,16,128]{2,1,0:T(8,128)(2,1)S(1)} collective-permute-done((f16[16,16,128]{2,1,0:T(8,128)(2,1)S(1)}, f16[16,16,128]{2,1,0:T(8,128)(2,1)S(1)}, u32[]{:S(2)}, u32[]{:S(2)}) %collective-permute-start.28) | collective-permute-done | bytes 65568 | tf_op jit(solution)/shard_map/ppermute | solution.py:25
  129.5 2.8 %collective-permute-done.29 = f16[16,16,128]{2,1,0:T(8,128)(2,1)S(1)} collective-permute-done((f16[16,16,128]{2,1,0:T(8,128)(2,1)S(1)}, f16[16,16,128]{2,1,0:T(8,128)(2,1)S(1)}, u32[]{:S(2)}, u32[]{:S(2)}) %collective-permute-start.29) | collective-permute-done | bytes 65568 | tf_op jit(solution)/shard_map/ppermute | solution.py:25
  132.3 0.7 fusion.22
  (129 shorter events, 4.9 us)
Async XLA Ops:
  0.0 5.2 %copy-start.3 = (bf16[6,48,2,8,128]{4,3,2,1,0:T(8,128)(2,1)S(1)}, bf16[6,48,2,8,128]{4,3,2,1,0:T(8,128)(2,1)}, u32[]{:S(2)}) copy-start(bf16[6,48,2,8,128]{4,3,2,1,0:T(8,128)(2,1)} %param.6) | copy-start | bytes 3538948
  4.0 0.6 copy-start.8
  6.3 1.3 copy-start
  7.7 6.7 %copy-start.4 = (f32[16,16,128]{2,1,0:T(8,128)S(1)}, f32[16,16,128]{2,1,0:T(8,128)}, u32[]{:S(2)}) copy-start(f32[16,16,128]{2,1,0:T(8,128)} %param.9) | copy-start | bytes 393220
  7.7 6.8 %copy-start.7 = (f32[6,3,31]{2,1,0:T(4,128)S(1)}, f32[6,3,31]{2,1,0:T(4,128)}, u32[]{:S(2)}) copy-start(f32[6,3,31]{2,1,0:T(4,128)} %param.8) | copy-start | bytes 6700
  7.7 31.6 %all-to-all-start.1 = ((bf16[8,56,16,128]{3,2,1,0:T(8,128)(2,1)}), bf16[8,56,16,128]{3,2,1,0:T(8,128)(2,1)S(1)}, u32[]{:S(2)}, u32[]{:S(2)}) async-start(bf16[8,56,16,128]{3,2,1,0:T(8,128)(2,1)} %copy-done), calls=%async_computation.1 | async-start | bytes 3670016 | tf_op jit(solution)/shard_map/all_to_all | solution.py:217
  18.9 8.9 %copy-start.9 = (s32[8,288]{1,0:T(8,128)S(1)}, s32[8,288]{1,0:T(8,128)}, u32[]{:S(2)}) copy-start(s32[8,288]{1,0:T(8,128)} %copy-done.8) | copy-start | bytes 27652
  21.6 7.4 %collective-permute-start.9 = (bf16[16,16,128]{2,1,0:T(8,128)(2,1)S(1)}, bf16[16,16,128]{2,1,0:T(8,128)(2,1)S(1)}, u32[]{:S(2)}, u32[]{:S(2)}) collective-permute-start(bf16[16,16,128]{2,1,0:T(8,128)(2,1)S(1)} %convert_element_type.249), channel_id=1, source_target_pairs={{0,32},{32,0},{64,96},{96,64},{128,160},{160,128},{192,224},{224,1... | collective-permute-start | bytes 196616 | tf_op jit(solution)/shard_map/ppermute | solution.py:25
  21.7 8.3 %collective-permute-start.8 = (bf16[16,16,128]{2,1,0:T(8,128)(2,1)S(1)}, bf16[16,16,128]{2,1,0:T(8,128)(2,1)}, u32[]{:S(2)}, u32[]{:S(2)}) collective-permute-start(bf16[16,16,128]{2,1,0:T(8,128)(2,1)S(1)} %convert_element_type.249), channel_id=1, source_target_pairs={{32,64},{64,32},{96,128},{128,96},{160,192},{192,160},{33,65},{65,... | collective-permute-start | bytes 196616 | tf_op jit(solution)/shard_map/ppermute | solution.py:25
  42.1 5.4 %collective-permute-start = (bf16[24,16,128]{2,1,0:T(8,128)(2,1)S(1)}, bf16[24,16,128]{2,1,0:T(8,128)(2,1)S(1)}, u32[]{:S(2)}, u32[]{:S(2)}) collective-permute-start(bf16[24,16,128]{2,1,0:T(8,128)(2,1)S(1)} %get-tuple-element.62), channel_id=1, source_target_pairs={{0,32},{32,64},{64,96},{96,128},{128,160},{160,192},{192,224},{224... | collective-permute-start | bytes 294920 | tf_op jit(solution)/shard_map/ppermute | solution.py:228
  45.2 5.8 %collective-permute-start.1 = (bf16[24,16,128]{2,1,0:T(8,128)(2,1)S(1)}, bf16[24,16,128]{2,1,0:T(8,128)(2,1)S(1)}, u32[]{:S(2)}, u32[]{:S(2)}) collective-permute-start(bf16[24,16,128]{2,1,0:T(8,128)(2,1)S(1)} %get-tuple-element.63), channel_id=1, source_target_pairs={{32,0},{64,32},{96,64},{128,96},{160,128},{192,160},{224,192},{0,2... | collective-permute-start | bytes 294920 | tf_op jit(solution)/shard_map/ppermute | solution.py:228
  45.3 19.2 %copy-start.6 = (s32[256,128]{1,0:T(8,128)S(1)}, s32[256,128]{1,0:T(8,128)}, u32[]{:S(2)}) copy-start(s32[256,128]{1,0:T(8,128)} %get-tuple-element.124) | copy-start | bytes 393220
  53.7 19.7 %collective-permute-start.11 = (bf16[48,16,128]{2,1,0:T(8,128)(2,1)S(1)}, bf16[48,16,128]{2,1,0:T(8,128)(2,1)S(1)}, u32[]{:S(2)}, u32[]{:S(2)}) collective-permute-start(bf16[48,16,128]{2,1,0:T(8,128)(2,1)S(1)} %pad_maximum_fusion.3), channel_id=1, source_target_pairs={{0,4},{4,0},{8,12},{12,8},{16,20},{20,16},{24,28},{28,24},{1,5},{5... | collective-permute-start | bytes 589832 | tf_op jit(solution)/shard_map/ppermute | solution.py:25
  55.5 18.0 %collective-permute-start.10 = (bf16[48,16,128]{2,1,0:T(8,128)(2,1)S(1)}, bf16[48,16,128]{2,1,0:T(8,128)(2,1)S(1)}, u32[]{:S(2)}, u32[]{:S(2)}) collective-permute-start(bf16[48,16,128]{2,1,0:T(8,128)(2,1)S(1)} %pad_maximum_fusion.3), channel_id=1, source_target_pairs={{4,8},{8,4},{12,16},{16,12},{20,24},{24,20},{5,9},{9,5},{13,17},{1... | collective-permute-start | bytes 589832 | tf_op jit(solution)/shard_map/ppermute | solution.py:25
  61.0 5.1 %copy-start.5 = (s32[256,128]{1,0:T(8,128)S(1)}, s32[256,128]{1,0:T(8,128)}, u32[]{:S(2)}) copy-start(s32[256,128]{1,0:T(8,128)} %get-tuple-element.125) | copy-start | bytes 393220
  61.1 10.2 %collective-permute-start.5 = (bf16[48,16,128]{2,1,0:T(8,128)(2,1)S(1)}, bf16[48,16,128]{2,1,0:T(8,128)(2,1)S(1)}, u32[]{:S(2)}, u32[]{:S(2)}) collective-permute-start(bf16[48,16,128]{2,1,0:T(8,128)(2,1)S(1)} %pad_maximum_fusion.2), channel_id=1, source_target_pairs={{32,0},{64,32},{96,64},{128,96},{160,128},{192,160},{224,192},{0,2... | collective-permute-start | bytes 589832 | tf_op jit(solution)/shard_map/ppermute | solution.py:228
  61.2 6.5 %collective-permute-start.16 = (bf16[24,16,128]{2,1,0:T(8,128)(2,1)S(1)}, bf16[24,16,128]{2,1,0:T(8,128)(2,1)S(1)}, u32[]{:S(2)}, u32[]{:S(2)}) collective-permute-start(bf16[24,16,128]{2,1,0:T(8,128)(2,1)S(1)} %get-tuple-element.81), channel_id=1, source_target_pairs={{0,32},{32,64},{64,96},{96,128},{128,160},{160,192},{192,224},{224... | collective-permute-start | bytes 294920 | tf_op jit(solution)/shard_map/ppermute | solution.py:228
  64.5 6.5 %collective-permute-start.17 = (bf16[24,16,128]{2,1,0:T(8,128)(2,1)S(1)}, bf16[24,16,128]{2,1,0:T(8,128)(2,1)S(1)}, u32[]{:S(2)}, u32[]{:S(2)}) collective-permute-start(bf16[24,16,128]{2,1,0:T(8,128)(2,1)S(1)} %get-tuple-element.82), channel_id=1, source_target_pairs={{32,0},{64,32},{96,64},{128,96},{160,128},{192,160},{224,192},{0,2... | collective-permute-start | bytes 294920 | tf_op jit(solution)/shard_map/ppermute | solution.py:228
  67.7 6.5 %collective-permute-start.2 = (bf16[48,16,128]{2,1,0:T(8,128)(2,1)S(1)}, bf16[48,16,128]{2,1,0:T(8,128)(2,1)S(1)}, u32[]{:S(2)}, u32[]{:S(2)}) collective-permute-start(bf16[48,16,128]{2,1,0:T(8,128)(2,1)S(1)} %pad_maximum_fusion.1), channel_id=1, source_target_pairs={{0,32},{32,64},{64,96},{96,128},{128,160},{160,192},{192,224},{224... | collective-permute-start | bytes 589832 | tf_op jit(solution)/shard_map/ppermute | solution.py:228
  71.1 13.8 %collective-permute-start.18 = (bf16[48,16,128]{2,1,0:T(8,128)(2,1)S(1)}, bf16[48,16,128]{2,1,0:T(8,128)(2,1)S(1)}, u32[]{:S(2)}, u32[]{:S(2)}) collective-permute-start(bf16[48,16,128]{2,1,0:T(8,128)(2,1)S(1)} %pad_maximum_fusion.4), channel_id=1, source_target_pairs={{0,32},{32,64},{64,96},{96,128},{128,160},{160,192},{192,224},{224... | collective-permute-start | bytes 589832 | tf_op jit(solution)/shard_map/ppermute | solution.py:228
  71.3 16.5 %collective-permute-start.21 = (bf16[48,16,128]{2,1,0:T(8,128)(2,1)S(1)}, bf16[48,16,128]{2,1,0:T(8,128)(2,1)S(1)}, u32[]{:S(2)}, u32[]{:S(2)}) collective-permute-start(bf16[48,16,128]{2,1,0:T(8,128)(2,1)S(1)} %pad_maximum_fusion.5), channel_id=1, source_target_pairs={{32,0},{64,32},{96,64},{128,96},{160,128},{192,160},{224,192},{0,2... | collective-permute-start | bytes 589832 | tf_op jit(solution)/shard_map/ppermute | solution.py:228
  73.4 14.8 %collective-permute-start.6 = (bf16[48,16,128]{2,1,0:T(8,128)(2,1)S(1)}, bf16[48,16,128]{2,1,0:T(8,128)(2,1)S(1)}, u32[]{:S(2)}, u32[]{:S(2)}) collective-permute-start(bf16[48,16,128]{2,1,0:T(8,128)(2,1)S(1)} %add_convert_fusion.5), channel_id=1, source_target_pairs={{32,0},{64,32},{96,64},{128,96},{160,128},{192,160},{224,192},{0,2... | collective-permute-start | bytes 589832 | tf_op jit(solution)/shard_map/ppermute | solution.py:228
  73.6 7.6 %copy-start.1 = (bf16[48,48,768]{2,1,0:T(8,128)(2,1)S(1)}, bf16[48,48,768]{2,1,0:T(8,128)(2,1)}, u32[]{:S(2)}) copy-start(bf16[48,48,768]{2,1,0:T(8,128)(2,1)} %multiply_convert_fusion) | copy-start | bytes 10616836
  74.0 3.5 %collective-permute-start.13 = (bf16[288,128]{1,0:T(8,128)(2,1)S(1)}, bf16[288,128]{1,0:T(8,128)(2,1)S(1)}, u32[]{:S(2)}, u32[]{:S(2)}) collective-permute-start(bf16[288,128]{1,0:T(8,128)(2,1)S(1)} %get-tuple-element.110), channel_id=1, source_target_pairs={{0,1},{1,0},{2,3},{3,2},{4,5},{5,4},{6,7},{7,6},{8,9},{9,8},{10,11... | collective-permute-start | bytes 221192 | tf_op jit(solution)/shard_map/ppermute | solution.py:25
  74.2 6.6 %collective-permute-start.12 = (bf16[288,128]{1,0:T(8,128)(2,1)S(1)}, bf16[288,128]{1,0:T(8,128)(2,1)S(1)}, u32[]{:S(2)}, u32[]{:S(2)}) collective-permute-start(bf16[288,128]{1,0:T(8,128)(2,1)S(1)} %get-tuple-element.111), channel_id=1, source_target_pairs={{1,2},{2,1},{5,6},{6,5},{9,10},{10,9},{13,14},{14,13},{17,18},{18,... | collective-permute-start | bytes 221192 | tf_op jit(solution)/shard_map/ppermute | solution.py:25
  77.5 10.8 %collective-permute-start.3 = (bf16[48,16,128]{2,1,0:T(8,128)(2,1)S(1)}, bf16[48,16,128]{2,1,0:T(8,128)(2,1)S(1)}, u32[]{:S(2)}, u32[]{:S(2)}) collective-permute-start(bf16[48,16,128]{2,1,0:T(8,128)(2,1)S(1)} %add_convert_fusion.7), channel_id=1, source_target_pairs={{0,32},{32,64},{64,96},{96,128},{128,160},{160,192},{192,224},{224... | collective-permute-start | bytes 589832 | tf_op jit(solution)/shard_map/ppermute | solution.py:228
  81.2 2.0 %copy-start.2 = (bf16[48,48,768]{2,1,0:T(8,128)(2,1)S(1)}, bf16[48,48,768]{2,1,0:T(8,128)(2,1)}, u32[]{:S(2)}) copy-start(bf16[48,48,768]{2,1,0:T(8,128)(2,1)} %multiply_convert_fusion.1) | copy-start | bytes 10616836
  85.0 8.1 %collective-permute-start.19 = (bf16[48,16,128]{2,1,0:T(8,128)(2,1)S(1)}, bf16[48,16,128]{2,1,0:T(8,128)(2,1)S(1)}, u32[]{:S(2)}, u32[]{:S(2)}) collective-permute-start(bf16[48,16,128]{2,1,0:T(8,128)(2,1)S(1)} %add_convert_fusion.3), channel_id=1, source_target_pairs={{0,32},{32,64},{64,96},{96,128},{128,160},{160,192},{192,224},{224... | collective-permute-start | bytes 589832 | tf_op jit(solution)/shard_map/ppermute | solution.py:228
  87.9 11.8 %collective-permute-start.22 = (bf16[48,16,128]{2,1,0:T(8,128)(2,1)S(1)}, bf16[48,16,128]{2,1,0:T(8,128)(2,1)S(1)}, u32[]{:S(2)}, u32[]{:S(2)}) collective-permute-start(bf16[48,16,128]{2,1,0:T(8,128)(2,1)S(1)} %add_convert_fusion.1), channel_id=1, source_target_pairs={{32,0},{64,32},{96,64},{128,96},{160,128},{192,160},{224,192},{0,2... | collective-permute-start | bytes 589832 | tf_op jit(solution)/shard_map/ppermute | solution.py:228
  88.2 8.9 %collective-permute-start.7 = (bf16[48,16,128]{2,1,0:T(8,128)(2,1)S(1)}, bf16[48,16,128]{2,1,0:T(8,128)(2,1)S(1)}, u32[]{:S(2)}, u32[]{:S(2)}) collective-permute-start(bf16[48,16,128]{2,1,0:T(8,128)(2,1)S(1)} %add_convert_fusion.4), channel_id=1, source_target_pairs={{32,0},{64,32},{96,64},{128,96},{160,128},{192,160},{224,192},{0,2... | collective-permute-start | bytes 589832 | tf_op jit(solution)/shard_map/ppermute | solution.py:228
  88.4 8.7 %collective-permute-start.4 = (bf16[48,16,128]{2,1,0:T(8,128)(2,1)S(1)}, bf16[48,16,128]{2,1,0:T(8,128)(2,1)S(1)}, u32[]{:S(2)}, u32[]{:S(2)}) collective-permute-start(bf16[48,16,128]{2,1,0:T(8,128)(2,1)S(1)} %add_convert_fusion.6), channel_id=1, source_target_pairs={{0,32},{32,64},{64,96},{96,128},{128,160},{160,192},{192,224},{224... | collective-permute-start | bytes 589832 | tf_op jit(solution)/shard_map/ppermute | solution.py:228
  93.2 10.0 %collective-permute-start.20 = (bf16[48,16,128]{2,1,0:T(8,128)(2,1)S(1)}, bf16[48,16,128]{2,1,0:T(8,128)(2,1)S(1)}, u32[]{:S(2)}, u32[]{:S(2)}) collective-permute-start(bf16[48,16,128]{2,1,0:T(8,128)(2,1)S(1)} %add_convert_fusion.2), channel_id=1, source_target_pairs={{0,32},{32,64},{64,96},{96,128},{128,160},{160,192},{192,224},{224... | collective-permute-start | bytes 589832 | tf_op jit(solution)/shard_map/ppermute | solution.py:228
  97.5 3.4 %collective-permute-start.15 = (bf16[96,128]{1,0:T(8,128)(2,1)S(1)}, bf16[96,128]{1,0:T(8,128)(2,1)S(1)}, u32[]{:S(2)}, u32[]{:S(2)}) collective-permute-start(bf16[96,128]{1,0:T(8,128)(2,1)S(1)} %get-tuple-element.120), channel_id=1, source_target_pairs={{0,1},{1,0},{2,3},{3,2},{4,5},{5,4},{6,7},{7,6},{8,9},{9,8},{10,11... | collective-permute-start | bytes 73736 | tf_op jit(solution)/shard_map/ppermute | solution.py:25
  97.6 5.1 %collective-permute-start.14 = (bf16[96,128]{1,0:T(8,128)(2,1)S(1)}, bf16[96,128]{1,0:T(8,128)(2,1)S(1)}, u32[]{:S(2)}, u32[]{:S(2)}) collective-permute-start(bf16[96,128]{1,0:T(8,128)(2,1)S(1)} %get-tuple-element.121), channel_id=1, source_target_pairs={{1,2},{2,1},{5,6},{6,5},{9,10},{10,9},{13,14},{14,13},{17,18},{18,... | collective-permute-start | bytes 73736 | tf_op jit(solution)/shard_map/ppermute | solution.py:25
  99.8 7.1 %collective-permute-start.23 = (bf16[48,16,128]{2,1,0:T(8,128)(2,1)S(1)}, bf16[48,16,128]{2,1,0:T(8,128)(2,1)S(1)}, u32[]{:S(2)}, u32[]{:S(2)}) collective-permute-start(bf16[48,16,128]{2,1,0:T(8,128)(2,1)S(1)} %add_convert_fusion), channel_id=1, source_target_pairs={{32,0},{64,32},{96,64},{128,96},{160,128},{192,160},{224,192},{0,2... | collective-permute-start | bytes 589832 | tf_op jit(solution)/shard_map/ppermute | solution.py:228
  107.2 3.6 %collective-permute-start.25 = (bf16[96,128]{1,0:T(8,128)(2,1)S(1)}, bf16[96,128]{1,0:T(8,128)(2,1)S(1)}, u32[]{:S(2)}, u32[]{:S(2)}) collective-permute-start(bf16[96,128]{1,0:T(8,128)(2,1)S(1)} %get-tuple-element.116), channel_id=1, source_target_pairs={{0,1},{1,0},{2,3},{3,2},{4,5},{5,4},{6,7},{7,6},{8,9},{9,8},{10,11... | collective-permute-start | bytes 73736 | tf_op jit(solution)/shard_map/ppermute | solution.py:25
  107.3 5.1 %collective-permute-start.24 = (bf16[96,128]{1,0:T(8,128)(2,1)S(1)}, bf16[96,128]{1,0:T(8,128)(2,1)S(1)}, u32[]{:S(2)}, u32[]{:S(2)}) collective-permute-start(bf16[96,128]{1,0:T(8,128)(2,1)S(1)} %get-tuple-element.117), channel_id=1, source_target_pairs={{1,2},{2,1},{5,6},{6,5},{9,10},{10,9},{13,14},{14,13},{17,18},{18,... | collective-permute-start | bytes 73736 | tf_op jit(solution)/shard_map/ppermute | solution.py:25
  114.1 8.8 %collective-permute-start.27 = (f16[16,48,128]{2,1,0:T(8,128)(2,1)S(1)}, f16[16,48,128]{2,1,0:T(8,128)(2,1)S(1)}, u32[]{:S(2)}, u32[]{:S(2)}) collective-permute-start(f16[16,48,128]{2,1,0:T(8,128)(2,1)S(1)} %bitcast.117), channel_id=1, source_target_pairs={{32,64},{64,32},{96,128},{128,96},{160,192},{192,160},{33,65},{65,... | collective-permute-start | bytes 589832 | tf_op jit(solution)/shard_map/ppermute | solution.py:25
  117.8 5.8 %collective-permute-start.26 = (f16[16,48,128]{2,1,0:T(8,128)(2,1)S(1)}, f16[16,48,128]{2,1,0:T(8,128)(2,1)S(1)}, u32[]{:S(2)}, u32[]{:S(2)}) collective-permute-start(f16[16,48,128]{2,1,0:T(8,128)(2,1)S(1)} %bitcast.116), channel_id=1, source_target_pairs={{0,32},{32,0},{64,96},{96,64},{128,160},{160,128},{192,224},{224,1... | collective-permute-start | bytes 589832 | tf_op jit(solution)/shard_map/ppermute | solution.py:25
  123.7 5.9 %collective-permute-start.28 = (f16[16,16,128]{2,1,0:T(8,128)(2,1)S(1)}, f16[16,16,128]{2,1,0:T(8,128)(2,1)S(1)}, u32[]{:S(2)}, u32[]{:S(2)}) collective-permute-start(f16[16,16,128]{2,1,0:T(8,128)(2,1)S(1)} %get-tuple-element.106), channel_id=1, source_target_pairs={{0,4},{4,0},{8,12},{12,8},{16,20},{20,16},{24,28},{28,24},{1,5},{5... | collective-permute-start | bytes 196616 | tf_op jit(solution)/shard_map/ppermute | solution.py:25
  123.8 8.6 %collective-permute-start.29 = (f16[16,16,128]{2,1,0:T(8,128)(2,1)S(1)}, f16[16,16,128]{2,1,0:T(8,128)(2,1)S(1)}, u32[]{:S(2)}, u32[]{:S(2)}) collective-permute-start(f16[16,16,128]{2,1,0:T(8,128)(2,1)S(1)} %get-tuple-element.107), channel_id=1, source_target_pairs={{4,8},{8,4},{12,16},{16,12},{20,24},{24,20},{5,9},{9,5},{13,17},{1... | collective-permute-start | bytes 196616 | tf_op jit(solution)/shard_map/ppermute | solution.py:25
where the time goes:
time: 135 us; the launch traced here: 133 us
  starting transfers between devices  61.3 us (45%)
  waiting for transfers between devices  35.7 us (26%)
  other arithmetic  12.1 us (9%)
  matrix products  9.52 us (7%)
  Pallas kernels  7.89 us (6%)
  local copies, waits for them, and re-layouts  4.95 us (4%)
  between operations  1.57 us (1%)
    ppermute x16, starting transfers between devices, ring_step(): return (lax.ppermute(upward, 'gz', up), lax.ppermute(downward, 'gz', down))  26.8 us
    ppermute x7, starting transfers between devices, neighbours(): lax.ppermute(second, axis, pairs[1])  25.4 us
    ppermute x7, waiting for transfers between devices, neighbours(): lax.ppermute(second, axis, pairs[1])  12.2 us
    ppermute x16, waiting for transfers between devices, ring_step(): return (lax.ppermute(upward, 'gz', up), lax.ppermute(downward, 'gz', down))  11.3 us
    all_to_all x1, waiting for transfers between devices, exchange(): return lax.all_to_all(value, 'gy', split_axis=0, concat_axis=0, tiled=True)  8.43 us
    all_to_all x1, starting transfers between devices, exchange(): return lax.all_to_all(value, 'gy', split_axis=0, concat_axis=0, tiled=True)  6.69 us
    pallas_call x2, Pallas kernels, join(): pl.pallas_call(functools.partial(join_kernel, chunk), out_shape=[jax.Shap...  5.4 us
    convert_element_type x2, other arithmetic, on_device(): sheet = (down * across).astype(jnp.bfloat16)  5.35 us
  transfers between devices with their start and end apart: 31, of which 14 were waited for; matrix products, arithmetic and copies ran while one was open for 13% of the time, Pallas kernels for 1%

commit v1 on v0

--- a/solution.py
+++ b/solution.py
@@ -25,9 +25,8 @@
     return lax.ppermute(first, axis, pairs[0]), lax.ppermute(second, axis, pairs[1])
 
 
-def from_sides(upward, downward, axis):
+def order_sides(first, second, axis):
     even = lax.axis_index(axis) % 2 == 0
-    first, second = neighbours(upward, downward, axis)
     return jnp.where(even, second, first), jnp.where(even, first, second)
 
 
@@ -72,7 +71,7 @@
         compiler_params=pltpu.CompilerParams(vmem_limit_bytes=32 << 20),
         name="edges",
     )(value)
-    before, after = from_sides(last, first, "gx")
+    before, after = order_sides(*neighbours(last, first, "gx"), "gx")
     return pl.pallas_call(
         widen_kernel,
         out_shape=jax.ShapeDtypeStruct((rows, 2 * cols), value.dtype),
@@ -228,9 +227,10 @@
     return lax.ppermute(upward, "gz", up), lax.ppermute(downward, "gz", down)
 
 
-def ring_sum(blocks, from_below, from_above):
+def ring_sum(blocks):
     devices = len(blocks) - 1
     half = devices // 2
+    from_below, from_above = ring_step(blocks[half], blocks[half + 1])
     middle = blocks[half].shape[0]
     for ahead in range(half - 1, 0, -1):
         upward, downward = blocks[ahead], blocks[devices - ahead + 1]
@@ -266,6 +266,8 @@
     tiles = recorded.reshape(-1, tile_depth * tile_rows, cols)
     lanes = gz_count * capacity * view_count
     usual = min(usual_slots, lanes)
+    own = estimate.astype(jnp.bfloat16)
+    own_rows = neighbours(own, own, "gy")
     table, ends = slot_tables(tile_place, positions, chunks, usual)
     usual_table = table(0, usual)
 
@@ -281,9 +283,9 @@
         most_slots(tile_place, positions) > usual, late_exchange, no_exchange
     )
     usual_table, late_cell = lax.optimization_barrier((usual_table, late_cell))
-    outgoing, psf = lax.optimization_barrier((pack(usual_table[0], tiles), psf))
+    outgoing = pack(usual_table[0], tiles)
+    outgoing, psf, own_rows = lax.optimization_barrier((outgoing, psf, own_rows))
     arrived = exchange(outgoing)
-    own = estimate.astype(jnp.bfloat16)
 
     kernels = psf / jnp.sum(psf, axis=-1, keepdims=True)
     line = jnp.arange(area)
@@ -299,40 +301,42 @@
         across = row_taps[v : v + chunk].transpose(1, 0, 2).reshape(1, wide, chunk * area)
         sheet = (down * across).astype(jnp.bfloat16)
         sheets.append(sheet.reshape(tall * wide, chunk * area))
-    own, _ = lax.optimization_barrier((own, sheets))
-    above, below = from_sides(own, own, "gz")
+    above, below = order_sides(*own_rows, "gy")
+    own = jnp.concatenate([above, own, below], axis=1)
+    above, below = order_sides(*neighbours(own, own, "gz"), "gz")
     own = jnp.concatenate([above, own, below], axis=0)
-    blocks, near = [], []
-    for c in range(chunks):
-        blocks.append(
-            join(c, ends, usual_table[1], late_cell, arrived, late, gz_count, chunk * positions)
-        )
-        near.append(ring_step(blocks[c][gz_count // 2], blocks[c][gz_count // 2 + 1]))
-        near[c], arrived = lax.optimization_barrier((near[c], arrived))
-    joined = [ring_sum(blocks[c], *near[c]) for c in range(chunks)]
-    own, column_kernels, _ = lax.optimization_barrier((own, kernels[:, 2], blocks[-1][0]))
-    above, below = from_sides(own, own, "gy")
-    own = jnp.concatenate([above, own, below], axis=1)
     own = own.reshape(tall * wide, cols)
     column = jnp.concatenate(
         [jnp.arange(cols), jnp.arange(-side, 0), jnp.arange(cols, cols + side)]
         + [jnp.full(cols - 2 * side, -cols)]
     )
     offset = column[:, None] - jnp.arange(cols)[None, :]
-    col_taps = taps_table(column_kernels, radius + offset).astype(jnp.bfloat16)
-    col_taps_back = taps_table(column_kernels, radius - offset).astype(jnp.bfloat16)
+    col_taps = taps_table(kernels[:, 2], radius + offset).astype(jnp.bfloat16)
+    col_taps_back = taps_table(kernels[:, 2], radius - offset).astype(jnp.bfloat16)
     field = with_columns(own, side)
-    total = jnp.zeros((tall * wide, cols), jnp.float32)
+    blurred = []
     for c in range(chunks):
-        views = slice(c * chunk, (c + 1) * chunk)
         swept = lax.dot_general(
             sheets[c], field, (((0,), (0,)), ((), ())), preferred_element_type=jnp.float32
         )
         swept = swept.astype(jnp.bfloat16).reshape(chunk, area, -1)
-        blurred = jnp.einsum(
-            "vac,vck->vak", swept, col_taps[views], preferred_element_type=jnp.float32
+        blurred.append(
+            jnp.einsum(
+                "vac,vck->vak",
+                swept,
+                col_taps[c * chunk : (c + 1) * chunk],
+                preferred_element_type=jnp.float32,
+            )
         )
-        ratio = joined[c].reshape(chunk, area, cols) / (blurred + background_level)
+    arrived, blurred = lax.optimization_barrier((arrived, blurred))
+    joined = []
+    for c in range(chunks):
+        blocks = join(c, ends, usual_table[1], late_cell, arrived, late, gz_count, chunk * positions)
+        joined.append(ring_sum(blocks))
+    total = jnp.zeros((tall * wide, cols), jnp.float32)
+    for c in range(chunks):
+        views = slice(c * chunk, (c + 1) * chunk)
+        ratio = joined[c].reshape(chunk, area, cols) / (blurred[c] + background_level)
         ratio = ratio.astype(jnp.bfloat16).reshape(chunk * area, cols)
         ratio = with_columns(ratio, side).reshape(chunk, area, -1)
         spread = jnp.einsum(

time: 135 us -> 128 us (0.948)
  waiting for transfers between devices: 35.7 us -> 24 us
  starting transfers between devices: 61.3 us -> 65.2 us
  matrix products: 9.52 us -> 12.8 us
    all_to_all x1, waiting for transfers between devices: 8.43 us -> 0.01 us  [exchange(): return lax.all_to_all(value, 'gy', split_axis=0, concat_axis=0, tiled=True)]
    ppermute x16, waiting for transfers between devices: 11.3 us -> 4.9 us  [ring_step(): return (lax.ppermute(upward, 'gz', up), lax.ppermute(downward, 'gz', down))]
    convert_element_type x2, other arithmetic: 5.35 us -> 1.86 us  [on_device(): sheet = (down * across).astype(jnp.bfloat16)]
    ppermute x7, waiting for transfers between devices: 12.2 us -> 14.9 us  [neighbours(): lax.ppermute(second, axis, pairs[1])]
    ppermute x7, starting transfers between devices: 25.4 us -> 27.9 us  [neighbours(): lax.ppermute(second, axis, pairs[1])]
    dot_general x4, matrix products: 3.96 us -> 6.41 us  [taps_table(): return jnp.einsum('eim,vm->vei', table, kernel_set, precision=highest)]
    ppermute x7, starting transfers between devices: 2.39 us -> 4.1 us  [neighbours(): lax.ppermute(first, axis, pairs[0])]
    unnamed x24 -> x44, local copies, waits for them, and re-layouts: 2.82 us -> 2.81 us
  transfers between devices with their start and end apart: 31 -> 31, of which waited for: 14 -> 12; matrix products, arithmetic and copies ran while one was open for 13% -> 18% of each run, Pallas kernels for 1% -> 4%
where the time goes in v1:
time: 128 us; the launch traced here: 127 us
  starting transfers between devices  65.2 us (51%)
  waiting for transfers between devices  24 us (19%)
  matrix products  12.8 us (10%)
  other arithmetic  11.1 us (9%)
  Pallas kernels  7.48 us (6%)
  local copies, waits for them, and re-layouts  4.93 us (4%)
  between operations  1.72 us (1%)
    ppermute x7, starting transfers between devices, neighbours(): lax.ppermute(second, axis, pairs[1])  27.9 us
    ppermute x16, starting transfers between devices, ring_step(): return (lax.ppermute(upward, 'gz', up), lax.ppermute(downward, 'gz', down))  25.9 us
    ppermute x7, waiting for transfers between devices, neighbours(): lax.ppermute(second, axis, pairs[1])  14.9 us
    all_to_all x1, starting transfers between devices, exchange(): return lax.all_to_all(value, 'gy', split_axis=0, concat_axis=0, tiled=True)  7.22 us
    dot_general x4, matrix products, taps_table(): return jnp.einsum('eim,vm->vei', table, kernel_set, precision=highest)  6.41 us
    pallas_call x2, Pallas kernels, join(): pl.pallas_call(functools.partial(join_kernel, chunk), out_shape=[jax.Shap...  4.99 us
    ppermute x16, waiting for transfers between devices, ring_step(): return (lax.ppermute(upward, 'gz', up), lax.ppermute(downward, 'gz', down))  4.9 us
    ppermute x7, waiting for transfers between devices, neighbours(): lax.ppermute(first, axis, pairs[0])  4.2 us
  transfers between devices with their start and end apart: 31, of which 12 were waited for; matrix products, arithmetic and copies ran while one was open for 18% of the time, Pallas kernels for 4%

profile of v1, /device:TPU:106, one launch (start us, length us, event | category | flops | bytes accessed | tf_op | source)
XLA Modules:
  0.0 127.2 jit_solution(17125327420881524754)
XLA Ops:
  0.0 1.0 convert_element_type.224
  1.0 2.4 %collective-permute-start = (bf16[16,16,128]{2,1,0:T(8,128)(2,1)S(1)}, bf16[16,16,128]{2,1,0:T(8,128)(2,1)S(1)}, u32[]{:S(2)}, u32[]{:S(2)}) collective-permute-start(bf16[16,16,128]{2,1,0:T(8,128)(2,1)S(1)} %convert_element_type.224), channel_id=1, source_target_pairs={{0,4},{4,0},{8,12},{12,8},{16,20},{20,16},{24,28},{28,24},{1,5},{5... | collective-permute-start | bytes 196616 | tf_op jit(solution)/shard_map/ppermute | solution.py:25
  3.4 3.1 %collective-permute-start.1 = (bf16[16,16,128]{2,1,0:T(8,128)(2,1)S(1)}, bf16[16,16,128]{2,1,0:T(8,128)(2,1)S(1)}, u32[]{:S(2)}, u32[]{:S(2)}) collective-permute-start(bf16[16,16,128]{2,1,0:T(8,128)(2,1)S(1)} %convert_element_type.224), channel_id=1, source_target_pairs={{4,8},{8,4},{12,16},{16,12},{20,24},{24,20},{5,9},{9,5},{13,17},{1... | collective-permute-start | bytes 196616 | tf_op jit(solution)/shard_map/ppermute | solution.py:25
  6.6 1.0 reshape.561
  7.8 1.0 add_select_fusion
  8.8 0.3 convert_reduce_fusion.1
  9.7 0.6 reduce_max.9
  11.2 0.4 select_reduce_fusion.1
  11.7 0.8 fusion.25
  12.6 1.1 pack.3
  13.7 1.3 %copy-done = bf16[8,56,16,128]{3,2,1,0:T(8,128)(2,1)} copy-done((bf16[8,56,16,128]{3,2,1,0:T(8,128)(2,1)}, bf16[8,56,16,128]{3,2,1,0:T(8,128)(2,1)S(1)}, u32[]{:S(2)}) %copy-start) | copy-done | bytes 1835032
  15.1 0.7 pad_maximum_fusion.1
  15.8 5.0 %collective-permute-start.2 = (bf16[16,48,128]{2,1,0:T(8,128)(2,1)}, bf16[16,48,128]{2,1,0:T(8,128)(2,1)}, u32[]{:S(2)}, u32[]{:S(2)}) collective-permute-start(bf16[16,48,128]{2,1,0:T(8,128)(2,1)} %pad_maximum_fusion.1), channel_id=1, source_target_pairs={{32,64},{64,32},{96,128},{128,96},{160,192},{192,160},{33,65},{65,... | collective-permute-start | bytes 589832 | tf_op jit(solution)/shard_map/ppermute | solution.py:25
  21.2 0.6 fusion.5
  21.9 0.7 copy.33
  22.6 0.6 fusion.4
  23.3 0.7 copy.32
  23.9 7.2 %all-to-all-start.1 = ((bf16[8,56,16,128]{3,2,1,0:T(8,128)(2,1)}), bf16[8,56,16,128]{3,2,1,0:T(8,128)(2,1)S(1)}, u32[]{:S(2)}, u32[]{:S(2)}) async-start(bf16[8,56,16,128]{3,2,1,0:T(8,128)(2,1)} %copy-done), calls=%async_computation.1 | async-start | bytes 3670016 | tf_op jit(solution)/shard_map/all_to_all | solution.py:216
  31.2 2.4 %fusion.7 = bf16[6,256,128]{2,0,1:T(8,128)(2,1)S(1)} fusion(s32[256,128]{1,0:T(8,128)} %get-tuple-element.119, f32[6,3,31]{2,0,1:T(8,128)} %copy-done.19), kind=kOutput, calls=%fused_computation.20 | convolution fusion | flops 74350592 | bytes 528384 | tf_op jit(solution)/shard_map/eim,vm->vei/dot_general | solution.py:88
  33.6 0.9 multiply_convert_fusion.1
  34.6 0.9 multiply_convert_fusion
  35.8 1.8 %broadcast_select_fusion.3 = (bf16[16,48,128]{2,1,0:T(8,128)(2,1)S(1)}, bf16[16,48,128]{2,1,0:T(8,128)(2,1)S(1)}) fusion(bf16[16,48,128]{2,1,0:T(8,128)(2,1)} %collective-permute-done.2, bf16[16,48,128]{2,1,0:T(8,128)(2,1)} %collective-permute-done.3, pred[]{:T(512)S(6)} %eq.203), kind=kLoop, calls=%fused_computation.68 | loop fusion | flops 196608 | bytes 786433 | tf_op jit(solution)/shard_map/jit(_where)/select_n | solution.py:30
  37.7 0.3 edges.3
  38.1 3.5 %collective-permute-start.4 = (bf16[288,128]{1,0:T(8,128)(2,1)S(1)}, bf16[288,128]{1,0:T(8,128)(2,1)S(1)}, u32[]{:S(2)}, u32[]{:S(2)}) collective-permute-start(bf16[288,128]{1,0:T(8,128)(2,1)S(1)} %get-tuple-element.105), channel_id=1, source_target_pairs={{1,2},{2,1},{5,6},{6,5},{9,10},{10,9},{13,14},{14,13},{17,18},{18,... | collective-permute-start | bytes 221192 | tf_op jit(solution)/shard_map/ppermute | solution.py:25
  41.7 2.9 %fusion.6 = bf16[6,256,128]{2,0,1:T(8,128)(2,1)} fusion(s32[256,128]{1,0:T(8,128)S(1)} %copy-done.17, f32[6,3,31]{2,0,1:T(8,128)} %copy-done.19), kind=kOutput, calls=%fused_computation.19 | convolution fusion | flops 74350592 | bytes 528384 | tf_op jit(solution)/shard_map/eim,vm->vei/dot_general | solution.py:88
  44.6 7.5 %collective-permute-done.4 = bf16[288,128]{1,0:T(8,128)(2,1)S(1)} collective-permute-done((bf16[288,128]{1,0:T(8,128)(2,1)S(1)}, bf16[288,128]{1,0:T(8,128)(2,1)S(1)}, u32[]{:S(2)}, u32[]{:S(2)}) %collective-permute-start.4) | collective-permute-done | bytes 73760 | tf_op jit(solution)/shard_map/ppermute | solution.py:25
  52.1 0.4 widen.3
  52.5 1.1 convolution_convert_fusion.1
  53.6 1.0 fusion.20
  54.6 1.1 convolution_convert_fusion
  55.8 0.2 fusion.18
  56.0 2.4 %join.2 = (bf16[48,16,128]{2,1,0:T(8,128)(2,1)S(1)}, bf16[48,16,128]{2,1,0:T(8,128)(2,1)S(1)}, bf16[48,16,128]{2,1,0:T(8,128)(2,1)S(1)}, bf16[48,16,128]{2,1,0:T...) custom-call(s32[3,8]{1,0:T(4,128)S(1)} %pad_add_fusion.1.ends, ...), custom_call_target="tpu_custom_call" | custom-call | tf_op jit(solution)/shard_map/join/pallas_call | solution.py:195
  58.4 1.9 %collective-permute-start.10 = (bf16[24,16,128]{2,1,0:T(8,128)(2,1)S(1)}, bf16[24,16,128]{2,1,0:T(8,128)(2,1)S(1)}, u32[]{:S(2)}, u32[]{:S(2)}) collective-permute-start(bf16[24,16,128]{2,1,0:T(8,128)(2,1)S(1)} %get-tuple-element.68), channel_id=1, source_target_pairs={{32,0},{64,32},{96,64},{128,96},{160,128},{192,160},{224,192},{0,2... | collective-permute-start | bytes 294920 | tf_op jit(solution)/shard_map/ppermute | solution.py:227
  60.5 2.6 %join.3 = (bf16[48,16,128]{2,1,0:T(8,128)(2,1)S(1)}, bf16[48,16,128]{2,1,0:T(8,128)(2,1)S(1)}, bf16[48,16,128]{2,1,0:T(8,128)(2,1)S(1)}, bf16[48,16,128]{2,1,0:T...) custom-call(s32[3,8]{1,0:T(4,128)S(1)} %pad_add_fusion.1.ends, ...), custom_call_target="tpu_custom_call" | custom-call | tf_op jit(solution)/shard_map/join/pallas_call | solution.py:195
  63.1 1.5 %collective-permute-start.6 = (bf16[24,16,128]{2,1,0:T(8,128)(2,1)S(1)}, bf16[24,16,128]{2,1,0:T(8,128)(2,1)S(1)}, u32[]{:S(2)}, u32[]{:S(2)}) collective-permute-start(bf16[24,16,128]{2,1,0:T(8,128)(2,1)S(1)} %get-tuple-element.64), channel_id=1, source_target_pairs={{0,32},{32,64},{64,96},{96,128},{128,160},{160,192},{192,224},{224... | collective-permute-start | bytes 294920 | tf_op jit(solution)/shard_map/ppermute | solution.py:227
  64.6 0.6 collective-permute-start.20
  65.3 2.7 %collective-permute-start.16 = (bf16[24,16,128]{2,1,0:T(8,128)(2,1)S(1)}, bf16[24,16,128]{2,1,0:T(8,128)(2,1)S(1)}, u32[]{:S(2)}, u32[]{:S(2)}) collective-permute-start(bf16[24,16,128]{2,1,0:T(8,128)(2,1)S(1)} %get-tuple-element.76), channel_id=1, source_target_pairs={{0,32},{32,64},{64,96},{96,128},{128,160},{160,192},{192,224},{224... | collective-permute-start | bytes 294920 | tf_op jit(solution)/shard_map/ppermute | solution.py:227
  68.1 0.7 collective-permute-done.6
  68.9 2.6 %collective-permute-start.7 = (bf16[48,16,128]{2,1,0:T(8,128)(2,1)S(1)}, bf16[48,16,128]{2,1,0:T(8,128)(2,1)S(1)}, u32[]{:S(2)}, u32[]{:S(2)}) collective-permute-start(bf16[48,16,128]{2,1,0:T(8,128)(2,1)S(1)} %pad_maximum_fusion.2), channel_id=1, source_target_pairs={{0,32},{32,64},{64,96},{96,128},{128,160},{160,192},{192,224},{224... | collective-permute-start | bytes 589832 | tf_op jit(solution)/shard_map/ppermute | solution.py:227
  71.7 3.3 %collective-permute-start.17 = (bf16[48,16,128]{2,1,0:T(8,128)(2,1)S(1)}, bf16[48,16,128]{2,1,0:T(8,128)(2,1)S(1)}, u32[]{:S(2)}, u32[]{:S(2)}) collective-permute-start(bf16[48,16,128]{2,1,0:T(8,128)(2,1)S(1)} %pad_maximum_fusion.4), channel_id=1, source_target_pairs={{0,32},{32,64},{64,96},{96,128},{128,160},{160,192},{192,224},{224... | collective-permute-start | bytes 589832 | tf_op jit(solution)/shard_map/ppermute | solution.py:227
  75.0 0.6 collective-permute-done.11
  75.7 0.3 collective-permute-start.12
  76.0 0.5 collective-permute-done.7
  76.6 2.8 %collective-permute-start.8 = (bf16[48,16,128]{2,1,0:T(8,128)(2,1)S(1)}, bf16[48,16,128]{2,1,0:T(8,128)(2,1)S(1)}, u32[]{:S(2)}, u32[]{:S(2)}) collective-permute-start(bf16[48,16,128]{2,1,0:T(8,128)(2,1)S(1)} %add_convert_fusion.7), channel_id=1, source_target_pairs={{0,32},{32,64},{64,96},{96,128},{128,160},{160,192},{192,224},{224... | collective-permute-start | bytes 589832 | tf_op jit(solution)/shard_map/ppermute | solution.py:227
  79.4 1.3 %collective-permute-done.21 = bf16[48,16,128]{2,1,0:T(8,128)(2,1)S(1)} collective-permute-done((bf16[48,16,128]{2,1,0:T(8,128)(2,1)S(1)}, bf16[48,16,128]{2,1,0:T(8,128)(2,1)S(1)}, u32[]{:S(2)}, u32[]{:S(2)}) %collective-permute-start.21) | collective-permute-done | bytes 196640 | tf_op jit(solution)/shard_map/ppermute | solution.py:227
  80.9 3.3 %collective-permute-start.18 = (bf16[48,16,128]{2,1,0:T(8,128)(2,1)S(1)}, bf16[48,16,128]{2,1,0:T(8,128)(2,1)S(1)}, u32[]{:S(2)}, u32[]{:S(2)}) collective-permute-start(bf16[48,16,128]{2,1,0:T(8,128)(2,1)S(1)} %add_convert_fusion.3), channel_id=1, source_target_pairs={{0,32},{32,64},{64,96},{96,128},{128,160},{160,192},{192,224},{224... | collective-permute-start | bytes 589832 | tf_op jit(solution)/shard_map/ppermute | solution.py:227
  84.2 0.8 collective-permute-done.12
  85.2 3.3 %collective-permute-start.9 = (bf16[48,16,128]{2,1,0:T(8,128)(2,1)S(1)}, bf16[48,16,128]{2,1,0:T(8,128)(2,1)S(1)}, u32[]{:S(2)}, u32[]{:S(2)}) collective-permute-start(bf16[48,16,128]{2,1,0:T(8,128)(2,1)S(1)} %add_convert_fusion.6), channel_id=1, source_target_pairs={{0,32},{32,64},{64,96},{96,128},{128,160},{160,192},{192,224},{224... | collective-permute-start | bytes 589832 | tf_op jit(solution)/shard_map/ppermute | solution.py:227
  88.5 1.0 collective-permute-done.22
  89.7 3.3 %collective-permute-start.19 = (bf16[48,16,128]{2,1,0:T(8,128)(2,1)S(1)}, bf16[48,16,128]{2,1,0:T(8,128)(2,1)S(1)}, u32[]{:S(2)}, u32[]{:S(2)}) collective-permute-start(bf16[48,16,128]{2,1,0:T(8,128)(2,1)S(1)} %add_convert_fusion.2), channel_id=1, source_target_pairs={{0,32},{32,64},{64,96},{96,128},{128,160},{160,192},{192,224},{224... | collective-permute-start | bytes 589832 | tf_op jit(solution)/shard_map/ppermute | solution.py:227
  93.4 3.8 %collective-permute-start.14 = (bf16[96,128]{1,0:T(8,128)(2,1)S(1)}, bf16[96,128]{1,0:T(8,128)(2,1)S(1)}, u32[]{:S(2)}, u32[]{:S(2)}) collective-permute-start(bf16[96,128]{1,0:T(8,128)(2,1)S(1)} %get-tuple-element.115), channel_id=1, source_target_pairs={{1,2},{2,1},{5,6},{6,5},{9,10},{10,9},{13,14},{14,13},{17,18},{18,... | collective-permute-start | bytes 73736 | tf_op jit(solution)/shard_map/ppermute | solution.py:25
  97.7 2.3 %collective-permute-start.24 = (bf16[96,128]{1,0:T(8,128)(2,1)S(1)}, bf16[96,128]{1,0:T(8,128)(2,1)S(1)}, u32[]{:S(2)}, u32[]{:S(2)}) collective-permute-start(bf16[96,128]{1,0:T(8,128)(2,1)S(1)} %get-tuple-element.111), channel_id=1, source_target_pairs={{1,2},{2,1},{5,6},{6,5},{9,10},{10,9},{13,14},{14,13},{17,18},{18,... | collective-permute-start | bytes 73736 | tf_op jit(solution)/shard_map/ppermute | solution.py:25
  100.2 0.2 convolution_convert_fusion.3
  100.4 1.1 fusion.67
  101.5 1.4 %collective-permute-done.24 = bf16[96,128]{1,0:T(8,128)(2,1)S(1)} collective-permute-done((bf16[96,128]{1,0:T(8,128)(2,1)S(1)}, bf16[96,128]{1,0:T(8,128)(2,1)S(1)}, u32[]{:S(2)}, u32[]{:S(2)}) %collective-permute-start.24) | collective-permute-done | bytes 24608 | tf_op jit(solution)/shard_map/ppermute | solution.py:25
  103.4 1.1 fusion.66
  104.6 5.4 %collective-permute-start.27 = (f16[16,48,128]{2,1,0:T(8,128)(2,1)S(1)}, f16[16,48,128]{2,1,0:T(8,128)(2,1)S(1)}, u32[]{:S(2)}, u32[]{:S(2)}) collective-permute-start(f16[16,48,128]{2,1,0:T(8,128)(2,1)S(1)} %bitcast.115), channel_id=1, source_target_pairs={{32,64},{64,32},{96,128},{128,96},{160,192},{192,160},{33,65},{65,... | collective-permute-start | bytes 589832 | tf_op jit(solution)/shard_map/ppermute | solution.py:25
  110.2 3.5 %collective-permute-done.27 = f16[16,48,128]{2,1,0:T(8,128)(2,1)S(1)} collective-permute-done((f16[16,48,128]{2,1,0:T(8,128)(2,1)S(1)}, f16[16,48,128]{2,1,0:T(8,128)(2,1)S(1)}, u32[]{:S(2)}, u32[]{:S(2)}) %collective-permute-start.27) | collective-permute-done | bytes 196640 | tf_op jit(solution)/shard_map/ppermute | solution.py:25
  113.7 2.1 %collective-permute-done.26 = f16[16,48,128]{2,1,0:T(8,128)(2,1)S(1)} collective-permute-done((f16[16,48,128]{2,1,0:T(8,128)(2,1)S(1)}, f16[16,48,128]{2,1,0:T(8,128)(2,1)S(1)}, u32[]{:S(2)}, u32[]{:S(2)}) %collective-permute-start.26) | collective-permute-done | bytes 196640 | tf_op jit(solution)/shard_map/ppermute | solution.py:25
  115.9 4.8 %collective-permute-start.29 = (f16[16,16,128]{2,1,0:T(8,128)(2,1)S(1)}, f16[16,16,128]{2,1,0:T(8,128)(2,1)S(1)}, u32[]{:S(2)}, u32[]{:S(2)}) collective-permute-start(f16[16,16,128]{2,1,0:T(8,128)(2,1)S(1)} %get-tuple-element.101), channel_id=1, source_target_pairs={{4,8},{8,4},{12,16},{16,12},{20,24},{24,20},{5,9},{9,5},{13,17},{1... | collective-permute-start | bytes 196616 | tf_op jit(solution)/shard_map/ppermute | solution.py:25
  120.7 1.3 collective-permute-start.28
  121.9 2.5 %collective-permute-done.29 = f16[16,16,128]{2,1,0:T(8,128)(2,1)S(1)} collective-permute-done((f16[16,16,128]{2,1,0:T(8,128)(2,1)S(1)}, f16[16,16,128]{2,1,0:T(8,128)(2,1)S(1)}, u32[]{:S(2)}, u32[]{:S(2)}) %collective-permute-start.29) | collective-permute-done | bytes 65568 | tf_op jit(solution)/shard_map/ppermute | solution.py:25
  124.5 2.1 %collective-permute-done.28 = f16[16,16,128]{2,1,0:T(8,128)(2,1)S(1)} collective-permute-done((f16[16,16,128]{2,1,0:T(8,128)(2,1)S(1)}, f16[16,16,128]{2,1,0:T(8,128)(2,1)S(1)}, u32[]{:S(2)}, u32[]{:S(2)}) %collective-permute-start.28) | collective-permute-done | bytes 65568 | tf_op jit(solution)/shard_map/ppermute | solution.py:25
  126.6 0.7 fusion.24
  (148 shorter events, 5.3 us)
Async XLA Ops:
  0.0 11.5 %copy-start.5 = (bf16[6,48,2,8,128]{4,3,2,1,0:T(8,128)(2,1)S(1)}, bf16[6,48,2,8,128]{4,3,2,1,0:T(8,128)(2,1)}, u32[]{:S(2)}) copy-start(bf16[6,48,2,8,128]{4,3,2,1,0:T(8,128)(2,1)} %param.6) | copy-start | bytes 3538948
  1.0 14.1 %copy-start.7 = (bf16[16,16,128]{2,1,0:T(8,128)(2,1)}, bf16[16,16,128]{2,1,0:T(8,128)(2,1)S(1)}, u32[]{:S(2)}) copy-start(bf16[16,16,128]{2,1,0:T(8,128)(2,1)S(1)} %convert_element_type.224) | copy-start | bytes 196612
  1.0 14.0 %collective-permute-start = (bf16[16,16,128]{2,1,0:T(8,128)(2,1)S(1)}, bf16[16,16,128]{2,1,0:T(8,128)(2,1)S(1)}, u32[]{:S(2)}, u32[]{:S(2)}) collective-permute-start(bf16[16,16,128]{2,1,0:T(8,128)(2,1)S(1)} %convert_element_type.224), channel_id=1, source_target_pairs={{0,4},{4,0},{8,12},{12,8},{16,20},{20,16},{24,28},{28,24},{1,5},{5... | collective-permute-start | bytes 196616 | tf_op jit(solution)/shard_map/ppermute | solution.py:25
  3.4 11.6 %collective-permute-start.1 = (bf16[16,16,128]{2,1,0:T(8,128)(2,1)S(1)}, bf16[16,16,128]{2,1,0:T(8,128)(2,1)S(1)}, u32[]{:S(2)}, u32[]{:S(2)}) collective-permute-start(bf16[16,16,128]{2,1,0:T(8,128)(2,1)S(1)} %convert_element_type.224), channel_id=1, source_target_pairs={{4,8},{8,4},{12,16},{16,12},{20,24},{24,20},{5,9},{9,5},{13,17},{1... | collective-permute-start | bytes 196616 | tf_op jit(solution)/shard_map/ppermute | solution.py:25
  12.6 8.3 %copy-start.18 = (f32[6,3,31]{2,1,0:T(4,128)S(1)}, f32[6,3,31]{2,1,0:T(4,128)}, u32[]{:S(2)}) copy-start(f32[6,3,31]{2,1,0:T(4,128)} %param.8) | copy-start | bytes 6700
  13.7 1.3 %copy-start = (bf16[8,56,16,128]{3,2,1,0:T(8,128)(2,1)}, bf16[8,56,16,128]{3,2,1,0:T(8,128)(2,1)S(1)}, u32[]{:S(2)}) copy-start(bf16[8,56,16,128]{3,2,1,0:T(8,128)(2,1)S(1)} %pack.3) | copy-start | bytes 5505028
  15.0 8.2 %copy-start.9 = (bf16[16,16,128]{2,1,0:T(8,128)(2,1)}, bf16[16,16,128]{2,1,0:T(8,128)(2,1)S(1)}, u32[]{:S(2)}) copy-start(bf16[16,16,128]{2,1,0:T(8,128)(2,1)S(1)} %get-tuple-element.106) | copy-start | bytes 196612
  15.1 8.2 %copy-start.11 = (bf16[16,16,128]{2,1,0:T(8,128)(2,1)}, bf16[16,16,128]{2,1,0:T(8,128)(2,1)S(1)}, u32[]{:S(2)}) copy-start(bf16[16,16,128]{2,1,0:T(8,128)(2,1)S(1)} %get-tuple-element.107) | copy-start | bytes 196612
  15.8 20.0 %collective-permute-start.2 = (bf16[16,48,128]{2,1,0:T(8,128)(2,1)}, bf16[16,48,128]{2,1,0:T(8,128)(2,1)}, u32[]{:S(2)}, u32[]{:S(2)}) collective-permute-start(bf16[16,48,128]{2,1,0:T(8,128)(2,1)} %pad_maximum_fusion.1), channel_id=1, source_target_pairs={{32,64},{64,32},{96,128},{128,96},{160,192},{192,160},{33,65},{65,... | collective-permute-start | bytes 589832 | tf_op jit(solution)/shard_map/ppermute | solution.py:25
  20.8 15.0 %collective-permute-start.3 = (bf16[16,48,128]{2,1,0:T(8,128)(2,1)}, bf16[16,48,128]{2,1,0:T(8,128)(2,1)}, u32[]{:S(2)}, u32[]{:S(2)}) collective-permute-start(bf16[16,48,128]{2,1,0:T(8,128)(2,1)} %pad_maximum_fusion.1), channel_id=1, source_target_pairs={{0,32},{32,0},{64,96},{96,64},{128,160},{160,128},{192,224},{224,1... | collective-permute-start | bytes 589832 | tf_op jit(solution)/shard_map/ppermute | solution.py:25
  21.2 2.8 %copy-start.19 = (f32[6,3,31]{2,0,1:T(8,128)}, f32[6,3,31]{2,0,1:T(8,128)S(1)}, u32[]{:S(2)}) copy-start(f32[6,3,31]{2,0,1:T(8,128)S(1)} %copy_divide_fusion) | copy-start | bytes 6700
  23.9 32.1 %all-to-all-start.1 = ((bf16[8,56,16,128]{3,2,1,0:T(8,128)(2,1)}), bf16[8,56,16,128]{3,2,1,0:T(8,128)(2,1)S(1)}, u32[]{:S(2)}, u32[]{:S(2)}) async-start(bf16[8,56,16,128]{3,2,1,0:T(8,128)(2,1)} %copy-done), calls=%async_computation.1 | async-start | bytes 3670016 | tf_op jit(solution)/shard_map/all_to_all | solution.py:216
  31.2 2.4 %copy-start.13 = (f32[6,8,3,256]{3,1,2,0:T(8,128)S(1)}, f32[6,8,3,256]{3,1,2,0:T(8,128)}, u32[]{:S(2)}) copy-start(f32[6,8,3,256]{3,1,2,0:T(8,128)} %copy.33) | copy-start | bytes 442372
  31.2 2.4 %copy-start.14 = (f32[6,8,3,256]{3,1,2,0:T(8,128)S(1)}, f32[6,8,3,256]{3,1,2,0:T(8,128)}, u32[]{:S(2)}) copy-start(f32[6,8,3,256]{3,1,2,0:T(8,128)} %copy.32) | copy-start | bytes 442372
  34.5 17.9 %copy-start.3 = (bf16[48,48,768]{2,1,0:T(8,128)(2,1)}, bf16[48,48,768]{2,1,0:T(8,128)(2,1)S(1)}, u32[]{:S(2)}) copy-start(bf16[48,48,768]{2,1,0:T(8,128)(2,1)S(1)} %multiply_convert_fusion.1) | copy-start | bytes 10616836
  35.5 19.1 %copy-start.1 = (bf16[48,48,768]{2,1,0:T(8,128)(2,1)}, bf16[48,48,768]{2,1,0:T(8,128)(2,1)S(1)}, u32[]{:S(2)}) copy-start(bf16[48,48,768]{2,1,0:T(8,128)(2,1)S(1)} %multiply_convert_fusion) | copy-start | bytes 10616836
  35.5 2.1 %copy-start.8 = (bf16[16,16,128]{2,1,0:T(8,128)(2,1)S(1)}, bf16[16,16,128]{2,1,0:T(8,128)(2,1)}, u32[]{:S(2)}) copy-start(bf16[16,16,128]{2,1,0:T(8,128)(2,1)} %copy-done.7) | copy-start | bytes 196612
  35.5 2.1 %copy-start.10 = (bf16[16,16,128]{2,1,0:T(8,128)(2,1)S(1)}, bf16[16,16,128]{2,1,0:T(8,128)(2,1)}, u32[]{:S(2)}) copy-start(bf16[16,16,128]{2,1,0:T(8,128)(2,1)} %copy-done.9) | copy-start | bytes 196612
  35.5 2.1 %copy-start.12 = (bf16[16,16,128]{2,1,0:T(8,128)(2,1)S(1)}, bf16[16,16,128]{2,1,0:T(8,128)(2,1)}, u32[]{:S(2)}) copy-start(bf16[16,16,128]{2,1,0:T(8,128)(2,1)} %copy-done.11) | copy-start | bytes 196612
  35.7 5.9 %copy-start.17 = (s32[256,128]{1,0:T(8,128)S(1)}, s32[256,128]{1,0:T(8,128)}, u32[]{:S(2)}) copy-start(s32[256,128]{1,0:T(8,128)} %get-tuple-element.118) | copy-start | bytes 393220
  38.0 6.5 %collective-permute-start.5 = (bf16[288,128]{1,0:T(8,128)(2,1)S(1)}, bf16[288,128]{1,0:T(8,128)(2,1)S(1)}, u32[]{:S(2)}, u32[]{:S(2)}) collective-permute-start(bf16[288,128]{1,0:T(8,128)(2,1)S(1)} %get-tuple-element.104), channel_id=1, source_target_pairs={{0,1},{1,0},{2,3},{3,2},{4,5},{5,4},{6,7},{7,6},{8,9},{9,8},{10,11... | collective-permute-start | bytes 221192 | tf_op jit(solution)/shard_map/ppermute | solution.py:25
  38.1 13.9 %collective-permute-start.4 = (bf16[288,128]{1,0:T(8,128)(2,1)S(1)}, bf16[288,128]{1,0:T(8,128)(2,1)S(1)}, u32[]{:S(2)}, u32[]{:S(2)}) collective-permute-start(bf16[288,128]{1,0:T(8,128)(2,1)S(1)} %get-tuple-element.105), channel_id=1, source_target_pairs={{1,2},{2,1},{5,6},{6,5},{9,10},{10,9},{13,14},{14,13},{17,18},{18,... | collective-permute-start | bytes 221192 | tf_op jit(solution)/shard_map/ppermute | solution.py:25
  56.0 4.3 %copy-start.15 = (bf16[6,256,128]{2,0,1:T(8,128)(2,1)S(1)}, bf16[6,256,128]{2,0,1:T(8,128)(2,1)}, u32[]{:S(2)}) copy-start(bf16[6,256,128]{2,0,1:T(8,128)(2,1)} %fusion.6) | copy-start | bytes 1179652
  58.4 9.5 %collective-permute-start.10 = (bf16[24,16,128]{2,1,0:T(8,128)(2,1)S(1)}, bf16[24,16,128]{2,1,0:T(8,128)(2,1)S(1)}, u32[]{:S(2)}, u32[]{:S(2)}) collective-permute-start(bf16[24,16,128]{2,1,0:T(8,128)(2,1)S(1)} %get-tuple-element.68), channel_id=1, source_target_pairs={{32,0},{64,32},{96,64},{128,96},{160,128},{192,160},{224,192},{0,2... | collective-permute-start | bytes 294920 | tf_op jit(solution)/shard_map/ppermute | solution.py:227
  63.1 5.6 %collective-permute-start.6 = (bf16[24,16,128]{2,1,0:T(8,128)(2,1)S(1)}, bf16[24,16,128]{2,1,0:T(8,128)(2,1)S(1)}, u32[]{:S(2)}, u32[]{:S(2)}) collective-permute-start(bf16[24,16,128]{2,1,0:T(8,128)(2,1)S(1)} %get-tuple-element.64), channel_id=1, source_target_pairs={{0,32},{32,64},{64,96},{96,128},{128,160},{160,192},{192,224},{224... | collective-permute-start | bytes 294920 | tf_op jit(solution)/shard_map/ppermute | solution.py:227
  64.6 6.9 %collective-permute-start.20 = (bf16[24,16,128]{2,1,0:T(8,128)(2,1)S(1)}, bf16[24,16,128]{2,1,0:T(8,128)(2,1)S(1)}, u32[]{:S(2)}, u32[]{:S(2)}) collective-permute-start(bf16[24,16,128]{2,1,0:T(8,128)(2,1)S(1)} %get-tuple-element.80), channel_id=1, source_target_pairs={{32,0},{64,32},{96,64},{128,96},{160,128},{192,160},{224,192},{0,2... | collective-permute-start | bytes 294920 | tf_op jit(solution)/shard_map/ppermute | solution.py:227
  65.3 6.4 %collective-permute-start.16 = (bf16[24,16,128]{2,1,0:T(8,128)(2,1)S(1)}, bf16[24,16,128]{2,1,0:T(8,128)(2,1)S(1)}, u32[]{:S(2)}, u32[]{:S(2)}) collective-permute-start(bf16[24,16,128]{2,1,0:T(8,128)(2,1)S(1)} %get-tuple-element.76), channel_id=1, source_target_pairs={{0,32},{32,64},{64,96},{96,128},{128,160},{160,192},{192,224},{224... | collective-permute-start | bytes 294920 | tf_op jit(solution)/shard_map/ppermute | solution.py:227
  68.0 7.6 %collective-permute-start.11 = (bf16[48,16,128]{2,1,0:T(8,128)(2,1)S(1)}, bf16[48,16,128]{2,1,0:T(8,128)(2,1)S(1)}, u32[]{:S(2)}, u32[]{:S(2)}) collective-permute-start(bf16[48,16,128]{2,1,0:T(8,128)(2,1)S(1)} %pad_maximum_fusion.3), channel_id=1, source_target_pairs={{32,0},{64,32},{96,64},{128,96},{160,128},{192,160},{224,192},{0,2... | collective-permute-start | bytes 589832 | tf_op jit(solution)/shard_map/ppermute | solution.py:227
  68.9 7.7 %collective-permute-start.7 = (bf16[48,16,128]{2,1,0:T(8,128)(2,1)S(1)}, bf16[48,16,128]{2,1,0:T(8,128)(2,1)S(1)}, u32[]{:S(2)}, u32[]{:S(2)}) collective-permute-start(bf16[48,16,128]{2,1,0:T(8,128)(2,1)S(1)} %pad_maximum_fusion.2), channel_id=1, source_target_pairs={{0,32},{32,64},{64,96},{96,128},{128,160},{160,192},{192,224},{224... | collective-permute-start | bytes 589832 | tf_op jit(solution)/shard_map/ppermute | solution.py:227
  71.5 9.1 %collective-permute-start.21 = (bf16[48,16,128]{2,1,0:T(8,128)(2,1)S(1)}, bf16[48,16,128]{2,1,0:T(8,128)(2,1)S(1)}, u32[]{:S(2)}, u32[]{:S(2)}) collective-permute-start(bf16[48,16,128]{2,1,0:T(8,128)(2,1)S(1)} %pad_maximum_fusion.5), channel_id=1, source_target_pairs={{32,0},{64,32},{96,64},{128,96},{160,128},{192,160},{224,192},{0,2... | collective-permute-start | bytes 589832 | tf_op jit(solution)/shard_map/ppermute | solution.py:227
  71.7 9.1 %collective-permute-start.17 = (bf16[48,16,128]{2,1,0:T(8,128)(2,1)S(1)}, bf16[48,16,128]{2,1,0:T(8,128)(2,1)S(1)}, u32[]{:S(2)}, u32[]{:S(2)}) collective-permute-start(bf16[48,16,128]{2,1,0:T(8,128)(2,1)S(1)} %pad_maximum_fusion.4), channel_id=1, source_target_pairs={{0,32},{32,64},{64,96},{96,128},{128,160},{160,192},{192,224},{224... | collective-permute-start | bytes 589832 | tf_op jit(solution)/shard_map/ppermute | solution.py:227
  75.7 9.3 %collective-permute-start.12 = (bf16[48,16,128]{2,1,0:T(8,128)(2,1)S(1)}, bf16[48,16,128]{2,1,0:T(8,128)(2,1)S(1)}, u32[]{:S(2)}, u32[]{:S(2)}) collective-permute-start(bf16[48,16,128]{2,1,0:T(8,128)(2,1)S(1)} %add_convert_fusion.5), channel_id=1, source_target_pairs={{32,0},{64,32},{96,64},{128,96},{160,128},{192,160},{224,192},{0,2... | collective-permute-start | bytes 589832 | tf_op jit(solution)/shard_map/ppermute | solution.py:227
  76.6 8.5 %collective-permute-start.8 = (bf16[48,16,128]{2,1,0:T(8,128)(2,1)S(1)}, bf16[48,16,128]{2,1,0:T(8,128)(2,1)S(1)}, u32[]{:S(2)}, u32[]{:S(2)}) collective-permute-start(bf16[48,16,128]{2,1,0:T(8,128)(2,1)S(1)} %add_convert_fusion.7), channel_id=1, source_target_pairs={{0,32},{32,64},{64,96},{96,128},{128,160},{160,192},{192,224},{224... | collective-permute-start | bytes 589832 | tf_op jit(solution)/shard_map/ppermute | solution.py:227
  80.7 8.7 %collective-permute-start.22 = (bf16[48,16,128]{2,1,0:T(8,128)(2,1)S(1)}, bf16[48,16,128]{2,1,0:T(8,128)(2,1)S(1)}, u32[]{:S(2)}, u32[]{:S(2)}) collective-permute-start(bf16[48,16,128]{2,1,0:T(8,128)(2,1)S(1)} %add_convert_fusion.1), channel_id=1, source_target_pairs={{32,0},{64,32},{96,64},{128,96},{160,128},{192,160},{224,192},{0,2... | collective-permute-start | bytes 589832 | tf_op jit(solution)/shard_map/ppermute | solution.py:227
  80.9 8.7 %collective-permute-start.18 = (bf16[48,16,128]{2,1,0:T(8,128)(2,1)S(1)}, bf16[48,16,128]{2,1,0:T(8,128)(2,1)S(1)}, u32[]{:S(2)}, u32[]{:S(2)}) collective-permute-start(bf16[48,16,128]{2,1,0:T(8,128)(2,1)S(1)} %add_convert_fusion.3), channel_id=1, source_target_pairs={{0,32},{32,64},{64,96},{96,128},{128,160},{160,192},{192,224},{224... | collective-permute-start | bytes 589832 | tf_op jit(solution)/shard_map/ppermute | solution.py:227
  85.0 7.9 %collective-permute-start.13 = (bf16[48,16,128]{2,1,0:T(8,128)(2,1)S(1)}, bf16[48,16,128]{2,1,0:T(8,128)(2,1)S(1)}, u32[]{:S(2)}, u32[]{:S(2)}) collective-permute-start(bf16[48,16,128]{2,1,0:T(8,128)(2,1)S(1)} %add_convert_fusion.4), channel_id=1, source_target_pairs={{32,0},{64,32},{96,64},{128,96},{160,128},{192,160},{224,192},{0,2... | collective-permute-start | bytes 589832 | tf_op jit(solution)/shard_map/ppermute | solution.py:227
  85.1 7.9 %copy-start.6 = (f32[3,256,128]{2,1,0:T(8,128)S(1)}, f32[3,256,128]{2,1,0:T(8,128)}, u32[]{:S(2)}) copy-start(f32[3,256,128]{2,1,0:T(8,128)} %fusion.20) | copy-start | bytes 1179652
  85.2 7.8 %collective-permute-start.9 = (bf16[48,16,128]{2,1,0:T(8,128)(2,1)S(1)}, bf16[48,16,128]{2,1,0:T(8,128)(2,1)S(1)}, u32[]{:S(2)}, u32[]{:S(2)}) collective-permute-start(bf16[48,16,128]{2,1,0:T(8,128)(2,1)S(1)} %add_convert_fusion.6), channel_id=1, source_target_pairs={{0,32},{32,64},{64,96},{96,128},{128,160},{160,192},{192,224},{224... | collective-permute-start | bytes 589832 | tf_op jit(solution)/shard_map/ppermute | solution.py:227
  89.5 7.7 %collective-permute-start.23 = (bf16[48,16,128]{2,1,0:T(8,128)(2,1)S(1)}, bf16[48,16,128]{2,1,0:T(8,128)(2,1)S(1)}, u32[]{:S(2)}, u32[]{:S(2)}) collective-permute-start(bf16[48,16,128]{2,1,0:T(8,128)(2,1)S(1)} %add_convert_fusion), channel_id=1, source_target_pairs={{32,0},{64,32},{96,64},{128,96},{160,128},{192,160},{224,192},{0,2... | collective-permute-start | bytes 589832 | tf_op jit(solution)/shard_map/ppermute | solution.py:227
  89.7 7.6 %collective-permute-start.19 = (bf16[48,16,128]{2,1,0:T(8,128)(2,1)S(1)}, bf16[48,16,128]{2,1,0:T(8,128)(2,1)S(1)}, u32[]{:S(2)}, u32[]{:S(2)}) collective-permute-start(bf16[48,16,128]{2,1,0:T(8,128)(2,1)S(1)} %add_convert_fusion.2), channel_id=1, source_target_pairs={{0,32},{32,64},{64,96},{96,128},{128,160},{160,192},{192,224},{224... | collective-permute-start | bytes 589832 | tf_op jit(solution)/shard_map/ppermute | solution.py:227
  93.3 6.6 %collective-permute-start.15 = (bf16[96,128]{1,0:T(8,128)(2,1)S(1)}, bf16[96,128]{1,0:T(8,128)(2,1)S(1)}, u32[]{:S(2)}, u32[]{:S(2)}) collective-permute-start(bf16[96,128]{1,0:T(8,128)(2,1)S(1)} %get-tuple-element.114), channel_id=1, source_target_pairs={{0,1},{1,0},{2,3},{3,2},{4,5},{5,4},{6,7},{7,6},{8,9},{9,8},{10,11... | collective-permute-start | bytes 73736 | tf_op jit(solution)/shard_map/ppermute | solution.py:25
  93.4 6.6 %collective-permute-start.14 = (bf16[96,128]{1,0:T(8,128)(2,1)S(1)}, bf16[96,128]{1,0:T(8,128)(2,1)S(1)}, u32[]{:S(2)}, u32[]{:S(2)}) collective-permute-start(bf16[96,128]{1,0:T(8,128)(2,1)S(1)} %get-tuple-element.115), channel_id=1, source_target_pairs={{1,2},{2,1},{5,6},{6,5},{9,10},{10,9},{13,14},{14,13},{17,18},{18,... | collective-permute-start | bytes 73736 | tf_op jit(solution)/shard_map/ppermute | solution.py:25
  97.2 3.2 %copy-start.4 = (bf16[48,48,768]{2,1,0:T(8,128)(2,1)S(1)}, bf16[48,48,768]{2,1,0:T(8,128)(2,1)}, u32[]{:S(2)}) copy-start(bf16[48,48,768]{2,1,0:T(8,128)(2,1)} %copy-done.3) | copy-start | bytes 10616836
  97.6 4.0 %collective-permute-start.25 = (bf16[96,128]{1,0:T(8,128)(2,1)S(1)}, bf16[96,128]{1,0:T(8,128)(2,1)S(1)}, u32[]{:S(2)}, u32[]{:S(2)}) collective-permute-start(bf16[96,128]{1,0:T(8,128)(2,1)S(1)} %get-tuple-element.110), channel_id=1, source_target_pairs={{0,1},{1,0},{2,3},{3,2},{4,5},{5,4},{6,7},{7,6},{8,9},{9,8},{10,11... | collective-permute-start | bytes 73736 | tf_op jit(solution)/shard_map/ppermute | solution.py:25
  97.7 5.3 %collective-permute-start.24 = (bf16[96,128]{1,0:T(8,128)(2,1)S(1)}, bf16[96,128]{1,0:T(8,128)(2,1)S(1)}, u32[]{:S(2)}, u32[]{:S(2)}) collective-permute-start(bf16[96,128]{1,0:T(8,128)(2,1)S(1)} %get-tuple-element.111), channel_id=1, source_target_pairs={{1,2},{2,1},{5,6},{6,5},{9,10},{10,9},{13,14},{14,13},{17,18},{18,... | collective-permute-start | bytes 73736 | tf_op jit(solution)/shard_map/ppermute | solution.py:25
  100.4 2.9 %copy-start.2 = (bf16[48,48,768]{2,1,0:T(8,128)(2,1)S(1)}, bf16[48,48,768]{2,1,0:T(8,128)(2,1)}, u32[]{:S(2)}) copy-start(bf16[48,48,768]{2,1,0:T(8,128)(2,1)} %copy-done.1) | copy-start | bytes 10616836
  104.6 22.0 %copy-start.16 = (f32[16,16,128]{2,1,0:T(8,128)S(1)}, f32[16,16,128]{2,1,0:T(8,128)}, u32[]{:S(2)}) copy-start(f32[16,16,128]{2,1,0:T(8,128)} %param.9) | copy-start | bytes 393220
  104.6 9.1 %collective-permute-start.27 = (f16[16,48,128]{2,1,0:T(8,128)(2,1)S(1)}, f16[16,48,128]{2,1,0:T(8,128)(2,1)S(1)}, u32[]{:S(2)}, u32[]{:S(2)}) collective-permute-start(f16[16,48,128]{2,1,0:T(8,128)(2,1)S(1)} %bitcast.115), channel_id=1, source_target_pairs={{32,64},{64,32},{96,128},{128,96},{160,192},{192,160},{33,65},{65,... | collective-permute-start | bytes 589832 | tf_op jit(solution)/shard_map/ppermute | solution.py:25
  110.0 5.8 %collective-permute-start.26 = (f16[16,48,128]{2,1,0:T(8,128)(2,1)S(1)}, f16[16,48,128]{2,1,0:T(8,128)(2,1)S(1)}, u32[]{:S(2)}, u32[]{:S(2)}) collective-permute-start(f16[16,48,128]{2,1,0:T(8,128)(2,1)S(1)} %bitcast.114), channel_id=1, source_target_pairs={{0,32},{32,0},{64,96},{96,64},{128,160},{160,128},{192,224},{224,1... | collective-permute-start | bytes 589832 | tf_op jit(solution)/shard_map/ppermute | solution.py:25
  115.9 8.6 %collective-permute-start.29 = (f16[16,16,128]{2,1,0:T(8,128)(2,1)S(1)}, f16[16,16,128]{2,1,0:T(8,128)(2,1)S(1)}, u32[]{:S(2)}, u32[]{:S(2)}) collective-permute-start(f16[16,16,128]{2,1,0:T(8,128)(2,1)S(1)} %get-tuple-element.101), channel_id=1, source_target_pairs={{4,8},{8,4},{12,16},{16,12},{20,24},{24,20},{5,9},{9,5},{13,17},{1... | collective-permute-start | bytes 196616 | tf_op jit(solution)/shard_map/ppermute | solution.py:25
  120.7 5.9 %collective-permute-start.28 = (f16[16,16,128]{2,1,0:T(8,128)(2,1)S(1)}, f16[16,16,128]{2,1,0:T(8,128)(2,1)S(1)}, u32[]{:S(2)}, u32[]{:S(2)}) collective-permute-start(f16[16,16,128]{2,1,0:T(8,128)(2,1)S(1)} %get-tuple-element.100), channel_id=1, source_target_pairs={{0,4},{4,0},{8,12},{12,8},{16,20},{20,16},{24,28},{28,24},{1,5},{5... | collective-permute-start | bytes 196616 | tf_op jit(solution)/shard_map/ppermute | solution.py:25

commit v2 on v1

--- a/solution.py
+++ b/solution.py
@@ -59,7 +59,7 @@
         wide[part, cols:] = halo.astype(wide.dtype)
 
 
-def with_columns(value, side):
+def column_sides(value, side):
     rows, cols = value.shape
     groups = cols // side
     packed = jax.ShapeDtypeStruct((rows // groups, cols), value.dtype)
@@ -71,7 +71,11 @@
         compiler_params=pltpu.CompilerParams(vmem_limit_bytes=32 << 20),
         name="edges",
     )(value)
-    before, after = order_sides(*neighbours(last, first, "gx"), "gx")
+    return order_sides(*neighbours(last, first, "gx"), "gx")
+
+
+def with_columns(value, before, after):
+    rows, cols = value.shape
     return pl.pallas_call(
         widen_kernel,
         out_shape=jax.ShapeDtypeStruct((rows, 2 * cols), value.dtype),
@@ -132,15 +136,23 @@
     return jnp.max(jnp.sum(dest_gy == jnp.arange(gy_count)[:, None], axis=(0, 3)))
 
 
-def pack_kernel(source, tiles, outgoing):
-    partners, lanes = outgoing.shape[:2]
-
-    def one(partner, carry):
-        for lane in range(lanes):
-            outgoing[partner, lane] = tiles[source[partner, lane]]
-        return carry
-
-    lax.fori_loop(0, partners, one, 0)
+def pack_kernel(source, tiles, outgoing, filled, done):
+    partners, lanes = filled.shape[:2]
+    copies = []
+    for partner in range(partners):
+
+        def fill(index, carry):
+            for lane in range(8):
+                lane = index * 8 + lane
+                filled[partner, lane] = tiles[source[partner, lane]]
+            return carry
+
+        lax.fori_loop(0, lanes // 8, fill, 0)
+        copy = pltpu.make_async_copy(filled.at[partner], outgoing.at[partner], done.at[partner])
+        copy.start()
+        copies.append(copy)
+    for copy in copies:
+        copy.wait()
 
 
 def join_kernel(chunk, ends, cell, late_cell, arrived, late, *blocks_and_total):
@@ -178,11 +190,16 @@
 
 
 def pack(source, tiles):
+    shape = source.shape + tiles.shape[1:]
     return pl.pallas_call(
         pack_kernel,
-        out_shape=jax.ShapeDtypeStruct(source.shape + tiles.shape[1:], tiles.dtype),
+        out_shape=jax.ShapeDtypeStruct(shape, tiles.dtype),
         in_specs=[smem, vmem],
-        out_specs=vmem,
+        out_specs=pl.BlockSpec(memory_space=pl.ANY),
+        scratch_shapes=[
+            pltpu.VMEM(shape, tiles.dtype),
+            pltpu.SemaphoreType.DMA((source.shape[0],)),
+        ],
         compiler_params=pltpu.CompilerParams(vmem_limit_bytes=32 << 20),
         name="pack",
     )(source, tiles)
@@ -301,6 +318,7 @@
         across = row_taps[v : v + chunk].transpose(1, 0, 2).reshape(1, wide, chunk * area)
         sheet = (down * across).astype(jnp.bfloat16)
         sheets.append(sheet.reshape(tall * wide, chunk * area))
+    own_rows, _ = lax.optimization_barrier((own_rows, sheets))
     above, below = order_sides(*own_rows, "gy")
     own = jnp.concatenate([above, own, below], axis=1)
     above, below = order_sides(*neighbours(own, own, "gz"), "gz")
@@ -313,7 +331,13 @@
     offset = column[:, None] - jnp.arange(cols)[None, :]
     col_taps = taps_table(kernels[:, 2], radius + offset).astype(jnp.bfloat16)
     col_taps_back = taps_table(kernels[:, 2], radius - offset).astype(jnp.bfloat16)
-    field = with_columns(own, side)
+    before, after = column_sides(own, side)
+    blocks = [
+        join(c, ends, usual_table[1], late_cell, arrived, late, gz_count, chunk * positions)
+        for c in range(chunks)
+    ]
+    own, before, after, _ = lax.optimization_barrier((own, before, after, blocks[-1][0]))
+    field = with_columns(own, before, after)
     blurred = []
     for c in range(chunks):
         swept = lax.dot_general(
@@ -328,17 +352,13 @@
                 preferred_element_type=jnp.float32,
             )
         )
-    arrived, blurred = lax.optimization_barrier((arrived, blurred))
-    joined = []
-    for c in range(chunks):
-        blocks = join(c, ends, usual_table[1], late_cell, arrived, late, gz_count, chunk * positions)
-        joined.append(ring_sum(blocks))
+    joined = [ring_sum(blocks[c]) for c in range(chunks)]
     total = jnp.zeros((tall * wide, cols), jnp.float32)
     for c in range(chunks):
         views = slice(c * chunk, (c + 1) * chunk)
         ratio = joined[c].reshape(chunk, area, cols) / (blurred[c] + background_level)
         ratio = ratio.astype(jnp.bfloat16).reshape(chunk * area, cols)
-        ratio = with_columns(ratio, side).reshape(chunk, area, -1)
+        ratio = with_columns(ratio, *column_sides(ratio, side)).reshape(chunk, area, -1)
         spread = jnp.einsum(
             "vac,vck->vak", ratio, col_taps_back[views], preferred_element_type=jnp.float32
         )

time: 128 us -> 148 us (1.16); the launches traced: 127 us -> 146 us
  waiting for transfers between devices: 24 us -> 41.7 us
  Pallas kernels: 7.48 us -> 11.7 us
  starting transfers between devices: 65.2 us -> 61.8 us
  matrix products: 12.8 us -> 9.54 us
  other arithmetic: 11.1 us -> 13.1 us
    ppermute x16, waiting for transfers between devices: 4.9 us -> 18.1 us  [ring_step(): return (lax.ppermute(upward, 'gz', up), lax.ppermute(downward, 'gz', down))]
    ppermute x16, starting transfers between devices: 25.9 us -> 21.6 us  [ring_step(): return (lax.ppermute(upward, 'gz', up), lax.ppermute(downward, 'gz', down))]
    ppermute x7, waiting for transfers between devices: 14.9 us -> 18.9 us  [neighbours(): lax.ppermute(second, axis, pairs[1])]
    convert_element_type x2, other arithmetic: 1.86 us -> 5.38 us  [on_device(): sheet = (down * across).astype(jnp.bfloat16)]
    pallas_call x4, Pallas kernels: 1.77 us -> 4.99 us  [the longest x1 4.33 us: pack(): pl.pallas_call(pack_kernel, out_shape=jax.ShapeDtypeStruct(shape, tiles.d...]
    ppermute x7, starting transfers between devices: 27.9 us -> 31.1 us  [neighbours(): lax.ppermute(second, axis, pairs[1])]
    all_to_all x1, waiting for transfers between devices: 0.01 us -> 2.59 us  [exchange(): return lax.all_to_all(value, 'gy', split_axis=0, concat_axis=0, tiled=True)]
    dot_general x4, matrix products: 6.41 us -> 3.96 us  [taps_table(): return jnp.einsum('eim,vm->vei', table, kernel_set, precision=highest)]
  transfers between devices with their start and end apart: 31 -> 31, of which waited for: 12 -> 13; matrix products, arithmetic and copies ran while one was open for 18% -> 9% of each run, Pallas kernels for 4% -> 5%
where the time goes in v2:
time: 148 us; the launch traced here: 146 us
  starting transfers between devices  61.8 us (42%)
  waiting for transfers between devices  41.7 us (28%)
  other arithmetic  13.1 us (9%)
  Pallas kernels  11.7 us (8%)
  matrix products  9.54 us (6%)
  local copies, waits for them, and re-layouts  6.25 us (4%)
  between operations  1.52 us (1%)
    ppermute x7, starting transfers between devices, neighbours(): lax.ppermute(second, axis, pairs[1])  31.1 us
    ppermute x16, starting transfers between devices, ring_step(): return (lax.ppermute(upward, 'gz', up), lax.ppermute(downward, 'gz', down))  21.6 us
    ppermute x7, waiting for transfers between devices, neighbours(): lax.ppermute(second, axis, pairs[1])  18.9 us
    ppermute x16, waiting for transfers between devices, ring_step(): return (lax.ppermute(upward, 'gz', up), lax.ppermute(downward, 'gz', down))  18.1 us
    pallas_call x2, Pallas kernels, join(): pl.pallas_call(functools.partial(join_kernel, chunk), out_shape=[jax.Shap...  5.99 us
    all_to_all x1, starting transfers between devices, exchange(): return lax.all_to_all(value, 'gy', split_axis=0, concat_axis=0, tiled=True)  5.65 us
    convert_element_type x2, other arithmetic, on_device(): sheet = (down * across).astype(jnp.bfloat16)  5.38 us
    pallas_call x1, Pallas kernels, pack(): pl.pallas_call(pack_kernel, out_shape=jax.ShapeDtypeStruct(shape, tiles.d...  4.33 us
  transfers between devices with their start and end apart: 31, of which 13 were waited for; matrix products, arithmetic and copies ran while one was open for 9% of the time, Pallas kernels for 5%

profile of v2, /device:TPU:106, one launch (start us, length us, event | category | flops | bytes accessed | tf_op | source)
XLA Modules:
  0.0 145.6 jit_solution(10095401234006366171)
XLA Ops:
  0.0 1.0 convert_element_type.224
  1.0 4.2 %collective-permute-start.1 = (bf16[16,16,128]{2,1,0:T(8,128)(2,1)S(1)}, bf16[16,16,128]{2,1,0:T(8,128)(2,1)S(1)}, u32[]{:S(2)}, u32[]{:S(2)}) collective-permute-start(bf16[16,16,128]{2,1,0:T(8,128)(2,1)S(1)} %convert_element_type.224), channel_id=1, source_target_pairs={{4,8},{8,4},{12,16},{16,12},{20,24},{24,20},{5,9},{9,5},{13,17},{1... | collective-permute-start | bytes 196616 | tf_op jit(solution)/shard_map/ppermute | solution.py:25
  5.2 2.3 %collective-permute-start = (bf16[16,16,128]{2,1,0:T(8,128)(2,1)S(1)}, bf16[16,16,128]{2,1,0:T(8,128)(2,1)S(1)}, u32[]{:S(2)}, u32[]{:S(2)}) collective-permute-start(bf16[16,16,128]{2,1,0:T(8,128)(2,1)S(1)} %convert_element_type.224), channel_id=1, source_target_pairs={{0,4},{4,0},{8,12},{12,8},{16,20},{20,16},{24,28},{28,24},{1,5},{5... | collective-permute-start | bytes 196616 | tf_op jit(solution)/shard_map/ppermute | solution.py:25
  7.5 1.0 add_select_fusion
  8.5 1.0 reshape.561
  9.6 0.3 convert_reduce_fusion.1
  10.4 0.6 reduce_max.9
  12.1 0.4 select_reduce_fusion.1
  12.6 0.8 fusion.23
  13.3 1.1 copy-done.3
  14.5 4.3 %pack.3 = bf16[8,56,16,128]{3,2,1,0:T(8,128)(2,1)S(1)} custom-call(s32[8,56]{1,0:T(8,128)S(1)} %get-tuple-element.121.source, bf16[288,16,128]{2,1,0:T(8,128)(2,1)S(1)} %bitcast.96), custom_call_target="tpu_custom_call" | custom-call | tf_op jit(solution)/shard_map/pack/pallas_call | solution.py:194
  18.9 1.3 copy-done
  20.4 0.6 fusion.5
  21.2 0.6 fusion.4
  22.0 2.7 %multiply_convert_fusion.1 = bf16[48,48,768]{2,1,0:T(8,128)(2,1)} fusion(f32[48,768]{1,0:T(8,128)S(1)} %bitcast.107, f32[48,768]{1,0:T(8,128)S(1)} %bitcast.109), kind=kLoop, calls=%fused_computation.5 | loop fusion | flops 3538944 | bytes 3833856 | tf_op jit(solution)/shard_map/convert_element_type | solution.py:319
  24.6 2.7 %multiply_convert_fusion = bf16[48,48,768]{2,1,0:T(8,128)(2,1)} fusion(f32[48,768]{1,0:T(8,128)S(1)} %bitcast.106, f32[48,768]{1,0:T(8,128)S(1)} %bitcast.108), kind=kLoop, calls=%fused_computation.4 | loop fusion | flops 3538944 | bytes 3833856 | tf_op jit(solution)/shard_map/convert_element_type | solution.py:319
  27.4 0.2 collective-permute-start.11
  27.6 5.9 %collective-permute-start.10 = (bf16[16,48,128]{2,1,0:T(8,128)(2,1)S(1)}, bf16[16,48,128]{2,1,0:T(8,128)(2,1)}, u32[]{:S(2)}, u32[]{:S(2)}) collective-permute-start(bf16[16,48,128]{2,1,0:T(8,128)(2,1)S(1)} %pad_maximum_fusion.3), channel_id=1, source_target_pairs={{32,64},{64,32},{96,128},{128,96},{160,192},{192,160},{33,65},{65,... | collective-permute-start | bytes 589832 | tf_op jit(solution)/shard_map/ppermute | solution.py:25
  33.5 5.6 %all-to-all-start.1 = ((bf16[8,56,16,128]{3,2,1,0:T(8,128)(2,1)}), bf16[8,56,16,128]{3,2,1,0:T(8,128)(2,1)S(1)}, u32[]{:S(2)}, u32[]{:S(2)}) async-start(bf16[8,56,16,128]{3,2,1,0:T(8,128)(2,1)} %copy-done), calls=%async_computation.1 | async-start | bytes 3670016 | tf_op jit(solution)/shard_map/all_to_all | solution.py:233
  39.2 1.4 fusion.6
  40.8 1.4 fusion.7
  42.2 1.1 broadcast_select_fusion.3
  43.3 0.3 edges.3
  43.8 3.3 %collective-permute-start.12 = (bf16[288,128]{1,0:T(8,128)(2,1)S(1)}, bf16[288,128]{1,0:T(8,128)(2,1)S(1)}, u32[]{:S(2)}, u32[]{:S(2)}) collective-permute-start(bf16[288,128]{1,0:T(8,128)(2,1)S(1)} %get-tuple-element.109), channel_id=1, source_target_pairs={{1,2},{2,1},{5,6},{6,5},{9,10},{10,9},{13,14},{14,13},{17,18},{18,... | collective-permute-start | bytes 221192 | tf_op jit(solution)/shard_map/ppermute | solution.py:25
  47.1 0.9 fusion.61
  48.0 11.7 %collective-permute-done.12 = bf16[288,128]{1,0:T(8,128)(2,1)S(1)} collective-permute-done((bf16[288,128]{1,0:T(8,128)(2,1)S(1)}, bf16[288,128]{1,0:T(8,128)(2,1)S(1)}, u32[]{:S(2)}, u32[]{:S(2)}) %collective-permute-start.12) | collective-permute-done | bytes 73760 | tf_op jit(solution)/shard_map/ppermute | solution.py:25
  59.8 2.6 %all-to-all-done.1.arrived = bf16[8,56,16,128]{3,2,1,0:T(8,128)(2,1)S(1)} async-done(((bf16[8,56,16,128]{3,2,1,0:T(8,128)(2,1)}), bf16[8,56,16,128]{3,2,1,0:T(8,128)(2,1)S(1)}, u32[]{:S(2)}, u32[]{:S(2)}) %all-to-all-start.1) | async-done | bytes 1835040 | tf_op jit(solution)/shard_map/all_to_all | solution.py:233
  62.4 3.5 %join.3 = (bf16[48,16,128]{2,1,0:T(8,128)(2,1)S(1)}, bf16[48,16,128]{2,1,0:T(8,128)(2,1)S(1)}, bf16[48,16,128]{2,1,0:T(8,128)(2,1)S(1)}, bf16[48,16,128]{2,1,0:T...) custom-call(s32[3,8]{1,0:T(4,128)S(1)} %pad_add_fusion.1.ends, ...), custom_call_target="tpu_custom_call" | custom-call | tf_op jit(solution)/shard_map/join/pallas_call | solution.py:212
  65.9 0.4 widen.3
  66.3 1.1 convolution_convert_fusion
  67.5 0.9 copy-done.2
  68.3 1.1 convolution_convert_fusion.1
  69.5 0.7 collective-permute-start.16
  70.1 1.4 collective-permute-start.20
  71.6 2.5 %join.2 = (bf16[48,16,128]{2,1,0:T(8,128)(2,1)S(1)}, bf16[48,16,128]{2,1,0:T(8,128)(2,1)S(1)}, bf16[48,16,128]{2,1,0:T(8,128)(2,1)S(1)}, bf16[48,16,128]{2,1,0:T...) custom-call(s32[3,8]{1,0:T(4,128)S(1)} %pad_add_fusion.1.ends, ...), custom_call_target="tpu_custom_call" | custom-call | tf_op jit(solution)/shard_map/join/pallas_call | solution.py:212
  74.0 1.9 %collective-permute-start.2 = (bf16[24,16,128]{2,1,0:T(8,128)(2,1)S(1)}, bf16[24,16,128]{2,1,0:T(8,128)(2,1)S(1)}, u32[]{:S(2)}, u32[]{:S(2)}) collective-permute-start(bf16[24,16,128]{2,1,0:T(8,128)(2,1)S(1)} %get-tuple-element.61), channel_id=1, source_target_pairs={{0,32},{32,64},{64,96},{96,128},{128,160},{160,192},{192,224},{224... | collective-permute-start | bytes 294920 | tf_op jit(solution)/shard_map/ppermute | solution.py:244
  76.1 0.2 convolution_add_fusion.2
  76.4 0.2 convolution_add_fusion.1
  76.7 5.1 %collective-permute-done.6 = bf16[24,16,128]{2,1,0:T(8,128)(2,1)S(1)} collective-permute-done((bf16[24,16,128]{2,1,0:T(8,128)(2,1)S(1)}, bf16[24,16,128]{2,1,0:T(8,128)(2,1)S(1)}, u32[]{:S(2)}, u32[]{:S(2)}) %collective-permute-start.6) | collective-permute-done | bytes 98336 | tf_op jit(solution)/shard_map/ppermute | solution.py:244
  82.0 3.3 %collective-permute-start.3 = (bf16[48,16,128]{2,1,0:T(8,128)(2,1)S(1)}, bf16[48,16,128]{2,1,0:T(8,128)(2,1)S(1)}, u32[]{:S(2)}, u32[]{:S(2)}) collective-permute-start(bf16[48,16,128]{2,1,0:T(8,128)(2,1)S(1)} %pad_maximum_fusion.1), channel_id=1, source_target_pairs={{0,32},{32,64},{64,96},{96,128},{128,160},{160,192},{192,224},{224... | collective-permute-start | bytes 589832 | tf_op jit(solution)/shard_map/ppermute | solution.py:244
  85.6 3.3 %collective-permute-start.17 = (bf16[48,16,128]{2,1,0:T(8,128)(2,1)S(1)}, bf16[48,16,128]{2,1,0:T(8,128)(2,1)S(1)}, u32[]{:S(2)}, u32[]{:S(2)}) collective-permute-start(bf16[48,16,128]{2,1,0:T(8,128)(2,1)S(1)} %pad_maximum_fusion.4), channel_id=1, source_target_pairs={{0,32},{32,64},{64,96},{96,128},{128,160},{160,192},{192,224},{224... | collective-permute-start | bytes 589832 | tf_op jit(solution)/shard_map/ppermute | solution.py:244
  88.8 1.7 %collective-permute-done.7 = bf16[48,16,128]{2,1,0:T(8,128)(2,1)S(1)} collective-permute-done((bf16[48,16,128]{2,1,0:T(8,128)(2,1)S(1)}, bf16[48,16,128]{2,1,0:T(8,128)(2,1)S(1)}, u32[]{:S(2)}, u32[]{:S(2)}) %collective-permute-start.7) | collective-permute-done | bytes 196640 | tf_op jit(solution)/shard_map/ppermute | solution.py:244
  90.8 3.3 %collective-permute-start.4 = (bf16[48,16,128]{2,1,0:T(8,128)(2,1)S(1)}, bf16[48,16,128]{2,1,0:T(8,128)(2,1)S(1)}, u32[]{:S(2)}, u32[]{:S(2)}) collective-permute-start(bf16[48,16,128]{2,1,0:T(8,128)(2,1)S(1)} %add_convert_fusion.7), channel_id=1, source_target_pairs={{0,32},{32,64},{64,96},{96,128},{128,160},{160,192},{192,224},{224... | collective-permute-start | bytes 589832 | tf_op jit(solution)/shard_map/ppermute | solution.py:244
  94.1 0.7 collective-permute-done.21
  95.0 3.5 %collective-permute-start.18 = (bf16[48,16,128]{2,1,0:T(8,128)(2,1)S(1)}, bf16[48,16,128]{2,1,0:T(8,128)(2,1)S(1)}, u32[]{:S(2)}, u32[]{:S(2)}) collective-permute-start(bf16[48,16,128]{2,1,0:T(8,128)(2,1)S(1)} %add_convert_fusion.3), channel_id=1, source_target_pairs={{0,32},{32,64},{64,96},{96,128},{128,160},{160,192},{192,224},{224... | collective-permute-start | bytes 589832 | tf_op jit(solution)/shard_map/ppermute | solution.py:244
  98.5 0.6 collective-permute-done.8
  99.3 4.7 %collective-permute-done.22 = bf16[48,16,128]{2,1,0:T(8,128)(2,1)S(1)} collective-permute-done((bf16[48,16,128]{2,1,0:T(8,128)(2,1)S(1)}, bf16[48,16,128]{2,1,0:T(8,128)(2,1)S(1)}, u32[]{:S(2)}, u32[]{:S(2)}) %collective-permute-start.22) | collective-permute-done | bytes 196640 | tf_op jit(solution)/shard_map/ppermute | solution.py:244
  104.2 3.4 %collective-permute-start.19 = (bf16[48,16,128]{2,1,0:T(8,128)(2,1)S(1)}, bf16[48,16,128]{2,1,0:T(8,128)(2,1)S(1)}, u32[]{:S(2)}, u32[]{:S(2)}) collective-permute-start(bf16[48,16,128]{2,1,0:T(8,128)(2,1)S(1)} %add_convert_fusion.2), channel_id=1, source_target_pairs={{0,32},{32,64},{64,96},{96,128},{128,160},{160,192},{192,224},{224... | collective-permute-start | bytes 589832 | tf_op jit(solution)/shard_map/ppermute | solution.py:244
  107.8 3.2 %collective-permute-done.23 = bf16[48,16,128]{2,1,0:T(8,128)(2,1)S(1)} collective-permute-done((bf16[48,16,128]{2,1,0:T(8,128)(2,1)S(1)}, bf16[48,16,128]{2,1,0:T(8,128)(2,1)S(1)}, u32[]{:S(2)}, u32[]{:S(2)}) %collective-permute-start.23) | collective-permute-done | bytes 196640 | tf_op jit(solution)/shard_map/ppermute | solution.py:244
  111.3 2.1 %collective-permute-done.5 = bf16[48,16,128]{2,1,0:T(8,128)(2,1)S(1)} collective-permute-done((bf16[48,16,128]{2,1,0:T(8,128)(2,1)S(1)}, bf16[48,16,128]{2,1,0:T(8,128)(2,1)S(1)}, u32[]{:S(2)}, u32[]{:S(2)}) %collective-permute-start.5) | collective-permute-done | bytes 196640 | tf_op jit(solution)/shard_map/ppermute | solution.py:244
  113.9 3.3 %collective-permute-start.14 = (bf16[96,128]{1,0:T(8,128)(2,1)S(1)}, bf16[96,128]{1,0:T(8,128)(2,1)S(1)}, u32[]{:S(2)}, u32[]{:S(2)}) collective-permute-start(bf16[96,128]{1,0:T(8,128)(2,1)S(1)} %get-tuple-element.119), channel_id=1, source_target_pairs={{1,2},{2,1},{5,6},{6,5},{9,10},{10,9},{13,14},{14,13},{17,18},{18,... | collective-permute-start | bytes 73736 | tf_op jit(solution)/shard_map/ppermute | solution.py:25
  117.3 2.2 %collective-permute-start.24 = (bf16[96,128]{1,0:T(8,128)(2,1)S(1)}, bf16[96,128]{1,0:T(8,128)(2,1)S(1)}, u32[]{:S(2)}, u32[]{:S(2)}) collective-permute-start(bf16[96,128]{1,0:T(8,128)(2,1)S(1)} %get-tuple-element.115), channel_id=1, source_target_pairs={{1,2},{2,1},{5,6},{6,5},{9,10},{10,9},{13,14},{14,13},{17,18},{18,... | collective-permute-start | bytes 73736 | tf_op jit(solution)/shard_map/ppermute | solution.py:25
  119.8 0.3 convolution_convert_fusion.3
  120.0 1.1 fusion.65
  121.1 1.4 collective-permute-done.24
  122.7 0.3 convolution_convert_fusion.2
  122.9 1.1 fusion.64
  124.1 5.2 %collective-permute-start.27 = (f16[16,48,128]{2,1,0:T(8,128)(2,1)S(1)}, f16[16,48,128]{2,1,0:T(8,128)(2,1)S(1)}, u32[]{:S(2)}, u32[]{:S(2)}) collective-permute-start(f16[16,48,128]{2,1,0:T(8,128)(2,1)S(1)} %bitcast.115), channel_id=1, source_target_pairs={{32,64},{64,32},{96,128},{128,96},{160,192},{192,160},{33,65},{65,... | collective-permute-start | bytes 589832 | tf_op jit(solution)/shard_map/ppermute | solution.py:25
  129.5 3.5 %collective-permute-done.27 = f16[16,48,128]{2,1,0:T(8,128)(2,1)S(1)} collective-permute-done((f16[16,48,128]{2,1,0:T(8,128)(2,1)S(1)}, f16[16,48,128]{2,1,0:T(8,128)(2,1)S(1)}, u32[]{:S(2)}, u32[]{:S(2)}) %collective-permute-start.27) | collective-permute-done | bytes 196640 | tf_op jit(solution)/shard_map/ppermute | solution.py:25
  133.0 2.1 %collective-permute-done.26 = f16[16,48,128]{2,1,0:T(8,128)(2,1)S(1)} collective-permute-done((f16[16,48,128]{2,1,0:T(8,128)(2,1)S(1)}, f16[16,48,128]{2,1,0:T(8,128)(2,1)S(1)}, u32[]{:S(2)}, u32[]{:S(2)}) %collective-permute-start.26) | collective-permute-done | bytes 196640 | tf_op jit(solution)/shard_map/ppermute | solution.py:25
  135.2 0.6 collective-permute-start.28
  135.8 6.8 %collective-permute-start.29 = (f16[16,16,128]{2,1,0:T(8,128)(2,1)S(1)}, f16[16,16,128]{2,1,0:T(8,128)(2,1)S(1)}, u32[]{:S(2)}, u32[]{:S(2)}) collective-permute-start(f16[16,16,128]{2,1,0:T(8,128)(2,1)S(1)} %get-tuple-element.105), channel_id=1, source_target_pairs={{4,8},{8,4},{12,16},{16,12},{20,24},{24,20},{5,9},{9,5},{13,17},{1... | collective-permute-start | bytes 196616 | tf_op jit(solution)/shard_map/ppermute | solution.py:25
  142.7 2.2 %collective-permute-done.29 = f16[16,16,128]{2,1,0:T(8,128)(2,1)S(1)} collective-permute-done((f16[16,16,128]{2,1,0:T(8,128)(2,1)S(1)}, f16[16,16,128]{2,1,0:T(8,128)(2,1)S(1)}, u32[]{:S(2)}, u32[]{:S(2)}) %collective-permute-start.29) | collective-permute-done | bytes 65568 | tf_op jit(solution)/shard_map/ppermute | solution.py:25
  144.9 0.7 fusion.22
  (128 shorter events, 5.1 us)
Async XLA Ops:
  0.0 12.6 %copy-start.5 = (bf16[6,48,2,8,128]{4,3,2,1,0:T(8,128)(2,1)S(1)}, bf16[6,48,2,8,128]{4,3,2,1,0:T(8,128)(2,1)}, u32[]{:S(2)}) copy-start(bf16[6,48,2,8,128]{4,3,2,1,0:T(8,128)(2,1)} %param.6) | copy-start | bytes 3538948
  1.0 19.2 %collective-permute-start.1 = (bf16[16,16,128]{2,1,0:T(8,128)(2,1)S(1)}, bf16[16,16,128]{2,1,0:T(8,128)(2,1)S(1)}, u32[]{:S(2)}, u32[]{:S(2)}) collective-permute-start(bf16[16,16,128]{2,1,0:T(8,128)(2,1)S(1)} %convert_element_type.224), channel_id=1, source_target_pairs={{4,8},{8,4},{12,16},{16,12},{20,24},{24,20},{5,9},{9,5},{13,17},{1... | collective-permute-start | bytes 196616 | tf_op jit(solution)/shard_map/ppermute | solution.py:25
  5.2 15.0 %collective-permute-start = (bf16[16,16,128]{2,1,0:T(8,128)(2,1)S(1)}, bf16[16,16,128]{2,1,0:T(8,128)(2,1)S(1)}, u32[]{:S(2)}, u32[]{:S(2)}) collective-permute-start(bf16[16,16,128]{2,1,0:T(8,128)(2,1)S(1)} %convert_element_type.224), channel_id=1, source_target_pairs={{0,4},{4,0},{8,12},{12,8},{16,20},{20,16},{24,28},{28,24},{1,5},{5... | collective-permute-start | bytes 196616 | tf_op jit(solution)/shard_map/ppermute | solution.py:25
  13.3 1.1 copy-start.3
  14.5 5.7 %copy-start.9 = (f32[6,3,31]{2,1,0:T(4,128)S(1)}, f32[6,3,31]{2,1,0:T(4,128)}, u32[]{:S(2)}) copy-start(f32[6,3,31]{2,1,0:T(4,128)} %param.8) | copy-start | bytes 6700
  18.8 1.3 copy-start
  27.4 14.8 %collective-permute-start.11 = (bf16[16,48,128]{2,1,0:T(8,128)(2,1)S(1)}, bf16[16,48,128]{2,1,0:T(8,128)(2,1)}, u32[]{:S(2)}, u32[]{:S(2)}) collective-permute-start(bf16[16,48,128]{2,1,0:T(8,128)(2,1)S(1)} %pad_maximum_fusion.3), channel_id=1, source_target_pairs={{0,32},{32,0},{64,96},{96,64},{128,160},{160,128},{192,224},{224,1... | collective-permute-start | bytes 589832 | tf_op jit(solution)/shard_map/ppermute | solution.py:25
  27.6 14.6 %collective-permute-start.10 = (bf16[16,48,128]{2,1,0:T(8,128)(2,1)S(1)}, bf16[16,48,128]{2,1,0:T(8,128)(2,1)}, u32[]{:S(2)}, u32[]{:S(2)}) collective-permute-start(bf16[16,48,128]{2,1,0:T(8,128)(2,1)S(1)} %pad_maximum_fusion.3), channel_id=1, source_target_pairs={{32,64},{64,32},{96,128},{128,96},{160,192},{192,160},{33,65},{65,... | collective-permute-start | bytes 589832 | tf_op jit(solution)/shard_map/ppermute | solution.py:25
  33.5 28.9 %all-to-all-start.1 = ((bf16[8,56,16,128]{3,2,1,0:T(8,128)(2,1)}), bf16[8,56,16,128]{3,2,1,0:T(8,128)(2,1)S(1)}, u32[]{:S(2)}, u32[]{:S(2)}) async-start(bf16[8,56,16,128]{3,2,1,0:T(8,128)(2,1)} %copy-done), calls=%async_computation.1 | async-start | bytes 3670016 | tf_op jit(solution)/shard_map/all_to_all | solution.py:233
  39.2 1.6 %copy-start.8 = (s32[256,128]{1,0:T(8,128)S(1)}, s32[256,128]{1,0:T(8,128)}, u32[]{:S(2)}) copy-start(s32[256,128]{1,0:T(8,128)} %get-tuple-element.123) | copy-start | bytes 393220
  43.7 4.4 %collective-permute-start.13 = (bf16[288,128]{1,0:T(8,128)(2,1)S(1)}, bf16[288,128]{1,0:T(8,128)(2,1)S(1)}, u32[]{:S(2)}, u32[]{:S(2)}) collective-permute-start(bf16[288,128]{1,0:T(8,128)(2,1)S(1)} %get-tuple-element.108), channel_id=1, source_target_pairs={{0,1},{1,0},{2,3},{3,2},{4,5},{5,4},{6,7},{7,6},{8,9},{9,8},{10,11... | collective-permute-start | bytes 221192 | tf_op jit(solution)/shard_map/ppermute | solution.py:25
  43.8 16.0 %collective-permute-start.12 = (bf16[288,128]{1,0:T(8,128)(2,1)S(1)}, bf16[288,128]{1,0:T(8,128)(2,1)S(1)}, u32[]{:S(2)}, u32[]{:S(2)}) collective-permute-start(bf16[288,128]{1,0:T(8,128)(2,1)S(1)} %get-tuple-element.109), channel_id=1, source_target_pairs={{1,2},{2,1},{5,6},{6,5},{9,10},{10,9},{13,14},{14,13},{17,18},{18,... | collective-permute-start | bytes 221192 | tf_op jit(solution)/shard_map/ppermute | solution.py:25
  62.4 3.9 %copy-start.1 = (bf16[48,48,768]{2,1,0:T(8,128)(2,1)S(1)}, bf16[48,48,768]{2,1,0:T(8,128)(2,1)}, u32[]{:S(2)}) copy-start(bf16[48,48,768]{2,1,0:T(8,128)(2,1)} %multiply_convert_fusion) | copy-start | bytes 10616836
  66.3 2.0 %copy-start.2 = (bf16[48,48,768]{2,1,0:T(8,128)(2,1)S(1)}, bf16[48,48,768]{2,1,0:T(8,128)(2,1)}, u32[]{:S(2)}) copy-start(bf16[48,48,768]{2,1,0:T(8,128)(2,1)} %multiply_convert_fusion.1) | copy-start | bytes 10616836
  68.3 3.2 %copy-start.4 = (bf16[8,40,16,128]{3,2,1,0:T(8,128)(2,1)S(1)}, bf16[8,40,16,128]{3,2,1,0:T(8,128)(2,1)}, u32[]{:S(2)}) copy-start(bf16[8,40,16,128]{3,2,1,0:T(8,128)(2,1)} %copy-done.3) | copy-start | bytes 3932164
  69.5 16.0 %collective-permute-start.16 = (bf16[24,16,128]{2,1,0:T(8,128)(2,1)S(1)}, bf16[24,16,128]{2,1,0:T(8,128)(2,1)S(1)}, u32[]{:S(2)}, u32[]{:S(2)}) collective-permute-start(bf16[24,16,128]{2,1,0:T(8,128)(2,1)S(1)} %get-tuple-element.81), channel_id=1, source_target_pairs={{0,32},{32,64},{64,96},{96,128},{128,160},{160,192},{192,224},{224... | collective-permute-start | bytes 294920 | tf_op jit(solution)/shard_map/ppermute | solution.py:244
  70.1 6.0 %copy-start.6 = (bf16[3,256,128]{2,0,1:T(4,128)(2,1)S(1)}, bf16[3,256,128]{2,0,1:T(4,128)(2,1)}, u32[]{:S(2)}) copy-start(bf16[3,256,128]{2,0,1:T(4,128)(2,1)} %get-tuple-element.97) | copy-start | bytes 589828
  70.1 15.2 %collective-permute-start.20 = (bf16[24,16,128]{2,1,0:T(8,128)(2,1)S(1)}, bf16[24,16,128]{2,1,0:T(8,128)(2,1)S(1)}, u32[]{:S(2)}, u32[]{:S(2)}) collective-permute-start(bf16[24,16,128]{2,1,0:T(8,128)(2,1)S(1)} %get-tuple-element.85), channel_id=1, source_target_pairs={{32,0},{64,32},{96,64},{128,96},{160,128},{192,160},{224,192},{0,2... | collective-permute-start | bytes 294920 | tf_op jit(solution)/shard_map/ppermute | solution.py:244
  74.0 7.9 %collective-permute-start.2 = (bf16[24,16,128]{2,1,0:T(8,128)(2,1)S(1)}, bf16[24,16,128]{2,1,0:T(8,128)(2,1)S(1)}, u32[]{:S(2)}, u32[]{:S(2)}) collective-permute-start(bf16[24,16,128]{2,1,0:T(8,128)(2,1)S(1)} %get-tuple-element.61), channel_id=1, source_target_pairs={{0,32},{32,64},{64,96},{96,128},{128,160},{160,192},{192,224},{224... | collective-permute-start | bytes 294920 | tf_op jit(solution)/shard_map/ppermute | solution.py:244
  76.0 5.8 %collective-permute-start.6 = (bf16[24,16,128]{2,1,0:T(8,128)(2,1)S(1)}, bf16[24,16,128]{2,1,0:T(8,128)(2,1)S(1)}, u32[]{:S(2)}, u32[]{:S(2)}) collective-permute-start(bf16[24,16,128]{2,1,0:T(8,128)(2,1)S(1)} %get-tuple-element.65), channel_id=1, source_target_pairs={{32,0},{64,32},{96,64},{128,96},{160,128},{192,160},{224,192},{0,2... | collective-permute-start | bytes 294920 | tf_op jit(solution)/shard_map/ppermute | solution.py:244
  81.9 8.7 %collective-permute-start.7 = (bf16[48,16,128]{2,1,0:T(8,128)(2,1)S(1)}, bf16[48,16,128]{2,1,0:T(8,128)(2,1)S(1)}, u32[]{:S(2)}, u32[]{:S(2)}) collective-permute-start(bf16[48,16,128]{2,1,0:T(8,128)(2,1)S(1)} %pad_maximum_fusion.2), channel_id=1, source_target_pairs={{32,0},{64,32},{96,64},{128,96},{160,128},{192,160},{224,192},{0,2... | collective-permute-start | bytes 589832 | tf_op jit(solution)/shard_map/ppermute | solution.py:244
  82.0 8.7 %collective-permute-start.3 = (bf16[48,16,128]{2,1,0:T(8,128)(2,1)S(1)}, bf16[48,16,128]{2,1,0:T(8,128)(2,1)S(1)}, u32[]{:S(2)}, u32[]{:S(2)}) collective-permute-start(bf16[48,16,128]{2,1,0:T(8,128)(2,1)S(1)} %pad_maximum_fusion.1), channel_id=1, source_target_pairs={{0,32},{32,64},{64,96},{96,128},{128,160},{160,192},{192,224},{224... | collective-permute-start | bytes 589832 | tf_op jit(solution)/shard_map/ppermute | solution.py:244
  85.4 9.4 %collective-permute-start.21 = (bf16[48,16,128]{2,1,0:T(8,128)(2,1)S(1)}, bf16[48,16,128]{2,1,0:T(8,128)(2,1)S(1)}, u32[]{:S(2)}, u32[]{:S(2)}) collective-permute-start(bf16[48,16,128]{2,1,0:T(8,128)(2,1)S(1)} %pad_maximum_fusion.5), channel_id=1, source_target_pairs={{32,0},{64,32},{96,64},{128,96},{160,128},{192,160},{224,192},{0,2... | collective-permute-start | bytes 589832 | tf_op jit(solution)/shard_map/ppermute | solution.py:244
  85.6 9.4 %collective-permute-start.17 = (bf16[48,16,128]{2,1,0:T(8,128)(2,1)S(1)}, bf16[48,16,128]{2,1,0:T(8,128)(2,1)S(1)}, u32[]{:S(2)}, u32[]{:S(2)}) collective-permute-start(bf16[48,16,128]{2,1,0:T(8,128)(2,1)S(1)} %pad_maximum_fusion.4), channel_id=1, source_target_pairs={{0,32},{32,64},{64,96},{96,128},{128,160},{160,192},{192,224},{224... | collective-permute-start | bytes 589832 | tf_op jit(solution)/shard_map/ppermute | solution.py:244
  90.6 8.5 %collective-permute-start.8 = (bf16[48,16,128]{2,1,0:T(8,128)(2,1)S(1)}, bf16[48,16,128]{2,1,0:T(8,128)(2,1)S(1)}, u32[]{:S(2)}, u32[]{:S(2)}) collective-permute-start(bf16[48,16,128]{2,1,0:T(8,128)(2,1)S(1)} %add_convert_fusion.5), channel_id=1, source_target_pairs={{32,0},{64,32},{96,64},{128,96},{160,128},{192,160},{224,192},{0,2... | collective-permute-start | bytes 589832 | tf_op jit(solution)/shard_map/ppermute | solution.py:244
  90.8 16.8 %collective-permute-start.4 = (bf16[48,16,128]{2,1,0:T(8,128)(2,1)S(1)}, bf16[48,16,128]{2,1,0:T(8,128)(2,1)S(1)}, u32[]{:S(2)}, u32[]{:S(2)}) collective-permute-start(bf16[48,16,128]{2,1,0:T(8,128)(2,1)S(1)} %add_convert_fusion.7), channel_id=1, source_target_pairs={{0,32},{32,64},{64,96},{96,128},{128,160},{160,192},{192,224},{224... | collective-permute-start | bytes 589832 | tf_op jit(solution)/shard_map/ppermute | solution.py:244
  94.8 9.1 %collective-permute-start.22 = (bf16[48,16,128]{2,1,0:T(8,128)(2,1)S(1)}, bf16[48,16,128]{2,1,0:T(8,128)(2,1)S(1)}, u32[]{:S(2)}, u32[]{:S(2)}) collective-permute-start(bf16[48,16,128]{2,1,0:T(8,128)(2,1)S(1)} %add_convert_fusion.1), channel_id=1, source_target_pairs={{32,0},{64,32},{96,64},{128,96},{160,128},{192,160},{224,192},{0,2... | collective-permute-start | bytes 589832 | tf_op jit(solution)/shard_map/ppermute | solution.py:244
  95.0 9.1 %collective-permute-start.18 = (bf16[48,16,128]{2,1,0:T(8,128)(2,1)S(1)}, bf16[48,16,128]{2,1,0:T(8,128)(2,1)S(1)}, u32[]{:S(2)}, u32[]{:S(2)}) collective-permute-start(bf16[48,16,128]{2,1,0:T(8,128)(2,1)S(1)} %add_convert_fusion.3), channel_id=1, source_target_pairs={{0,32},{32,64},{64,96},{96,128},{128,160},{160,192},{192,224},{224... | collective-permute-start | bytes 589832 | tf_op jit(solution)/shard_map/ppermute | solution.py:244
  99.2 12.1 %collective-permute-start.9 = (bf16[48,16,128]{2,1,0:T(8,128)(2,1)S(1)}, bf16[48,16,128]{2,1,0:T(8,128)(2,1)S(1)}, u32[]{:S(2)}, u32[]{:S(2)}) collective-permute-start(bf16[48,16,128]{2,1,0:T(8,128)(2,1)S(1)} %add_convert_fusion.4), channel_id=1, source_target_pairs={{32,0},{64,32},{96,64},{128,96},{160,128},{192,160},{224,192},{0,2... | collective-permute-start | bytes 589832 | tf_op jit(solution)/shard_map/ppermute | solution.py:244
  104.0 7.0 %collective-permute-start.23 = (bf16[48,16,128]{2,1,0:T(8,128)(2,1)S(1)}, bf16[48,16,128]{2,1,0:T(8,128)(2,1)S(1)}, u32[]{:S(2)}, u32[]{:S(2)}) collective-permute-start(bf16[48,16,128]{2,1,0:T(8,128)(2,1)S(1)} %add_convert_fusion), channel_id=1, source_target_pairs={{32,0},{64,32},{96,64},{128,96},{160,128},{192,160},{224,192},{0,2... | collective-permute-start | bytes 589832 | tf_op jit(solution)/shard_map/ppermute | solution.py:244
  104.2 6.8 %collective-permute-start.19 = (bf16[48,16,128]{2,1,0:T(8,128)(2,1)S(1)}, bf16[48,16,128]{2,1,0:T(8,128)(2,1)S(1)}, u32[]{:S(2)}, u32[]{:S(2)}) collective-permute-start(bf16[48,16,128]{2,1,0:T(8,128)(2,1)S(1)} %add_convert_fusion.2), channel_id=1, source_target_pairs={{0,32},{32,64},{64,96},{96,128},{128,160},{160,192},{192,224},{224... | collective-permute-start | bytes 589832 | tf_op jit(solution)/shard_map/ppermute | solution.py:244
  107.7 5.7 %collective-permute-start.5 = (bf16[48,16,128]{2,1,0:T(8,128)(2,1)S(1)}, bf16[48,16,128]{2,1,0:T(8,128)(2,1)S(1)}, u32[]{:S(2)}, u32[]{:S(2)}) collective-permute-start(bf16[48,16,128]{2,1,0:T(8,128)(2,1)S(1)} %add_convert_fusion.6), channel_id=1, source_target_pairs={{0,32},{32,64},{64,96},{96,128},{128,160},{160,192},{192,224},{224... | collective-permute-start | bytes 589832 | tf_op jit(solution)/shard_map/ppermute | solution.py:244
  113.8 5.8 %collective-permute-start.15 = (bf16[96,128]{1,0:T(8,128)(2,1)S(1)}, bf16[96,128]{1,0:T(8,128)(2,1)S(1)}, u32[]{:S(2)}, u32[]{:S(2)}) collective-permute-start(bf16[96,128]{1,0:T(8,128)(2,1)S(1)} %get-tuple-element.118), channel_id=1, source_target_pairs={{0,1},{1,0},{2,3},{3,2},{4,5},{5,4},{6,7},{7,6},{8,9},{9,8},{10,11... | collective-permute-start | bytes 73736 | tf_op jit(solution)/shard_map/ppermute | solution.py:25
  113.9 5.7 %collective-permute-start.14 = (bf16[96,128]{1,0:T(8,128)(2,1)S(1)}, bf16[96,128]{1,0:T(8,128)(2,1)S(1)}, u32[]{:S(2)}, u32[]{:S(2)}) collective-permute-start(bf16[96,128]{1,0:T(8,128)(2,1)S(1)} %get-tuple-element.119), channel_id=1, source_target_pairs={{1,2},{2,1},{5,6},{6,5},{9,10},{10,9},{13,14},{14,13},{17,18},{18,... | collective-permute-start | bytes 73736 | tf_op jit(solution)/shard_map/ppermute | solution.py:25
  117.2 3.9 %collective-permute-start.25 = (bf16[96,128]{1,0:T(8,128)(2,1)S(1)}, bf16[96,128]{1,0:T(8,128)(2,1)S(1)}, u32[]{:S(2)}, u32[]{:S(2)}) collective-permute-start(bf16[96,128]{1,0:T(8,128)(2,1)S(1)} %get-tuple-element.114), channel_id=1, source_target_pairs={{0,1},{1,0},{2,3},{3,2},{4,5},{5,4},{6,7},{7,6},{8,9},{9,8},{10,11... | collective-permute-start | bytes 73736 | tf_op jit(solution)/shard_map/ppermute | solution.py:25
  117.3 5.1 %collective-permute-start.24 = (bf16[96,128]{1,0:T(8,128)(2,1)S(1)}, bf16[96,128]{1,0:T(8,128)(2,1)S(1)}, u32[]{:S(2)}, u32[]{:S(2)}) collective-permute-start(bf16[96,128]{1,0:T(8,128)(2,1)S(1)} %get-tuple-element.115), channel_id=1, source_target_pairs={{1,2},{2,1},{5,6},{6,5},{9,10},{10,9},{13,14},{14,13},{17,18},{18,... | collective-permute-start | bytes 73736 | tf_op jit(solution)/shard_map/ppermute | solution.py:25
  124.1 20.8 %copy-start.7 = (f32[16,16,128]{2,1,0:T(8,128)S(1)}, f32[16,16,128]{2,1,0:T(8,128)}, u32[]{:S(2)}) copy-start(f32[16,16,128]{2,1,0:T(8,128)} %param.9) | copy-start | bytes 393220
  124.1 8.9 %collective-permute-start.27 = (f16[16,48,128]{2,1,0:T(8,128)(2,1)S(1)}, f16[16,48,128]{2,1,0:T(8,128)(2,1)S(1)}, u32[]{:S(2)}, u32[]{:S(2)}) collective-permute-start(f16[16,48,128]{2,1,0:T(8,128)(2,1)S(1)} %bitcast.115), channel_id=1, source_target_pairs={{32,64},{64,32},{96,128},{128,96},{160,192},{192,160},{33,65},{65,... | collective-permute-start | bytes 589832 | tf_op jit(solution)/shard_map/ppermute | solution.py:25
  129.4 5.8 %collective-permute-start.26 = (f16[16,48,128]{2,1,0:T(8,128)(2,1)S(1)}, f16[16,48,128]{2,1,0:T(8,128)(2,1)S(1)}, u32[]{:S(2)}, u32[]{:S(2)}) collective-permute-start(f16[16,48,128]{2,1,0:T(8,128)(2,1)S(1)} %bitcast.114), channel_id=1, source_target_pairs={{0,32},{32,0},{64,96},{96,64},{128,160},{160,128},{192,224},{224,1... | collective-permute-start | bytes 589832 | tf_op jit(solution)/shard_map/ppermute | solution.py:25
  135.2 7.4 %collective-permute-start.28 = (f16[16,16,128]{2,1,0:T(8,128)(2,1)S(1)}, f16[16,16,128]{2,1,0:T(8,128)(2,1)S(1)}, u32[]{:S(2)}, u32[]{:S(2)}) collective-permute-start(f16[16,16,128]{2,1,0:T(8,128)(2,1)S(1)} %get-tuple-element.104), channel_id=1, source_target_pairs={{0,4},{4,0},{8,12},{12,8},{16,20},{20,16},{24,28},{28,24},{1,5},{5... | collective-permute-start | bytes 196616 | tf_op jit(solution)/shard_map/ppermute | solution.py:25
  135.8 9.1 %collective-permute-start.29 = (f16[16,16,128]{2,1,0:T(8,128)(2,1)S(1)}, f16[16,16,128]{2,1,0:T(8,128)(2,1)S(1)}, u32[]{:S(2)}, u32[]{:S(2)}) collective-permute-start(f16[16,16,128]{2,1,0:T(8,128)(2,1)S(1)} %get-tuple-element.105), channel_id=1, source_target_pairs={{4,8},{8,4},{12,16},{16,12},{20,24},{24,20},{5,9},{9,5},{13,17},{1... | collective-permute-start | bytes 196616 | tf_op jit(solution)/shard_map/ppermute | solution.py:25

commit v3 on v0

--- a/solution.py
+++ b/solution.py
@@ -308,7 +308,6 @@
             join(c, ends, usual_table[1], late_cell, arrived, late, gz_count, chunk * positions)
         )
         near.append(ring_step(blocks[c][gz_count // 2], blocks[c][gz_count // 2 + 1]))
-        near[c], arrived = lax.optimization_barrier((near[c], arrived))
     joined = [ring_sum(blocks[c], *near[c]) for c in range(chunks)]
     own, column_kernels, _ = lax.optimization_barrier((own, kernels[:, 2], blocks[-1][0]))
     above, below = from_sides(own, own, "gy")

time: 135 us -> 138 us (1.022)
  the two profiles are of different devices: /device:TPU:106 before, /device:TPU:26 now
where the time goes in v3:
time: 138 us
  starting transfers between devices  55.8 us (40%)
  waiting for transfers between devices  47.4 us (34%)
  other arithmetic  11.2 us (8%)
  matrix products  9.52 us (7%)
  Pallas kernels  7.68 us (6%)
  local copies, waits for them, and re-layouts  4.44 us (3%)
  between operations  1.56 us (1%)
    ppermute x16, starting transfers between devices, ring_step(): return (lax.ppermute(upward, 'gz', up), lax.ppermute(downward, 'gz', down))  22.3 us
    ppermute x16, waiting for transfers between devices, ring_step(): return (lax.ppermute(upward, 'gz', up), lax.ppermute(downward, 'gz', down))  18.6 us
    ppermute x7, starting transfers between devices, neighbours(): lax.ppermute(second, axis, pairs[1])  16 us
    all_to_all x1, waiting for transfers between devices, exchange(): return lax.all_to_all(value, 'gy', split_axis=0, concat_axis=0, tiled=True)  12.2 us
    ppermute x7, waiting for transfers between devices, neighbours(): lax.ppermute(second, axis, pairs[1])  10.7 us
    ppermute x7, starting transfers between devices, neighbours(): lax.ppermute(first, axis, pairs[0])  10 us
    all_to_all x1, starting transfers between devices, exchange(): return lax.all_to_all(value, 'gy', split_axis=0, concat_axis=0, tiled=True)  7.37 us
    ppermute x7, waiting for transfers between devices, neighbours(): lax.ppermute(first, axis, pairs[0])  5.93 us
  transfers between devices with their start and end apart: 31, of which 12 were waited for; matrix products, arithmetic and copies ran while one was open for 12% of the time, Pallas kernels for 3%

profile of v3, /device:TPU:26, one launch (start us, length us, event | category | flops | bytes accessed | tf_op | source)
XLA Modules:
  0.0 137.7 jit_solution(17005667865412342041)
XLA Ops:
  0.0 1.1 add_select_fusion
  1.1 1.0 reshape.561
  2.7 0.6 reduce_max.9
  4.3 0.4 select_reduce_fusion.1
  4.7 1.1 pack.3
  5.9 1.3 copy-done
  7.2 7.4 %all-to-all-start.1 = ((bf16[8,56,16,128]{3,2,1,0:T(8,128)(2,1)}), bf16[8,56,16,128]{3,2,1,0:T(8,128)(2,1)S(1)}, u32[]{:S(2)}, u32[]{:S(2)}) async-start(bf16[8,56,16,128]{3,2,1,0:T(8,128)(2,1)} %copy-done), calls=%async_computation.1 | async-start | bytes 3670016 | tf_op jit(solution)/shard_map/all_to_all | solution.py:217
  14.9 0.6 fusion.5
  15.6 0.6 fusion.4
  16.4 2.6 %multiply_convert_fusion.1 = bf16[48,48,768]{2,1,0:T(8,128)(2,1)} fusion(f32[48,768]{1,0:T(8,128)S(1)} %bitcast.109, f32[48,768]{1,0:T(8,128)S(1)} %bitcast.111), kind=kLoop, calls=%fused_computation.5 | loop fusion | flops 3538944 | bytes 3833856 | tf_op jit(solution)/shard_map/convert_element_type | solution.py:300
  19.0 2.7 %multiply_convert_fusion = bf16[48,48,768]{2,1,0:T(8,128)(2,1)} fusion(f32[48,768]{1,0:T(8,128)S(1)} %bitcast.108, f32[48,768]{1,0:T(8,128)S(1)} %bitcast.110), kind=kLoop, calls=%fused_computation.4 | loop fusion | flops 3538944 | bytes 3833856 | tf_op jit(solution)/shard_map/convert_element_type | solution.py:300
  21.7 2.0 %collective-permute-start.9 = (bf16[16,16,128]{2,1,0:T(8,128)(2,1)S(1)}, bf16[16,16,128]{2,1,0:T(8,128)(2,1)S(1)}, u32[]{:S(2)}, u32[]{:S(2)}) collective-permute-start(bf16[16,16,128]{2,1,0:T(8,128)(2,1)S(1)} %convert_element_type.249), channel_id=1, source_target_pairs={{0,32},{32,0},{64,96},{96,64},{128,160},{160,128},{192,224},{224,1... | collective-permute-start | bytes 196616 | tf_op jit(solution)/shard_map/ppermute | solution.py:25
  23.8 0.7 collective-permute-start.8
  24.6 0.3 convert_reduce_fusion.1
  24.9 0.8 fusion.23
  25.8 0.3 collective-permute-done.9
  26.2 12.2 %all-to-all-done.1.arrived = bf16[8,56,16,128]{3,2,1,0:T(8,128)(2,1)S(1)} async-done(((bf16[8,56,16,128]{3,2,1,0:T(8,128)(2,1)}), bf16[8,56,16,128]{3,2,1,0:T(8,128)(2,1)S(1)}, u32[]{:S(2)}, u32[]{:S(2)}) %all-to-all-start.1) | async-done | bytes 1835040 | tf_op jit(solution)/shard_map/all_to_all | solution.py:217
  38.4 2.7 %join.3 = (bf16[48,16,128]{2,1,0:T(8,128)(2,1)S(1)}, bf16[48,16,128]{2,1,0:T(8,128)(2,1)S(1)}, bf16[48,16,128]{2,1,0:T(8,128)(2,1)S(1)}, bf16[48,16,128]{2,1,0:T...) custom-call(s32[3,8]{1,0:T(4,128)S(1)} %pad_add_fusion.1.ends, ...), custom_call_target="tpu_custom_call" | custom-call | tf_op jit(solution)/shard_map/join/pallas_call | solution.py:196
  41.1 1.7 %collective-permute-start.11 = (bf16[48,16,128]{2,1,0:T(8,128)(2,1)S(1)}, bf16[48,16,128]{2,1,0:T(8,128)(2,1)S(1)}, u32[]{:S(2)}, u32[]{:S(2)}) collective-permute-start(bf16[48,16,128]{2,1,0:T(8,128)(2,1)S(1)} %pad_maximum_fusion.3), channel_id=1, source_target_pairs={{0,4},{4,0},{8,12},{12,8},{16,20},{20,16},{24,28},{28,24},{1,5},{5... | collective-permute-start | bytes 589832 | tf_op jit(solution)/shard_map/ppermute | solution.py:25
  42.8 2.7 %collective-permute-start.10 = (bf16[48,16,128]{2,1,0:T(8,128)(2,1)S(1)}, bf16[48,16,128]{2,1,0:T(8,128)(2,1)S(1)}, u32[]{:S(2)}, u32[]{:S(2)}) collective-permute-start(bf16[48,16,128]{2,1,0:T(8,128)(2,1)S(1)} %pad_maximum_fusion.3), channel_id=1, source_target_pairs={{4,8},{8,4},{12,16},{16,12},{20,24},{24,20},{5,9},{9,5},{13,17},{1... | collective-permute-start | bytes 589832 | tf_op jit(solution)/shard_map/ppermute | solution.py:25
  45.5 6.1 %collective-permute-start.20 = (bf16[24,16,128]{2,1,0:T(8,128)(2,1)S(1)}, bf16[24,16,128]{2,1,0:T(8,128)(2,1)S(1)}, u32[]{:S(2)}, u32[]{:S(2)}) collective-permute-start(bf16[24,16,128]{2,1,0:T(8,128)(2,1)S(1)} %get-tuple-element.77), channel_id=1, source_target_pairs={{32,0},{64,32},{96,64},{128,96},{160,128},{192,160},{224,192},{0,2... | collective-permute-start | bytes 294920 | tf_op jit(solution)/shard_map/ppermute | solution.py:228
  51.7 2.5 %join.2 = (bf16[48,16,128]{2,1,0:T(8,128)(2,1)S(1)}, bf16[48,16,128]{2,1,0:T(8,128)(2,1)S(1)}, bf16[48,16,128]{2,1,0:T(8,128)(2,1)S(1)}, bf16[48,16,128]{2,1,0:T...) custom-call(s32[3,8]{1,0:T(4,128)S(1)} %pad_add_fusion.1.ends, ...), custom_call_target="tpu_custom_call" | custom-call | tf_op jit(solution)/shard_map/join/pallas_call | solution.py:196
  54.2 1.4 collective-permute-start.4
  55.5 1.4 %fusion.6 = bf16[6,256,128]{2,0,1:T(8,128)(2,1)S(1)} fusion(s32[256,128]{1,0:T(8,128)S(1)} %copy-done.6, f32[6,31]{1,0:T(8,128)S(1)} %slice_bitcast_fusion.2), kind=kOutput, calls=%fused_computation.19 | convolution fusion | flops 74350592 | bytes 525032 | tf_op jit(solution)/shard_map/eim,vm->vei/dot_general | solution.py:89
  57.1 1.4 %fusion.7 = bf16[6,256,128]{2,0,1:T(8,128)(2,1)S(1)} fusion(s32[256,128]{1,0:T(8,128)S(1)} %copy-done.5, f32[6,31]{1,0:T(8,128)S(1)} %slice_bitcast_fusion.2), kind=kOutput, calls=%fused_computation.20 | convolution fusion | flops 74350592 | bytes 525032 | tf_op jit(solution)/shard_map/eim,vm->vei/dot_general | solution.py:89
  58.8 1.0 collective-permute-start.16
  59.9 5.8 %collective-permute-done = bf16[24,16,128]{2,1,0:T(8,128)(2,1)S(1)} collective-permute-done((bf16[24,16,128]{2,1,0:T(8,128)(2,1)S(1)}, bf16[24,16,128]{2,1,0:T(8,128)(2,1)S(1)}, u32[]{:S(2)}, u32[]{:S(2)}) %collective-permute-start) | collective-permute-done | bytes 98336 | tf_op jit(solution)/shard_map/ppermute | solution.py:228
  65.7 1.0 collective-permute-start.5
  66.8 1.1 collective-permute-start.1
  68.0 2.3 %collective-permute-start.21 = (bf16[48,16,128]{2,1,0:T(8,128)(2,1)S(1)}, bf16[48,16,128]{2,1,0:T(8,128)(2,1)S(1)}, u32[]{:S(2)}, u32[]{:S(2)}) collective-permute-start(bf16[48,16,128]{2,1,0:T(8,128)(2,1)S(1)} %pad_maximum_fusion.5), channel_id=1, source_target_pairs={{32,0},{64,32},{96,64},{128,96},{160,128},{192,160},{224,192},{0,2... | collective-permute-start | bytes 589832 | tf_op jit(solution)/shard_map/ppermute | solution.py:228
  70.4 0.3 edges.3
  70.9 2.7 %collective-permute-start.12 = (bf16[288,128]{1,0:T(8,128)(2,1)S(1)}, bf16[288,128]{1,0:T(8,128)(2,1)S(1)}, u32[]{:S(2)}, u32[]{:S(2)}) collective-permute-start(bf16[288,128]{1,0:T(8,128)(2,1)S(1)} %get-tuple-element.101), channel_id=1, source_target_pairs={{1,2},{2,1},{5,6},{6,5},{9,10},{10,9},{13,14},{14,13},{17,18},{18,... | collective-permute-start | bytes 221192 | tf_op jit(solution)/shard_map/ppermute | solution.py:25
  73.7 2.9 %collective-permute-done.12 = bf16[288,128]{1,0:T(8,128)(2,1)S(1)} collective-permute-done((bf16[288,128]{1,0:T(8,128)(2,1)S(1)}, bf16[288,128]{1,0:T(8,128)(2,1)S(1)}, u32[]{:S(2)}, u32[]{:S(2)}) %collective-permute-start.12) | collective-permute-done | bytes 73760 | tf_op jit(solution)/shard_map/ppermute | solution.py:25
  76.7 0.4 widen.3
  77.1 1.1 convolution_convert_fusion
  78.2 0.9 copy-done.2
  79.1 1.1 convolution_convert_fusion.1
  80.2 0.2 convolution_add_fusion.2
  80.5 0.2 convolution_add_fusion.1
  80.8 0.6 collective-permute-start.6
  81.5 1.8 %collective-permute-start.2 = (bf16[48,16,128]{2,1,0:T(8,128)(2,1)S(1)}, bf16[48,16,128]{2,1,0:T(8,128)(2,1)S(1)}, u32[]{:S(2)}, u32[]{:S(2)}) collective-permute-start(bf16[48,16,128]{2,1,0:T(8,128)(2,1)S(1)} %add_convert_fusion.7), channel_id=1, source_target_pairs={{0,32},{32,64},{64,96},{96,128},{128,160},{160,192},{192,224},{224... | collective-permute-start | bytes 589832 | tf_op jit(solution)/shard_map/ppermute | solution.py:228
  83.3 1.6 %collective-permute-start.22 = (bf16[48,16,128]{2,1,0:T(8,128)(2,1)S(1)}, bf16[48,16,128]{2,1,0:T(8,128)(2,1)S(1)}, u32[]{:S(2)}, u32[]{:S(2)}) collective-permute-start(bf16[48,16,128]{2,1,0:T(8,128)(2,1)S(1)} %add_convert_fusion.1), channel_id=1, source_target_pairs={{32,0},{64,32},{96,64},{128,96},{160,128},{192,160},{224,192},{0,2... | collective-permute-start | bytes 589832 | tf_op jit(solution)/shard_map/ppermute | solution.py:228
  85.0 0.6 collective-permute-start.18
  85.6 2.8 %collective-permute-done.6 = bf16[48,16,128]{2,1,0:T(8,128)(2,1)S(1)} collective-permute-done((bf16[48,16,128]{2,1,0:T(8,128)(2,1)S(1)}, bf16[48,16,128]{2,1,0:T(8,128)(2,1)S(1)}, u32[]{:S(2)}, u32[]{:S(2)}) %collective-permute-start.6) | collective-permute-done | bytes 196640 | tf_op jit(solution)/shard_map/ppermute | solution.py:228
  88.4 1.9 %collective-permute-start.7 = (bf16[48,16,128]{2,1,0:T(8,128)(2,1)S(1)}, bf16[48,16,128]{2,1,0:T(8,128)(2,1)S(1)}, u32[]{:S(2)}, u32[]{:S(2)}) collective-permute-start(bf16[48,16,128]{2,1,0:T(8,128)(2,1)S(1)} %add_convert_fusion.4), channel_id=1, source_target_pairs={{32,0},{64,32},{96,64},{128,96},{160,128},{192,160},{224,192},{0,2... | collective-permute-start | bytes 589832 | tf_op jit(solution)/shard_map/ppermute | solution.py:228
  90.3 1.8 %collective-permute-done.22 = bf16[48,16,128]{2,1,0:T(8,128)(2,1)S(1)} collective-permute-done((bf16[48,16,128]{2,1,0:T(8,128)(2,1)S(1)}, bf16[48,16,128]{2,1,0:T(8,128)(2,1)S(1)}, u32[]{:S(2)}, u32[]{:S(2)}) %collective-permute-start.22) | collective-permute-done | bytes 196640 | tf_op jit(solution)/shard_map/ppermute | solution.py:228
  92.2 2.3 %collective-permute-start.23 = (bf16[48,16,128]{2,1,0:T(8,128)(2,1)S(1)}, bf16[48,16,128]{2,1,0:T(8,128)(2,1)S(1)}, u32[]{:S(2)}, u32[]{:S(2)}) collective-permute-start(bf16[48,16,128]{2,1,0:T(8,128)(2,1)S(1)} %add_convert_fusion), channel_id=1, source_target_pairs={{32,0},{64,32},{96,64},{128,96},{160,128},{192,160},{224,192},{0,2... | collective-permute-start | bytes 589832 | tf_op jit(solution)/shard_map/ppermute | solution.py:228
  94.7 0.5 collective-permute-start.3
  95.2 2.7 %collective-permute-done.23 = bf16[48,16,128]{2,1,0:T(8,128)(2,1)S(1)} collective-permute-done((bf16[48,16,128]{2,1,0:T(8,128)(2,1)S(1)}, bf16[48,16,128]{2,1,0:T(8,128)(2,1)S(1)}, u32[]{:S(2)}, u32[]{:S(2)}) %collective-permute-start.23) | collective-permute-done | bytes 196640 | tf_op jit(solution)/shard_map/ppermute | solution.py:228
  97.9 3.6 %collective-permute-done.19 = bf16[48,16,128]{2,1,0:T(8,128)(2,1)S(1)} collective-permute-done((bf16[48,16,128]{2,1,0:T(8,128)(2,1)S(1)}, bf16[48,16,128]{2,1,0:T(8,128)(2,1)S(1)}, u32[]{:S(2)}, u32[]{:S(2)}) %collective-permute-start.19) | collective-permute-done | bytes 196640 | tf_op jit(solution)/shard_map/ppermute | solution.py:228
  101.8 1.8 %collective-permute-done.3 = bf16[48,16,128]{2,1,0:T(8,128)(2,1)S(1)} collective-permute-done((bf16[48,16,128]{2,1,0:T(8,128)(2,1)S(1)}, bf16[48,16,128]{2,1,0:T(8,128)(2,1)S(1)}, u32[]{:S(2)}, u32[]{:S(2)}) %collective-permute-start.3) | collective-permute-done | bytes 196640 | tf_op jit(solution)/shard_map/ppermute | solution.py:228
  104.1 4.9 %collective-permute-start.14 = (bf16[96,128]{1,0:T(8,128)(2,1)S(1)}, bf16[96,128]{1,0:T(8,128)(2,1)S(1)}, u32[]{:S(2)}, u32[]{:S(2)}) collective-permute-start(bf16[96,128]{1,0:T(8,128)(2,1)S(1)} %get-tuple-element.111), channel_id=1, source_target_pairs={{1,2},{2,1},{5,6},{6,5},{9,10},{10,9},{13,14},{14,13},{17,18},{18,... | collective-permute-start | bytes 73736 | tf_op jit(solution)/shard_map/ppermute | solution.py:25
  109.1 1.9 %collective-permute-start.24 = (bf16[96,128]{1,0:T(8,128)(2,1)S(1)}, bf16[96,128]{1,0:T(8,128)(2,1)S(1)}, u32[]{:S(2)}, u32[]{:S(2)}) collective-permute-start(bf16[96,128]{1,0:T(8,128)(2,1)S(1)} %get-tuple-element.107), channel_id=1, source_target_pairs={{1,2},{2,1},{5,6},{6,5},{9,10},{10,9},{13,14},{14,13},{17,18},{18,... | collective-permute-start | bytes 73736 | tf_op jit(solution)/shard_map/ppermute | solution.py:25
  111.2 0.2 convolution_convert_fusion.3
  111.5 1.1 fusion.67
  112.6 1.7 %collective-permute-done.24 = bf16[96,128]{1,0:T(8,128)(2,1)S(1)} collective-permute-done((bf16[96,128]{1,0:T(8,128)(2,1)S(1)}, bf16[96,128]{1,0:T(8,128)(2,1)S(1)}, u32[]{:S(2)}, u32[]{:S(2)}) %collective-permute-start.24) | collective-permute-done | bytes 24608 | tf_op jit(solution)/shard_map/ppermute | solution.py:25
  114.4 0.2 convolution_convert_fusion.2
  114.7 1.1 fusion.66
  115.9 0.7 collective-permute-start.27
  116.7 5.6 %collective-permute-done.26 = f16[16,48,128]{2,1,0:T(8,128)(2,1)S(1)} collective-permute-done((f16[16,48,128]{2,1,0:T(8,128)(2,1)S(1)}, f16[16,48,128]{2,1,0:T(8,128)(2,1)S(1)}, u32[]{:S(2)}, u32[]{:S(2)}) %collective-permute-start.26) | collective-permute-done | bytes 196640 | tf_op jit(solution)/shard_map/ppermute | solution.py:25
  122.4 6.0 %collective-permute-start.28 = (f16[16,16,128]{2,1,0:T(8,128)(2,1)S(1)}, f16[16,16,128]{2,1,0:T(8,128)(2,1)S(1)}, u32[]{:S(2)}, u32[]{:S(2)}) collective-permute-start(f16[16,16,128]{2,1,0:T(8,128)(2,1)S(1)} %get-tuple-element.96), channel_id=1, source_target_pairs={{0,4},{4,0},{8,12},{12,8},{16,20},{20,16},{24,28},{28,24},{1,5},{5... | collective-permute-start | bytes 196616 | tf_op jit(solution)/shard_map/ppermute | solution.py:25
  128.4 2.4 %collective-permute-start.29 = (f16[16,16,128]{2,1,0:T(8,128)(2,1)S(1)}, f16[16,16,128]{2,1,0:T(8,128)(2,1)S(1)}, u32[]{:S(2)}, u32[]{:S(2)}) collective-permute-start(f16[16,16,128]{2,1,0:T(8,128)(2,1)S(1)} %get-tuple-element.97), channel_id=1, source_target_pairs={{4,8},{8,4},{12,16},{16,12},{20,24},{24,20},{5,9},{9,5},{13,17},{1... | collective-permute-start | bytes 196616 | tf_op jit(solution)/shard_map/ppermute | solution.py:25
  130.8 6.1 %collective-permute-done.29 = f16[16,16,128]{2,1,0:T(8,128)(2,1)S(1)} collective-permute-done((f16[16,16,128]{2,1,0:T(8,128)(2,1)S(1)}, f16[16,16,128]{2,1,0:T(8,128)(2,1)S(1)}, u32[]{:S(2)}, u32[]{:S(2)}) %collective-permute-start.29) | collective-permute-done | bytes 65568 | tf_op jit(solution)/shard_map/ppermute | solution.py:25
  137.0 0.7 fusion.22
  (125 shorter events, 4.8 us)
Async XLA Ops:
  0.0 4.7 %copy-start.3 = (bf16[6,48,2,8,128]{4,3,2,1,0:T(8,128)(2,1)S(1)}, bf16[6,48,2,8,128]{4,3,2,1,0:T(8,128)(2,1)}, u32[]{:S(2)}) copy-start(bf16[6,48,2,8,128]{4,3,2,1,0:T(8,128)(2,1)} %param.6) | copy-start | bytes 3538948
  5.9 1.3 copy-start
  7.2 7.4 %copy-start.7 = (f32[6,3,31]{2,1,0:T(4,128)S(1)}, f32[6,3,31]{2,1,0:T(4,128)}, u32[]{:S(2)}) copy-start(f32[6,3,31]{2,1,0:T(4,128)} %param.8) | copy-start | bytes 6700
  7.2 31.2 %all-to-all-start.1 = ((bf16[8,56,16,128]{3,2,1,0:T(8,128)(2,1)}), bf16[8,56,16,128]{3,2,1,0:T(8,128)(2,1)S(1)}, u32[]{:S(2)}, u32[]{:S(2)}) async-start(bf16[8,56,16,128]{3,2,1,0:T(8,128)(2,1)} %copy-done), calls=%async_computation.1 | async-start | bytes 3670016 | tf_op jit(solution)/shard_map/all_to_all | solution.py:217
  19.0 2.7 %copy-start.4 = (f32[16,16,128]{2,1,0:T(8,128)S(1)}, f32[16,16,128]{2,1,0:T(8,128)}, u32[]{:S(2)}) copy-start(f32[16,16,128]{2,1,0:T(8,128)} %param.9) | copy-start | bytes 393220
  21.7 4.4 %collective-permute-start.9 = (bf16[16,16,128]{2,1,0:T(8,128)(2,1)S(1)}, bf16[16,16,128]{2,1,0:T(8,128)(2,1)S(1)}, u32[]{:S(2)}, u32[]{:S(2)}) collective-permute-start(bf16[16,16,128]{2,1,0:T(8,128)(2,1)S(1)} %convert_element_type.249), channel_id=1, source_target_pairs={{0,32},{32,0},{64,96},{96,64},{128,160},{160,128},{192,224},{224,1... | collective-permute-start | bytes 196616 | tf_op jit(solution)/shard_map/ppermute | solution.py:25
  23.8 2.4 %collective-permute-start.8 = (bf16[16,16,128]{2,1,0:T(8,128)(2,1)S(1)}, bf16[16,16,128]{2,1,0:T(8,128)(2,1)S(1)}, u32[]{:S(2)}, u32[]{:S(2)}) collective-permute-start(bf16[16,16,128]{2,1,0:T(8,128)(2,1)S(1)} %convert_element_type.249), channel_id=1, source_target_pairs={{32,64},{64,32},{96,128},{128,96},{160,192},{192,160},{33,65},{65,... | collective-permute-start | bytes 196616 | tf_op jit(solution)/shard_map/ppermute | solution.py:25
  41.1 29.2 %collective-permute-start.11 = (bf16[48,16,128]{2,1,0:T(8,128)(2,1)S(1)}, bf16[48,16,128]{2,1,0:T(8,128)(2,1)S(1)}, u32[]{:S(2)}, u32[]{:S(2)}) collective-permute-start(bf16[48,16,128]{2,1,0:T(8,128)(2,1)S(1)} %pad_maximum_fusion.3), channel_id=1, source_target_pairs={{0,4},{4,0},{8,12},{12,8},{16,20},{20,16},{24,28},{28,24},{1,5},{5... | collective-permute-start | bytes 589832 | tf_op jit(solution)/shard_map/ppermute | solution.py:25
  42.8 27.5 %collective-permute-start.10 = (bf16[48,16,128]{2,1,0:T(8,128)(2,1)S(1)}, bf16[48,16,128]{2,1,0:T(8,128)(2,1)S(1)}, u32[]{:S(2)}, u32[]{:S(2)}) collective-permute-start(bf16[48,16,128]{2,1,0:T(8,128)(2,1)S(1)} %pad_maximum_fusion.3), channel_id=1, source_target_pairs={{4,8},{8,4},{12,16},{16,12},{20,24},{24,20},{5,9},{9,5},{13,17},{1... | collective-permute-start | bytes 589832 | tf_op jit(solution)/shard_map/ppermute | solution.py:25
  45.5 10.0 %copy-start.6 = (s32[256,128]{1,0:T(8,128)S(1)}, s32[256,128]{1,0:T(8,128)}, u32[]{:S(2)}) copy-start(s32[256,128]{1,0:T(8,128)} %get-tuple-element.114) | copy-start | bytes 393220
  45.5 21.2 %collective-permute-start.20 = (bf16[24,16,128]{2,1,0:T(8,128)(2,1)S(1)}, bf16[24,16,128]{2,1,0:T(8,128)(2,1)S(1)}, u32[]{:S(2)}, u32[]{:S(2)}) collective-permute-start(bf16[24,16,128]{2,1,0:T(8,128)(2,1)S(1)} %get-tuple-element.77), channel_id=1, source_target_pairs={{32,0},{64,32},{96,64},{128,96},{160,128},{192,160},{224,192},{0,2... | collective-permute-start | bytes 294920 | tf_op jit(solution)/shard_map/ppermute | solution.py:228
  54.1 3.0 %copy-start.5 = (s32[256,128]{1,0:T(8,128)S(1)}, s32[256,128]{1,0:T(8,128)}, u32[]{:S(2)}) copy-start(s32[256,128]{1,0:T(8,128)} %get-tuple-element.115) | copy-start | bytes 393220
  54.2 5.6 %collective-permute-start.4 = (bf16[24,16,128]{2,1,0:T(8,128)(2,1)S(1)}, bf16[24,16,128]{2,1,0:T(8,128)(2,1)S(1)}, u32[]{:S(2)}, u32[]{:S(2)}) collective-permute-start(bf16[24,16,128]{2,1,0:T(8,128)(2,1)S(1)} %get-tuple-element.61), channel_id=1, source_target_pairs={{32,0},{64,32},{96,64},{128,96},{160,128},{192,160},{224,192},{0,2... | collective-permute-start | bytes 294920 | tf_op jit(solution)/shard_map/ppermute | solution.py:228
  58.8 9.2 %collective-permute-start.16 = (bf16[24,16,128]{2,1,0:T(8,128)(2,1)S(1)}, bf16[24,16,128]{2,1,0:T(8,128)(2,1)S(1)}, u32[]{:S(2)}, u32[]{:S(2)}) collective-permute-start(bf16[24,16,128]{2,1,0:T(8,128)(2,1)S(1)} %get-tuple-element.73), channel_id=1, source_target_pairs={{0,32},{32,64},{64,96},{96,128},{128,160},{160,192},{192,224},{224... | collective-permute-start | bytes 294920 | tf_op jit(solution)/shard_map/ppermute | solution.py:228
  59.8 6.0 %collective-permute-start = (bf16[24,16,128]{2,1,0:T(8,128)(2,1)S(1)}, bf16[24,16,128]{2,1,0:T(8,128)(2,1)S(1)}, u32[]{:S(2)}, u32[]{:S(2)}) collective-permute-start(bf16[24,16,128]{2,1,0:T(8,128)(2,1)S(1)} %get-tuple-element.57), channel_id=1, source_target_pairs={{0,32},{32,64},{64,96},{96,128},{128,160},{160,192},{192,224},{224... | collective-permute-start | bytes 294920 | tf_op jit(solution)/shard_map/ppermute | solution.py:228
  65.7 15.0 %collective-permute-start.5 = (bf16[48,16,128]{2,1,0:T(8,128)(2,1)S(1)}, bf16[48,16,128]{2,1,0:T(8,128)(2,1)S(1)}, u32[]{:S(2)}, u32[]{:S(2)}) collective-permute-start(bf16[48,16,128]{2,1,0:T(8,128)(2,1)S(1)} %pad_maximum_fusion.2), channel_id=1, source_target_pairs={{32,0},{64,32},{96,64},{128,96},{160,128},{192,160},{224,192},{0,2... | collective-permute-start | bytes 589832 | tf_op jit(solution)/shard_map/ppermute | solution.py:228
  66.8 14.6 %collective-permute-start.1 = (bf16[48,16,128]{2,1,0:T(8,128)(2,1)S(1)}, bf16[48,16,128]{2,1,0:T(8,128)(2,1)S(1)}, u32[]{:S(2)}, u32[]{:S(2)}) collective-permute-start(bf16[48,16,128]{2,1,0:T(8,128)(2,1)S(1)} %pad_maximum_fusion.1), channel_id=1, source_target_pairs={{0,32},{32,64},{64,96},{96,128},{128,160},{160,192},{192,224},{224... | collective-permute-start | bytes 589832 | tf_op jit(solution)/shard_map/ppermute | solution.py:228
  68.0 15.3 %collective-permute-start.21 = (bf16[48,16,128]{2,1,0:T(8,128)(2,1)S(1)}, bf16[48,16,128]{2,1,0:T(8,128)(2,1)S(1)}, u32[]{:S(2)}, u32[]{:S(2)}) collective-permute-start(bf16[48,16,128]{2,1,0:T(8,128)(2,1)S(1)} %pad_maximum_fusion.5), channel_id=1, source_target_pairs={{32,0},{64,32},{96,64},{128,96},{160,128},{192,160},{224,192},{0,2... | collective-permute-start | bytes 589832 | tf_op jit(solution)/shard_map/ppermute | solution.py:228
  70.3 6.8 %copy-start.1 = (bf16[48,48,768]{2,1,0:T(8,128)(2,1)S(1)}, bf16[48,48,768]{2,1,0:T(8,128)(2,1)}, u32[]{:S(2)}) copy-start(bf16[48,48,768]{2,1,0:T(8,128)(2,1)} %multiply_convert_fusion) | copy-start | bytes 10616836
  70.8 2.9 %collective-permute-start.13 = (bf16[288,128]{1,0:T(8,128)(2,1)S(1)}, bf16[288,128]{1,0:T(8,128)(2,1)S(1)}, u32[]{:S(2)}, u32[]{:S(2)}) collective-permute-start(bf16[288,128]{1,0:T(8,128)(2,1)S(1)} %get-tuple-element.100), channel_id=1, source_target_pairs={{0,1},{1,0},{2,3},{3,2},{4,5},{5,4},{6,7},{7,6},{8,9},{9,8},{10,11... | collective-permute-start | bytes 221192 | tf_op jit(solution)/shard_map/ppermute | solution.py:25
  70.9 5.8 %collective-permute-start.12 = (bf16[288,128]{1,0:T(8,128)(2,1)S(1)}, bf16[288,128]{1,0:T(8,128)(2,1)S(1)}, u32[]{:S(2)}, u32[]{:S(2)}) collective-permute-start(bf16[288,128]{1,0:T(8,128)(2,1)S(1)} %get-tuple-element.101), channel_id=1, source_target_pairs={{1,2},{2,1},{5,6},{6,5},{9,10},{10,9},{13,14},{14,13},{17,18},{18,... | collective-permute-start | bytes 221192 | tf_op jit(solution)/shard_map/ppermute | solution.py:25
  73.7 11.3 %collective-permute-start.17 = (bf16[48,16,128]{2,1,0:T(8,128)(2,1)S(1)}, bf16[48,16,128]{2,1,0:T(8,128)(2,1)S(1)}, u32[]{:S(2)}, u32[]{:S(2)}) collective-permute-start(bf16[48,16,128]{2,1,0:T(8,128)(2,1)S(1)} %pad_maximum_fusion.4), channel_id=1, source_target_pairs={{0,32},{32,64},{64,96},{96,128},{128,160},{160,192},{192,224},{224... | collective-permute-start | bytes 589832 | tf_op jit(solution)/shard_map/ppermute | solution.py:228
  77.1 2.0 %copy-start.2 = (bf16[48,48,768]{2,1,0:T(8,128)(2,1)S(1)}, bf16[48,48,768]{2,1,0:T(8,128)(2,1)}, u32[]{:S(2)}) copy-start(bf16[48,48,768]{2,1,0:T(8,128)(2,1)} %multiply_convert_fusion.1) | copy-start | bytes 10616836
  80.8 7.6 %collective-permute-start.6 = (bf16[48,16,128]{2,1,0:T(8,128)(2,1)S(1)}, bf16[48,16,128]{2,1,0:T(8,128)(2,1)S(1)}, u32[]{:S(2)}, u32[]{:S(2)}) collective-permute-start(bf16[48,16,128]{2,1,0:T(8,128)(2,1)S(1)} %add_convert_fusion.5), channel_id=1, source_target_pairs={{32,0},{64,32},{96,64},{128,96},{160,128},{192,160},{224,192},{0,2... | collective-permute-start | bytes 589832 | tf_op jit(solution)/shard_map/ppermute | solution.py:228
  81.5 13.2 %collective-permute-start.2 = (bf16[48,16,128]{2,1,0:T(8,128)(2,1)S(1)}, bf16[48,16,128]{2,1,0:T(8,128)(2,1)S(1)}, u32[]{:S(2)}, u32[]{:S(2)}) collective-permute-start(bf16[48,16,128]{2,1,0:T(8,128)(2,1)S(1)} %add_convert_fusion.7), channel_id=1, source_target_pairs={{0,32},{32,64},{64,96},{96,128},{128,160},{160,192},{192,224},{224... | collective-permute-start | bytes 589832 | tf_op jit(solution)/shard_map/ppermute | solution.py:228
  83.3 8.8 %collective-permute-start.22 = (bf16[48,16,128]{2,1,0:T(8,128)(2,1)S(1)}, bf16[48,16,128]{2,1,0:T(8,128)(2,1)S(1)}, u32[]{:S(2)}, u32[]{:S(2)}) collective-permute-start(bf16[48,16,128]{2,1,0:T(8,128)(2,1)S(1)} %add_convert_fusion.1), channel_id=1, source_target_pairs={{32,0},{64,32},{96,64},{128,96},{160,128},{192,160},{224,192},{0,2... | collective-permute-start | bytes 589832 | tf_op jit(solution)/shard_map/ppermute | solution.py:228
  85.0 9.5 %collective-permute-start.18 = (bf16[48,16,128]{2,1,0:T(8,128)(2,1)S(1)}, bf16[48,16,128]{2,1,0:T(8,128)(2,1)S(1)}, u32[]{:S(2)}, u32[]{:S(2)}) collective-permute-start(bf16[48,16,128]{2,1,0:T(8,128)(2,1)S(1)} %add_convert_fusion.3), channel_id=1, source_target_pairs={{0,32},{32,64},{64,96},{96,128},{128,160},{160,192},{192,224},{224... | collective-permute-start | bytes 589832 | tf_op jit(solution)/shard_map/ppermute | solution.py:228
  88.4 13.4 %collective-permute-start.7 = (bf16[48,16,128]{2,1,0:T(8,128)(2,1)S(1)}, bf16[48,16,128]{2,1,0:T(8,128)(2,1)S(1)}, u32[]{:S(2)}, u32[]{:S(2)}) collective-permute-start(bf16[48,16,128]{2,1,0:T(8,128)(2,1)S(1)} %add_convert_fusion.4), channel_id=1, source_target_pairs={{32,0},{64,32},{96,64},{128,96},{160,128},{192,160},{224,192},{0,2... | collective-permute-start | bytes 589832 | tf_op jit(solution)/shard_map/ppermute | solution.py:228
  92.2 5.7 %collective-permute-start.23 = (bf16[48,16,128]{2,1,0:T(8,128)(2,1)S(1)}, bf16[48,16,128]{2,1,0:T(8,128)(2,1)S(1)}, u32[]{:S(2)}, u32[]{:S(2)}) collective-permute-start(bf16[48,16,128]{2,1,0:T(8,128)(2,1)S(1)} %add_convert_fusion), channel_id=1, source_target_pairs={{32,0},{64,32},{96,64},{128,96},{160,128},{192,160},{224,192},{0,2... | collective-permute-start | bytes 589832 | tf_op jit(solution)/shard_map/ppermute | solution.py:228
  94.6 7.0 %collective-permute-start.19 = (bf16[48,16,128]{2,1,0:T(8,128)(2,1)S(1)}, bf16[48,16,128]{2,1,0:T(8,128)(2,1)S(1)}, u32[]{:S(2)}, u32[]{:S(2)}) collective-permute-start(bf16[48,16,128]{2,1,0:T(8,128)(2,1)S(1)} %add_convert_fusion.2), channel_id=1, source_target_pairs={{0,32},{32,64},{64,96},{96,128},{128,160},{160,192},{192,224},{224... | collective-permute-start | bytes 589832 | tf_op jit(solution)/shard_map/ppermute | solution.py:228
  94.7 8.9 %collective-permute-start.3 = (bf16[48,16,128]{2,1,0:T(8,128)(2,1)S(1)}, bf16[48,16,128]{2,1,0:T(8,128)(2,1)S(1)}, u32[]{:S(2)}, u32[]{:S(2)}) collective-permute-start(bf16[48,16,128]{2,1,0:T(8,128)(2,1)S(1)} %add_convert_fusion.6), channel_id=1, source_target_pairs={{0,32},{32,64},{64,96},{96,128},{128,160},{160,192},{192,224},{224... | collective-permute-start | bytes 589832 | tf_op jit(solution)/shard_map/ppermute | solution.py:228
  104.0 7.1 %collective-permute-start.15 = (bf16[96,128]{1,0:T(8,128)(2,1)S(1)}, bf16[96,128]{1,0:T(8,128)(2,1)S(1)}, u32[]{:S(2)}, u32[]{:S(2)}) collective-permute-start(bf16[96,128]{1,0:T(8,128)(2,1)S(1)} %get-tuple-element.110), channel_id=1, source_target_pairs={{0,1},{1,0},{2,3},{3,2},{4,5},{5,4},{6,7},{7,6},{8,9},{9,8},{10,11... | collective-permute-start | bytes 73736 | tf_op jit(solution)/shard_map/ppermute | solution.py:25
  104.1 7.0 %collective-permute-start.14 = (bf16[96,128]{1,0:T(8,128)(2,1)S(1)}, bf16[96,128]{1,0:T(8,128)(2,1)S(1)}, u32[]{:S(2)}, u32[]{:S(2)}) collective-permute-start(bf16[96,128]{1,0:T(8,128)(2,1)S(1)} %get-tuple-element.111), channel_id=1, source_target_pairs={{1,2},{2,1},{5,6},{6,5},{9,10},{10,9},{13,14},{14,13},{17,18},{18,... | collective-permute-start | bytes 73736 | tf_op jit(solution)/shard_map/ppermute | solution.py:25
  109.0 3.6 %collective-permute-start.25 = (bf16[96,128]{1,0:T(8,128)(2,1)S(1)}, bf16[96,128]{1,0:T(8,128)(2,1)S(1)}, u32[]{:S(2)}, u32[]{:S(2)}) collective-permute-start(bf16[96,128]{1,0:T(8,128)(2,1)S(1)} %get-tuple-element.106), channel_id=1, source_target_pairs={{0,1},{1,0},{2,3},{3,2},{4,5},{5,4},{6,7},{7,6},{8,9},{9,8},{10,11... | collective-permute-start | bytes 73736 | tf_op jit(solution)/shard_map/ppermute | solution.py:25
  109.1 5.1 %collective-permute-start.24 = (bf16[96,128]{1,0:T(8,128)(2,1)S(1)}, bf16[96,128]{1,0:T(8,128)(2,1)S(1)}, u32[]{:S(2)}, u32[]{:S(2)}) collective-permute-start(bf16[96,128]{1,0:T(8,128)(2,1)S(1)} %get-tuple-element.107), channel_id=1, source_target_pairs={{1,2},{2,1},{5,6},{6,5},{9,10},{10,9},{13,14},{14,13},{17,18},{18,... | collective-permute-start | bytes 73736 | tf_op jit(solution)/shard_map/ppermute | solution.py:25
  115.9 0.8 collective-permute-start.27
  116.5 5.8 %collective-permute-start.26 = (f16[16,48,128]{2,1,0:T(8,128)(2,1)S(1)}, f16[16,48,128]{2,1,0:T(8,128)(2,1)S(1)}, u32[]{:S(2)}, u32[]{:S(2)}) collective-permute-start(f16[16,48,128]{2,1,0:T(8,128)(2,1)S(1)} %bitcast.116), channel_id=1, source_target_pairs={{0,32},{32,0},{64,96},{96,64},{128,160},{160,128},{192,224},{224,1... | collective-permute-start | bytes 589832 | tf_op jit(solution)/shard_map/ppermute | solution.py:25
  122.4 8.4 %collective-permute-start.28 = (f16[16,16,128]{2,1,0:T(8,128)(2,1)S(1)}, f16[16,16,128]{2,1,0:T(8,128)(2,1)S(1)}, u32[]{:S(2)}, u32[]{:S(2)}) collective-permute-start(f16[16,16,128]{2,1,0:T(8,128)(2,1)S(1)} %get-tuple-element.96), channel_id=1, source_target_pairs={{0,4},{4,0},{8,12},{12,8},{16,20},{20,16},{24,28},{28,24},{1,5},{5... | collective-permute-start | bytes 196616 | tf_op jit(solution)/shard_map/ppermute | solution.py:25
  128.4 8.6 %collective-permute-start.29 = (f16[16,16,128]{2,1,0:T(8,128)(2,1)S(1)}, f16[16,16,128]{2,1,0:T(8,128)(2,1)S(1)}, u32[]{:S(2)}, u32[]{:S(2)}) collective-permute-start(f16[16,16,128]{2,1,0:T(8,128)(2,1)S(1)} %get-tuple-element.97), channel_id=1, source_target_pairs={{4,8},{8,4},{12,16},{16,12},{20,24},{24,20},{5,9},{9,5},{13,17},{1... | collective-permute-start | bytes 196616 | tf_op jit(solution)/shard_map/ppermute | solution.py:25

commit v4 on v1

--- a/solution.py
+++ b/solution.py
@@ -267,6 +267,7 @@
     lanes = gz_count * capacity * view_count
     usual = min(usual_slots, lanes)
     own = estimate.astype(jnp.bfloat16)
+    own = with_columns(own.reshape(area, cols), side).reshape(depth, rows, -1)
     own_rows = neighbours(own, own, "gy")
     table, ends = slot_tables(tile_place, positions, chunks, usual)
     usual_table = table(0, usual)
@@ -305,7 +306,7 @@
     own = jnp.concatenate([above, own, below], axis=1)
     above, below = order_sides(*neighbours(own, own, "gz"), "gz")
     own = jnp.concatenate([above, own, below], axis=0)
-    own = own.reshape(tall * wide, cols)
+    field = own.reshape(tall * wide, -1)
     column = jnp.concatenate(
         [jnp.arange(cols), jnp.arange(-side, 0), jnp.arange(cols, cols + side)]
         + [jnp.full(cols - 2 * side, -cols)]
@@ -313,7 +314,6 @@
     offset = column[:, None] - jnp.arange(cols)[None, :]
     col_taps = taps_table(kernels[:, 2], radius + offset).astype(jnp.bfloat16)
     col_taps_back = taps_table(kernels[:, 2], radius - offset).astype(jnp.bfloat16)
-    field = with_columns(own, side)
     blurred = []
     for c in range(chunks):
         swept = lax.dot_general(

time: 128 us -> 143 us (1.12)
  the two profiles are of different devices: /device:TPU:106 before, /device:TPU:48 now
where the time goes in v4:
time: 143 us; the launch traced here: 142 us
  starting transfers between devices  63.6 us (44%)
  waiting for transfers between devices  33.3 us (23%)
  other arithmetic  14.9 us (10%)
  matrix products  12.6 us (9%)
  local copies, waits for them, and re-layouts  8.5 us (6%)
  Pallas kernels  7.73 us (5%)
  between operations  1.49 us (1%)
    ppermute x16, starting transfers between devices, ring_step(): return (lax.ppermute(upward, 'gz', up), lax.ppermute(downward, 'gz', down))  21.9 us
    ppermute x7, starting transfers between devices, neighbours(): lax.ppermute(second, axis, pairs[1])  19.5 us
    ppermute x7, starting transfers between devices, neighbours(): lax.ppermute(first, axis, pairs[0])  14.9 us
    ppermute x7, waiting for transfers between devices, neighbours(): lax.ppermute(second, axis, pairs[1])  14.7 us
    ppermute x16, waiting for transfers between devices, ring_step(): return (lax.ppermute(upward, 'gz', up), lax.ppermute(downward, 'gz', down))  10.5 us
    all_to_all x1, starting transfers between devices, exchange(): return lax.all_to_all(value, 'gy', split_axis=0, concat_axis=0, tiled=True)  7.26 us
    all_to_all x1, waiting for transfers between devices, exchange(): return lax.all_to_all(value, 'gy', split_axis=0, concat_axis=0, tiled=True)  6.84 us
    convert_element_type x2, other arithmetic, on_device(): sheet = (down * across).astype(jnp.bfloat16)  6.38 us
  transfers between devices with their start and end apart: 31, of which 17 were waited for; matrix products, arithmetic and copies ran while one was open for 20% of the time, Pallas kernels for 3%

profile of v4, /device:TPU:48, one launch (start us, length us, event | category | flops | bytes accessed | tf_op | source)
XLA Modules:
  0.0 142.2 jit_solution(17723227348145557599)
XLA Ops:
  0.0 0.9 convert_element_type.222
  1.0 0.7 collective-permute-start
  1.7 2.7 %collective-permute-start.1 = (bf16[32,128]{1,0:T(8,128)(2,1)S(1)}, bf16[32,128]{1,0:T(8,128)(2,1)S(1)}, u32[]{:S(2)}, u32[]{:S(2)}) collective-permute-start(bf16[32,128]{1,0:T(8,128)(2,1)S(1)} %get-tuple-element.114), channel_id=1, source_target_pairs={{0,1},{1,0},{2,3},{3,2},{4,5},{5,4},{6,7},{7,6},{8,9},{9,8},{10,11... | collective-permute-start | bytes 24584 | tf_op jit(solution)/shard_map/ppermute | solution.py:25
  4.4 1.0 reshape.561
  5.7 1.0 add_select_fusion
  8.0 0.6 reduce_max.9
  9.5 0.8 fusion.27
  10.4 1.8 %pack.3 = bf16[8,56,16,128]{3,2,1,0:T(8,128)(2,1)S(1)} custom-call(s32[8,56]{1,0:T(8,128)S(1)} %get-tuple-element.117.source, bf16[288,16,128]{2,1,0:T(8,128)(2,1)} %bitcast.104), custom_call_target="tpu_custom_call" | custom-call | tf_op jit(solution)/shard_map/pack/pallas_call | solution.py:181
  12.2 1.3 copy-done
  13.6 0.7 collective-permute-start.2
  14.3 5.7 %collective-permute-start.3 = (bf16[16,16,256]{2,1,0:T(8,128)(2,1)S(1)}, bf16[16,16,256]{2,1,0:T(8,128)(2,1)S(1)}, u32[]{:S(2)}, u32[]{:S(2)}) collective-permute-start(bf16[16,16,256]{2,1,0:T(8,128)(2,1)S(1)} %bitcast.97), channel_id=1, source_target_pairs={{4,8},{8,4},{12,16},{16,12},{20,24},{24,20},{5,9},{9,5},{13,17},{1... | collective-permute-start | bytes 393224 | tf_op jit(solution)/shard_map/ppermute | solution.py:25
  20.6 3.1 %collective-permute-done.3 = bf16[16,16,256]{2,1,0:T(8,128)(2,1)S(1)} collective-permute-done((bf16[16,16,256]{2,1,0:T(8,128)(2,1)S(1)}, bf16[16,16,256]{2,1,0:T(8,128)(2,1)S(1)}, u32[]{:S(2)}, u32[]{:S(2)}) %collective-permute-start.3) | collective-permute-done | bytes 131104 | tf_op jit(solution)/shard_map/ppermute | solution.py:25
  23.8 0.6 copy-done.11
  24.4 0.8 pad_maximum_fusion.1
  25.2 3.8 %collective-permute-start.4 = (bf16[16,48,256]{2,1,0:T(8,128)(2,1)}, bf16[16,48,256]{2,1,0:T(8,128)(2,1)}, u32[]{:S(2)}, u32[]{:S(2)}) collective-permute-start(bf16[16,48,256]{2,1,0:T(8,128)(2,1)} %pad_maximum_fusion.1), channel_id=1, source_target_pairs={{32,64},{64,32},{96,128},{128,96},{160,192},{192,160},{33,65},{65,... | collective-permute-start | bytes 1179656 | tf_op jit(solution)/shard_map/ppermute | solution.py:25
  29.4 0.6 fusion.4
  30.0 0.8 fusion.66
  31.4 0.8 fusion.67
  32.2 1.4 fusion.7
  33.6 0.9 fusion.65
  34.4 0.7 copy.32
  35.1 0.7 copy.33
  35.8 7.3 %all-to-all-start.1 = ((bf16[8,56,16,128]{3,2,1,0:T(8,128)(2,1)}), bf16[8,56,16,128]{3,2,1,0:T(8,128)(2,1)S(1)}, u32[]{:S(2)}, u32[]{:S(2)}) async-start(bf16[8,56,16,128]{3,2,1,0:T(8,128)(2,1)} %copy-done), calls=%async_computation.1 | async-start | bytes 3670016 | tf_op jit(solution)/shard_map/all_to_all | solution.py:216
  43.1 3.7 %multiply_convert_fusion.1 = bf16[48,48,768]{2,1,0:T(8,128)(2,1)} fusion(f32[48,768]{1,0:T(8,128)} %bitcast.116, f32[48,768]{1,0:T(8,128)} %bitcast.114), kind=kLoop, calls=%fused_computation.5 | loop fusion | flops 3538944 | bytes 3833856 | tf_op jit(solution)/shard_map/convert_element_type | solution.py:303
  46.8 2.9 %fusion.6 = bf16[6,256,128]{2,0,1:T(8,128)(2,1)} fusion(s32[256,128]{1,0:T(8,128)S(1)} %copy-done.16, f32[6,3,31]{2,0,1:T(8,128)} %copy-done.18), kind=kOutput, calls=%fused_computation.19 | convolution fusion | flops 74350592 | bytes 528384 | tf_op jit(solution)/shard_map/eim,vm->vei/dot_general | solution.py:88
  49.8 2.7 %multiply_convert_fusion = bf16[48,48,768]{2,1,0:T(8,128)(2,1)} fusion(f32[48,768]{1,0:T(8,128)S(1)} %bitcast.120, f32[48,768]{1,0:T(8,128)S(1)} %bitcast.118), kind=kLoop, calls=%fused_computation.4 | loop fusion | flops 3538944 | bytes 3833856 | tf_op jit(solution)/shard_map/convert_element_type | solution.py:303
  52.5 1.2 broadcast_select_fusion.1
  53.7 1.1 fusion.9
  54.8 1.0 fusion.20
  55.9 1.1 fusion.8
  57.0 1.0 fusion.22
  58.0 6.8 %all-to-all-done.1.arrived = bf16[8,56,16,128]{3,2,1,0:T(8,128)(2,1)S(1)} async-done(((bf16[8,56,16,128]{3,2,1,0:T(8,128)(2,1)}), bf16[8,56,16,128]{3,2,1,0:T(8,128)(2,1)S(1)}, u32[]{:S(2)}, u32[]{:S(2)}) %all-to-all-start.1) | async-done | bytes 1835040 | tf_op jit(solution)/shard_map/all_to_all | solution.py:216
  64.9 2.5 %join.3 = (bf16[48,16,128]{2,1,0:T(8,128)(2,1)S(1)}, bf16[48,16,128]{2,1,0:T(8,128)(2,1)S(1)}, bf16[48,16,128]{2,1,0:T(8,128)(2,1)S(1)}, bf16[48,16,128]{2,1,0:T...) custom-call(s32[3,8]{1,0:T(4,128)S(1)} %pad_add_fusion.1.ends, ...), custom_call_target="tpu_custom_call" | custom-call | tf_op jit(solution)/shard_map/join/pallas_call | solution.py:195
  67.4 4.9 %collective-permute-start.16 = (bf16[24,16,128]{2,1,0:T(8,128)(2,1)S(1)}, bf16[24,16,128]{2,1,0:T(8,128)(2,1)S(1)}, u32[]{:S(2)}, u32[]{:S(2)}) collective-permute-start(bf16[24,16,128]{2,1,0:T(8,128)(2,1)S(1)} %get-tuple-element.76), channel_id=1, source_target_pairs={{0,32},{32,64},{64,96},{96,128},{128,160},{160,192},{192,224},{224... | collective-permute-start | bytes 294920 | tf_op jit(solution)/shard_map/ppermute | solution.py:227
  72.5 2.6 %join.2 = (bf16[48,16,128]{2,1,0:T(8,128)(2,1)S(1)}, bf16[48,16,128]{2,1,0:T(8,128)(2,1)S(1)}, bf16[48,16,128]{2,1,0:T(8,128)(2,1)S(1)}, bf16[48,16,128]{2,1,0:T...) custom-call(s32[3,8]{1,0:T(4,128)S(1)} %pad_add_fusion.1.ends, ...), custom_call_target="tpu_custom_call" | custom-call | tf_op jit(solution)/shard_map/join/pallas_call | solution.py:195
  75.2 2.1 %collective-permute-start.6 = (bf16[24,16,128]{2,1,0:T(8,128)(2,1)S(1)}, bf16[24,16,128]{2,1,0:T(8,128)(2,1)S(1)}, u32[]{:S(2)}, u32[]{:S(2)}) collective-permute-start(bf16[24,16,128]{2,1,0:T(8,128)(2,1)S(1)} %get-tuple-element.64), channel_id=1, source_target_pairs={{0,32},{32,64},{64,96},{96,128},{128,160},{160,192},{192,224},{224... | collective-permute-start | bytes 294920 | tf_op jit(solution)/shard_map/ppermute | solution.py:227
  77.5 2.1 %collective-permute-start.17 = (bf16[48,16,128]{2,1,0:T(8,128)(2,1)S(1)}, bf16[48,16,128]{2,1,0:T(8,128)(2,1)S(1)}, u32[]{:S(2)}, u32[]{:S(2)}) collective-permute-start(bf16[48,16,128]{2,1,0:T(8,128)(2,1)S(1)} %pad_maximum_fusion.4), channel_id=1, source_target_pairs={{0,32},{32,64},{64,96},{96,128},{128,160},{160,192},{192,224},{224... | collective-permute-start | bytes 589832 | tf_op jit(solution)/shard_map/ppermute | solution.py:227
  79.6 1.2 collective-permute-done.20
  81.1 2.0 %collective-permute-start.7 = (bf16[48,16,128]{2,1,0:T(8,128)(2,1)S(1)}, bf16[48,16,128]{2,1,0:T(8,128)(2,1)S(1)}, u32[]{:S(2)}, u32[]{:S(2)}) collective-permute-start(bf16[48,16,128]{2,1,0:T(8,128)(2,1)S(1)} %pad_maximum_fusion.2), channel_id=1, source_target_pairs={{0,32},{32,64},{64,96},{96,128},{128,160},{160,192},{192,224},{224... | collective-permute-start | bytes 589832 | tf_op jit(solution)/shard_map/ppermute | solution.py:227
  83.6 1.3 collective-permute-done.17
  85.0 2.6 %collective-permute-start.18 = (bf16[48,16,128]{2,1,0:T(8,128)(2,1)S(1)}, bf16[48,16,128]{2,1,0:T(8,128)(2,1)S(1)}, u32[]{:S(2)}, u32[]{:S(2)}) collective-permute-start(bf16[48,16,128]{2,1,0:T(8,128)(2,1)S(1)} %add_convert_fusion.3), channel_id=1, source_target_pairs={{0,32},{32,64},{64,96},{96,128},{128,160},{160,192},{192,224},{224... | collective-permute-start | bytes 589832 | tf_op jit(solution)/shard_map/ppermute | solution.py:227
  87.5 1.1 collective-permute-done.21
  89.2 2.6 %collective-permute-start.8 = (bf16[48,16,128]{2,1,0:T(8,128)(2,1)S(1)}, bf16[48,16,128]{2,1,0:T(8,128)(2,1)S(1)}, u32[]{:S(2)}, u32[]{:S(2)}) collective-permute-start(bf16[48,16,128]{2,1,0:T(8,128)(2,1)S(1)} %add_convert_fusion.7), channel_id=1, source_target_pairs={{0,32},{32,64},{64,96},{96,128},{128,160},{160,192},{192,224},{224... | collective-permute-start | bytes 589832 | tf_op jit(solution)/shard_map/ppermute | solution.py:227
  91.8 1.1 collective-permute-done.11
  93.5 2.5 %collective-permute-start.19 = (bf16[48,16,128]{2,1,0:T(8,128)(2,1)S(1)}, bf16[48,16,128]{2,1,0:T(8,128)(2,1)S(1)}, u32[]{:S(2)}, u32[]{:S(2)}) collective-permute-start(bf16[48,16,128]{2,1,0:T(8,128)(2,1)S(1)} %add_convert_fusion.2), channel_id=1, source_target_pairs={{0,32},{32,64},{64,96},{96,128},{128,160},{160,192},{192,224},{224... | collective-permute-start | bytes 589832 | tf_op jit(solution)/shard_map/ppermute | solution.py:227
  96.0 1.1 collective-permute-done.22
  97.3 0.7 collective-permute-done.8
  98.1 2.1 %collective-permute-start.9 = (bf16[48,16,128]{2,1,0:T(8,128)(2,1)S(1)}, bf16[48,16,128]{2,1,0:T(8,128)(2,1)S(1)}, u32[]{:S(2)}, u32[]{:S(2)}) collective-permute-start(bf16[48,16,128]{2,1,0:T(8,128)(2,1)S(1)} %add_convert_fusion.6), channel_id=1, source_target_pairs={{0,32},{32,64},{64,96},{96,128},{128,160},{160,192},{192,224},{224... | collective-permute-start | bytes 589832 | tf_op jit(solution)/shard_map/ppermute | solution.py:227
  100.2 1.1 collective-permute-done.12
  101.5 2.0 %collective-permute-done.23 = bf16[48,16,128]{2,1,0:T(8,128)(2,1)S(1)} collective-permute-done((bf16[48,16,128]{2,1,0:T(8,128)(2,1)S(1)}, bf16[48,16,128]{2,1,0:T(8,128)(2,1)S(1)}, u32[]{:S(2)}, u32[]{:S(2)}) %collective-permute-start.23) | collective-permute-done | bytes 196640 | tf_op jit(solution)/shard_map/ppermute | solution.py:227
  103.9 0.7 collective-permute-start.24
  104.5 3.7 %collective-permute-start.25 = (bf16[96,128]{1,0:T(8,128)(2,1)S(1)}, bf16[96,128]{1,0:T(8,128)(2,1)S(1)}, u32[]{:S(2)}, u32[]{:S(2)}) collective-permute-start(bf16[96,128]{1,0:T(8,128)(2,1)S(1)} %get-tuple-element.106), channel_id=1, source_target_pairs={{0,1},{1,0},{2,3},{3,2},{4,5},{5,4},{6,7},{7,6},{8,9},{9,8},{10,11... | collective-permute-start | bytes 73736 | tf_op jit(solution)/shard_map/ppermute | solution.py:25
  108.6 0.8 collective-permute-start.14
  109.4 2.2 %collective-permute-start.15 = (bf16[96,128]{1,0:T(8,128)(2,1)S(1)}, bf16[96,128]{1,0:T(8,128)(2,1)S(1)}, u32[]{:S(2)}, u32[]{:S(2)}) collective-permute-start(bf16[96,128]{1,0:T(8,128)(2,1)S(1)} %get-tuple-element.110), channel_id=1, source_target_pairs={{0,1},{1,0},{2,3},{3,2},{4,5},{5,4},{6,7},{7,6},{8,9},{9,8},{10,11... | collective-permute-start | bytes 73736 | tf_op jit(solution)/shard_map/ppermute | solution.py:25
  112.9 1.1 fusion.69
  114.0 0.9 copy-done.1
  114.9 1.1 fusion.68
  116.1 1.5 %collective-permute-start.26 = (f16[16,48,128]{2,1,0:T(8,128)(2,1)S(1)}, f16[16,48,128]{2,1,0:T(8,128)(2,1)S(1)}, u32[]{:S(2)}, u32[]{:S(2)}) collective-permute-start(f16[16,48,128]{2,1,0:T(8,128)(2,1)S(1)} %bitcast.127), channel_id=1, source_target_pairs={{0,32},{32,0},{64,96},{96,64},{128,160},{160,128},{192,224},{224,1... | collective-permute-start | bytes 589832 | tf_op jit(solution)/shard_map/ppermute | solution.py:25
  117.6 5.9 %collective-permute-start.27 = (f16[16,48,128]{2,1,0:T(8,128)(2,1)S(1)}, f16[16,48,128]{2,1,0:T(8,128)(2,1)S(1)}, u32[]{:S(2)}, u32[]{:S(2)}) collective-permute-start(f16[16,48,128]{2,1,0:T(8,128)(2,1)S(1)} %bitcast.126), channel_id=1, source_target_pairs={{32,64},{64,32},{96,128},{128,96},{160,192},{192,160},{33,65},{65,... | collective-permute-start | bytes 589832 | tf_op jit(solution)/shard_map/ppermute | solution.py:25
  123.5 5.3 %collective-permute-done.27 = f16[16,48,128]{2,1,0:T(8,128)(2,1)S(1)} collective-permute-done((f16[16,48,128]{2,1,0:T(8,128)(2,1)S(1)}, f16[16,48,128]{2,1,0:T(8,128)(2,1)S(1)}, u32[]{:S(2)}, u32[]{:S(2)}) %collective-permute-start.27) | collective-permute-done | bytes 196640 | tf_op jit(solution)/shard_map/ppermute | solution.py:25
  129.0 4.0 %collective-permute-start.28 = (f16[16,16,128]{2,1,0:T(8,128)(2,1)S(1)}, f16[16,16,128]{2,1,0:T(8,128)(2,1)S(1)}, u32[]{:S(2)}, u32[]{:S(2)}) collective-permute-start(f16[16,16,128]{2,1,0:T(8,128)(2,1)S(1)} %get-tuple-element.102), channel_id=1, source_target_pairs={{0,4},{4,0},{8,12},{12,8},{16,20},{20,16},{24,28},{28,24},{1,5},{5... | collective-permute-start | bytes 196616 | tf_op jit(solution)/shard_map/ppermute | solution.py:25
  133.0 1.9 %collective-permute-start.29 = (f16[16,16,128]{2,1,0:T(8,128)(2,1)S(1)}, f16[16,16,128]{2,1,0:T(8,128)(2,1)S(1)}, u32[]{:S(2)}, u32[]{:S(2)}) collective-permute-start(f16[16,16,128]{2,1,0:T(8,128)(2,1)S(1)} %get-tuple-element.103), channel_id=1, source_target_pairs={{4,8},{8,4},{12,16},{16,12},{20,24},{24,20},{5,9},{9,5},{13,17},{1... | collective-permute-start | bytes 196616 | tf_op jit(solution)/shard_map/ppermute | solution.py:25
  135.2 6.3 %collective-permute-done.29 = f16[16,16,128]{2,1,0:T(8,128)(2,1)S(1)} collective-permute-done((f16[16,16,128]{2,1,0:T(8,128)(2,1)S(1)}, f16[16,16,128]{2,1,0:T(8,128)(2,1)S(1)}, u32[]{:S(2)}, u32[]{:S(2)}) %collective-permute-start.29) | collective-permute-done | bytes 65568 | tf_op jit(solution)/shard_map/ppermute | solution.py:25
  141.5 0.7 fusion.26
  (145 shorter events, 8.7 us)
Async XLA Ops:
  1.0 12.5 %collective-permute-start = (bf16[32,128]{1,0:T(8,128)(2,1)S(1)}, bf16[32,128]{1,0:T(8,128)(2,1)S(1)}, u32[]{:S(2)}, u32[]{:S(2)}) collective-permute-start(bf16[32,128]{1,0:T(8,128)(2,1)S(1)} %get-tuple-element.115), channel_id=1, source_target_pairs={{1,2},{2,1},{5,6},{6,5},{9,10},{10,9},{13,14},{14,13},{17,18},{18,... | collective-permute-start | bytes 24584 | tf_op jit(solution)/shard_map/ppermute | solution.py:25
  1.7 11.8 %collective-permute-start.1 = (bf16[32,128]{1,0:T(8,128)(2,1)S(1)}, bf16[32,128]{1,0:T(8,128)(2,1)S(1)}, u32[]{:S(2)}, u32[]{:S(2)}) collective-permute-start(bf16[32,128]{1,0:T(8,128)(2,1)S(1)} %get-tuple-element.114), channel_id=1, source_target_pairs={{0,1},{1,0},{2,3},{3,2},{4,5},{5,4},{6,7},{7,6},{8,9},{9,8},{10,11... | collective-permute-start | bytes 24584 | tf_op jit(solution)/shard_map/ppermute | solution.py:25
  10.2 18.9 %copy-start.17 = (f32[6,3,31]{2,1,0:T(4,128)S(1)}, f32[6,3,31]{2,1,0:T(4,128)}, u32[]{:S(2)}) copy-start(f32[6,3,31]{2,1,0:T(4,128)} %param.8) | copy-start | bytes 6700
  12.2 1.3 copy-start
  13.6 7.0 %collective-permute-start.2 = (bf16[16,16,256]{2,1,0:T(8,128)(2,1)S(1)}, bf16[16,16,256]{2,1,0:T(8,128)(2,1)S(1)}, u32[]{:S(2)}, u32[]{:S(2)}) collective-permute-start(bf16[16,16,256]{2,1,0:T(8,128)(2,1)S(1)} %bitcast.96), channel_id=1, source_target_pairs={{0,4},{4,0},{8,12},{12,8},{16,20},{20,16},{24,28},{28,24},{1,5},{5... | collective-permute-start | bytes 393224 | tf_op jit(solution)/shard_map/ppermute | solution.py:25
  14.3 9.4 %collective-permute-start.3 = (bf16[16,16,256]{2,1,0:T(8,128)(2,1)S(1)}, bf16[16,16,256]{2,1,0:T(8,128)(2,1)S(1)}, u32[]{:S(2)}, u32[]{:S(2)}) collective-permute-start(bf16[16,16,256]{2,1,0:T(8,128)(2,1)S(1)} %bitcast.97), channel_id=1, source_target_pairs={{4,8},{8,4},{12,16},{16,12},{20,24},{24,20},{5,9},{9,5},{13,17},{1... | collective-permute-start | bytes 393224 | tf_op jit(solution)/shard_map/ppermute | solution.py:25
  23.8 0.6 copy-start.11
  23.8 1.4 %copy-start.13 = (bf16[16,16,256]{2,1,0:T(8,128)(2,1)}, bf16[16,16,256]{2,1,0:T(8,128)(2,1)S(1)}, u32[]{:S(2)}) copy-start(bf16[16,16,256]{2,1,0:T(8,128)(2,1)S(1)} %get-tuple-element.101) | copy-start | bytes 393220
  25.2 27.2 %collective-permute-start.4 = (bf16[16,48,256]{2,1,0:T(8,128)(2,1)}, bf16[16,48,256]{2,1,0:T(8,128)(2,1)}, u32[]{:S(2)}, u32[]{:S(2)}) collective-permute-start(bf16[16,48,256]{2,1,0:T(8,128)(2,1)} %pad_maximum_fusion.1), channel_id=1, source_target_pairs={{32,64},{64,32},{96,128},{128,96},{160,192},{192,160},{33,65},{65,... | collective-permute-start | bytes 1179656 | tf_op jit(solution)/shard_map/ppermute | solution.py:25
  29.1 23.4 %collective-permute-start.5 = (bf16[16,48,256]{2,1,0:T(8,128)(2,1)}, bf16[16,48,256]{2,1,0:T(8,128)(2,1)}, u32[]{:S(2)}, u32[]{:S(2)}) collective-permute-start(bf16[16,48,256]{2,1,0:T(8,128)(2,1)} %pad_maximum_fusion.1), channel_id=1, source_target_pairs={{0,32},{32,0},{64,96},{96,64},{128,160},{160,128},{192,224},{224,1... | collective-permute-start | bytes 1179656 | tf_op jit(solution)/shard_map/ppermute | solution.py:25
  29.4 2.7 %copy-start.18 = (f32[6,3,31]{2,0,1:T(8,128)}, f32[6,3,31]{2,0,1:T(8,128)S(1)}, u32[]{:S(2)}) copy-start(f32[6,3,31]{2,0,1:T(8,128)S(1)} %copy_divide_fusion) | copy-start | bytes 6700
  35.8 29.1 %all-to-all-start.1 = ((bf16[8,56,16,128]{3,2,1,0:T(8,128)(2,1)}), bf16[8,56,16,128]{3,2,1,0:T(8,128)(2,1)S(1)}, u32[]{:S(2)}, u32[]{:S(2)}) async-start(bf16[8,56,16,128]{3,2,1,0:T(8,128)(2,1)} %copy-done), calls=%async_computation.1 | async-start | bytes 3670016 | tf_op jit(solution)/shard_map/all_to_all | solution.py:216
  43.1 3.7 %copy-start.16 = (s32[256,128]{1,0:T(8,128)S(1)}, s32[256,128]{1,0:T(8,128)}, u32[]{:S(2)}) copy-start(s32[256,128]{1,0:T(8,128)} %get-tuple-element.118) | copy-start | bytes 393220
  43.1 6.6 %copy-start.6 = (f32[3,48,256]{2,0,1:T(4,128)S(1)}, f32[3,48,256]{2,0,1:T(4,128)}, u32[]{:S(2)}) copy-start(f32[3,48,256]{2,0,1:T(4,128)} %get-tuple-element.96) | copy-start | bytes 442372
  43.1 6.6 %copy-start.7 = (f32[3,48,256]{2,0,1:T(4,128)S(1)}, f32[3,48,256]{2,0,1:T(4,128)}, u32[]{:S(2)}) copy-start(f32[3,48,256]{2,0,1:T(4,128)} %get-tuple-element.98) | copy-start | bytes 442372
  49.8 3.9 %copy-start.12 = (bf16[16,16,256]{2,1,0:T(8,128)(2,1)S(1)}, bf16[16,16,256]{2,1,0:T(8,128)(2,1)}, u32[]{:S(2)}) copy-start(bf16[16,16,256]{2,1,0:T(8,128)(2,1)} %copy-done.11) | copy-start | bytes 393220
  49.8 3.9 %copy-start.14 = (bf16[16,16,256]{2,1,0:T(8,128)(2,1)S(1)}, bf16[16,16,256]{2,1,0:T(8,128)(2,1)}, u32[]{:S(2)}) copy-start(bf16[16,16,256]{2,1,0:T(8,128)(2,1)} %copy-done.13) | copy-start | bytes 393220
  53.6 1.2 copy-start.5
  53.7 2.2 %copy-start.8 = (f32[6,8,3,256]{3,1,2,0:T(8,128)S(1)}, f32[6,8,3,256]{3,1,2,0:T(8,128)}, u32[]{:S(2)}) copy-start(f32[6,8,3,256]{3,1,2,0:T(8,128)} %copy.32) | copy-start | bytes 442372
  53.7 2.2 %copy-start.9 = (f32[6,8,3,256]{3,1,2,0:T(8,128)S(1)}, f32[6,8,3,256]{3,1,2,0:T(8,128)}, u32[]{:S(2)}) copy-start(f32[6,8,3,256]{3,1,2,0:T(8,128)} %copy.33) | copy-start | bytes 442372
  64.9 7.4 %copy-start.10 = (bf16[6,256,128]{2,0,1:T(8,128)(2,1)S(1)}, bf16[6,256,128]{2,0,1:T(8,128)(2,1)}, u32[]{:S(2)}) copy-start(bf16[6,256,128]{2,0,1:T(8,128)(2,1)} %fusion.6) | copy-start | bytes 1179652
  67.4 10.0 %collective-permute-start.16 = (bf16[24,16,128]{2,1,0:T(8,128)(2,1)S(1)}, bf16[24,16,128]{2,1,0:T(8,128)(2,1)S(1)}, u32[]{:S(2)}, u32[]{:S(2)}) collective-permute-start(bf16[24,16,128]{2,1,0:T(8,128)(2,1)S(1)} %get-tuple-element.76), channel_id=1, source_target_pairs={{0,32},{32,64},{64,96},{96,128},{128,160},{160,192},{192,224},{224... | collective-permute-start | bytes 294920 | tf_op jit(solution)/shard_map/ppermute | solution.py:227
  75.1 5.7 %collective-permute-start.20 = (bf16[24,16,128]{2,1,0:T(8,128)(2,1)S(1)}, bf16[24,16,128]{2,1,0:T(8,128)(2,1)S(1)}, u32[]{:S(2)}, u32[]{:S(2)}) collective-permute-start(bf16[24,16,128]{2,1,0:T(8,128)(2,1)S(1)} %get-tuple-element.80), channel_id=1, source_target_pairs={{32,0},{64,32},{96,64},{128,96},{160,128},{192,160},{224,192},{0,2... | collective-permute-start | bytes 294920 | tf_op jit(solution)/shard_map/ppermute | solution.py:227
  75.2 5.8 %collective-permute-start.6 = (bf16[24,16,128]{2,1,0:T(8,128)(2,1)S(1)}, bf16[24,16,128]{2,1,0:T(8,128)(2,1)S(1)}, u32[]{:S(2)}, u32[]{:S(2)}) collective-permute-start(bf16[24,16,128]{2,1,0:T(8,128)(2,1)S(1)} %get-tuple-element.64), channel_id=1, source_target_pairs={{0,32},{32,64},{64,96},{96,128},{128,160},{160,192},{192,224},{224... | collective-permute-start | bytes 294920 | tf_op jit(solution)/shard_map/ppermute | solution.py:227
  77.3 5.8 %collective-permute-start.10 = (bf16[24,16,128]{2,1,0:T(8,128)(2,1)S(1)}, bf16[24,16,128]{2,1,0:T(8,128)(2,1)S(1)}, u32[]{:S(2)}, u32[]{:S(2)}) collective-permute-start(bf16[24,16,128]{2,1,0:T(8,128)(2,1)S(1)} %get-tuple-element.68), channel_id=1, source_target_pairs={{32,0},{64,32},{96,64},{128,96},{160,128},{192,160},{224,192},{0,2... | collective-permute-start | bytes 294920 | tf_op jit(solution)/shard_map/ppermute | solution.py:227
  77.5 7.4 %collective-permute-start.17 = (bf16[48,16,128]{2,1,0:T(8,128)(2,1)S(1)}, bf16[48,16,128]{2,1,0:T(8,128)(2,1)S(1)}, u32[]{:S(2)}, u32[]{:S(2)}) collective-permute-start(bf16[48,16,128]{2,1,0:T(8,128)(2,1)S(1)} %pad_maximum_fusion.4), channel_id=1, source_target_pairs={{0,32},{32,64},{64,96},{96,128},{128,160},{160,192},{192,224},{224... | collective-permute-start | bytes 589832 | tf_op jit(solution)/shard_map/ppermute | solution.py:227
  80.9 7.8 %collective-permute-start.21 = (bf16[48,16,128]{2,1,0:T(8,128)(2,1)S(1)}, bf16[48,16,128]{2,1,0:T(8,128)(2,1)S(1)}, u32[]{:S(2)}, u32[]{:S(2)}) collective-permute-start(bf16[48,16,128]{2,1,0:T(8,128)(2,1)S(1)} %pad_maximum_fusion.5), channel_id=1, source_target_pairs={{32,0},{64,32},{96,64},{128,96},{160,128},{192,160},{224,192},{0,2... | collective-permute-start | bytes 589832 | tf_op jit(solution)/shard_map/ppermute | solution.py:227
  81.1 8.1 %collective-permute-start.7 = (bf16[48,16,128]{2,1,0:T(8,128)(2,1)S(1)}, bf16[48,16,128]{2,1,0:T(8,128)(2,1)S(1)}, u32[]{:S(2)}, u32[]{:S(2)}) collective-permute-start(bf16[48,16,128]{2,1,0:T(8,128)(2,1)S(1)} %pad_maximum_fusion.2), channel_id=1, source_target_pairs={{0,32},{32,64},{64,96},{96,128},{128,160},{160,192},{192,224},{224... | collective-permute-start | bytes 589832 | tf_op jit(solution)/shard_map/ppermute | solution.py:227
  83.2 9.7 %collective-permute-start.11 = (bf16[48,16,128]{2,1,0:T(8,128)(2,1)S(1)}, bf16[48,16,128]{2,1,0:T(8,128)(2,1)S(1)}, u32[]{:S(2)}, u32[]{:S(2)}) collective-permute-start(bf16[48,16,128]{2,1,0:T(8,128)(2,1)S(1)} %pad_maximum_fusion.3), channel_id=1, source_target_pairs={{32,0},{64,32},{96,64},{128,96},{160,128},{192,160},{224,192},{0,2... | collective-permute-start | bytes 589832 | tf_op jit(solution)/shard_map/ppermute | solution.py:227
  85.0 8.4 %collective-permute-start.18 = (bf16[48,16,128]{2,1,0:T(8,128)(2,1)S(1)}, bf16[48,16,128]{2,1,0:T(8,128)(2,1)S(1)}, u32[]{:S(2)}, u32[]{:S(2)}) collective-permute-start(bf16[48,16,128]{2,1,0:T(8,128)(2,1)S(1)} %add_convert_fusion.3), channel_id=1, source_target_pairs={{0,32},{32,64},{64,96},{96,128},{128,160},{160,192},{192,224},{224... | collective-permute-start | bytes 589832 | tf_op jit(solution)/shard_map/ppermute | solution.py:227
  88.7 14.8 %copy-start.4 = (f32[3,256,128]{2,1,0:T(8,128)S(1)}, f32[3,256,128]{2,1,0:T(8,128)}, u32[]{:S(2)}) copy-start(f32[3,256,128]{2,1,0:T(8,128)} %fusion.20) | copy-start | bytes 1179652
  88.8 8.4 %collective-permute-start.22 = (bf16[48,16,128]{2,1,0:T(8,128)(2,1)S(1)}, bf16[48,16,128]{2,1,0:T(8,128)(2,1)S(1)}, u32[]{:S(2)}, u32[]{:S(2)}) collective-permute-start(bf16[48,16,128]{2,1,0:T(8,128)(2,1)S(1)} %add_convert_fusion.1), channel_id=1, source_target_pairs={{32,0},{64,32},{96,64},{128,96},{160,128},{192,160},{224,192},{0,2... | collective-permute-start | bytes 589832 | tf_op jit(solution)/shard_map/ppermute | solution.py:227
  89.2 8.8 %collective-permute-start.8 = (bf16[48,16,128]{2,1,0:T(8,128)(2,1)S(1)}, bf16[48,16,128]{2,1,0:T(8,128)(2,1)S(1)}, u32[]{:S(2)}, u32[]{:S(2)}) collective-permute-start(bf16[48,16,128]{2,1,0:T(8,128)(2,1)S(1)} %add_convert_fusion.7), channel_id=1, source_target_pairs={{0,32},{32,64},{64,96},{96,128},{128,160},{160,192},{192,224},{224... | collective-permute-start | bytes 589832 | tf_op jit(solution)/shard_map/ppermute | solution.py:227
  93.0 8.4 %collective-permute-start.12 = (bf16[48,16,128]{2,1,0:T(8,128)(2,1)S(1)}, bf16[48,16,128]{2,1,0:T(8,128)(2,1)S(1)}, u32[]{:S(2)}, u32[]{:S(2)}) collective-permute-start(bf16[48,16,128]{2,1,0:T(8,128)(2,1)S(1)} %add_convert_fusion.5), channel_id=1, source_target_pairs={{32,0},{64,32},{96,64},{128,96},{160,128},{192,160},{224,192},{0,2... | collective-permute-start | bytes 589832 | tf_op jit(solution)/shard_map/ppermute | solution.py:227
  93.5 8.0 %collective-permute-start.19 = (bf16[48,16,128]{2,1,0:T(8,128)(2,1)S(1)}, bf16[48,16,128]{2,1,0:T(8,128)(2,1)S(1)}, u32[]{:S(2)}, u32[]{:S(2)}) collective-permute-start(bf16[48,16,128]{2,1,0:T(8,128)(2,1)S(1)} %add_convert_fusion.2), channel_id=1, source_target_pairs={{0,32},{32,64},{64,96},{96,128},{128,160},{160,192},{192,224},{224... | collective-permute-start | bytes 589832 | tf_op jit(solution)/shard_map/ppermute | solution.py:227
  97.2 11.2 %copy-start.3 = (f32[3,256,128]{2,1,0:T(8,128)S(1)}, f32[3,256,128]{2,1,0:T(8,128)}, u32[]{:S(2)}) copy-start(f32[3,256,128]{2,1,0:T(8,128)} %fusion.22) | copy-start | bytes 1179652
  97.2 6.3 %collective-permute-start.23 = (bf16[48,16,128]{2,1,0:T(8,128)(2,1)S(1)}, bf16[48,16,128]{2,1,0:T(8,128)(2,1)S(1)}, u32[]{:S(2)}, u32[]{:S(2)}) collective-permute-start(bf16[48,16,128]{2,1,0:T(8,128)(2,1)S(1)} %add_convert_fusion), channel_id=1, source_target_pairs={{32,0},{64,32},{96,64},{128,96},{160,128},{192,160},{224,192},{0,2... | collective-permute-start | bytes 589832 | tf_op jit(solution)/shard_map/ppermute | solution.py:227
  98.1 10.2 %collective-permute-start.9 = (bf16[48,16,128]{2,1,0:T(8,128)(2,1)S(1)}, bf16[48,16,128]{2,1,0:T(8,128)(2,1)S(1)}, u32[]{:S(2)}, u32[]{:S(2)}) collective-permute-start(bf16[48,16,128]{2,1,0:T(8,128)(2,1)S(1)} %add_convert_fusion.6), channel_id=1, source_target_pairs={{0,32},{32,64},{64,96},{96,128},{128,160},{160,192},{192,224},{224... | collective-permute-start | bytes 589832 | tf_op jit(solution)/shard_map/ppermute | solution.py:227
  101.4 6.8 %collective-permute-start.13 = (bf16[48,16,128]{2,1,0:T(8,128)(2,1)S(1)}, bf16[48,16,128]{2,1,0:T(8,128)(2,1)S(1)}, u32[]{:S(2)}, u32[]{:S(2)}) collective-permute-start(bf16[48,16,128]{2,1,0:T(8,128)(2,1)S(1)} %add_convert_fusion.4), channel_id=1, source_target_pairs={{32,0},{64,32},{96,64},{128,96},{160,128},{192,160},{224,192},{0,2... | collective-permute-start | bytes 589832 | tf_op jit(solution)/shard_map/ppermute | solution.py:227
  103.9 7.7 %collective-permute-start.24 = (bf16[96,128]{1,0:T(8,128)(2,1)S(1)}, bf16[96,128]{1,0:T(8,128)(2,1)S(1)}, u32[]{:S(2)}, u32[]{:S(2)}) collective-permute-start(bf16[96,128]{1,0:T(8,128)(2,1)S(1)} %get-tuple-element.107), channel_id=1, source_target_pairs={{1,2},{2,1},{5,6},{6,5},{9,10},{10,9},{13,14},{14,13},{17,18},{18,... | collective-permute-start | bytes 73736 | tf_op jit(solution)/shard_map/ppermute | solution.py:25
  104.5 7.0 %collective-permute-start.25 = (bf16[96,128]{1,0:T(8,128)(2,1)S(1)}, bf16[96,128]{1,0:T(8,128)(2,1)S(1)}, u32[]{:S(2)}, u32[]{:S(2)}) collective-permute-start(bf16[96,128]{1,0:T(8,128)(2,1)S(1)} %get-tuple-element.106), channel_id=1, source_target_pairs={{0,1},{1,0},{2,3},{3,2},{4,5},{5,4},{6,7},{7,6},{8,9},{9,8},{10,11... | collective-permute-start | bytes 73736 | tf_op jit(solution)/shard_map/ppermute | solution.py:25
  108.3 4.5 %copy-start.2 = (bf16[48,48,768]{2,1,0:T(8,128)(2,1)S(1)}, bf16[48,48,768]{2,1,0:T(8,128)(2,1)}, u32[]{:S(2)}) copy-start(bf16[48,48,768]{2,1,0:T(8,128)(2,1)} %multiply_convert_fusion.1) | copy-start | bytes 10616836
  108.6 3.4 %collective-permute-start.14 = (bf16[96,128]{1,0:T(8,128)(2,1)S(1)}, bf16[96,128]{1,0:T(8,128)(2,1)S(1)}, u32[]{:S(2)}, u32[]{:S(2)}) collective-permute-start(bf16[96,128]{1,0:T(8,128)(2,1)S(1)} %get-tuple-element.111), channel_id=1, source_target_pairs={{1,2},{2,1},{5,6},{6,5},{9,10},{10,9},{13,14},{14,13},{17,18},{18,... | collective-permute-start | bytes 73736 | tf_op jit(solution)/shard_map/ppermute | solution.py:25
  109.4 3.0 %collective-permute-start.15 = (bf16[96,128]{1,0:T(8,128)(2,1)S(1)}, bf16[96,128]{1,0:T(8,128)(2,1)S(1)}, u32[]{:S(2)}, u32[]{:S(2)}) collective-permute-start(bf16[96,128]{1,0:T(8,128)(2,1)S(1)} %get-tuple-element.110), channel_id=1, source_target_pairs={{0,1},{1,0},{2,3},{3,2},{4,5},{5,4},{6,7},{7,6},{8,9},{9,8},{10,11... | collective-permute-start | bytes 73736 | tf_op jit(solution)/shard_map/ppermute | solution.py:25
  112.9 2.0 %copy-start.1 = (bf16[48,48,768]{2,1,0:T(8,128)(2,1)S(1)}, bf16[48,48,768]{2,1,0:T(8,128)(2,1)}, u32[]{:S(2)}) copy-start(bf16[48,48,768]{2,1,0:T(8,128)(2,1)} %multiply_convert_fusion) | copy-start | bytes 10616836
  115.9 25.6 %copy-start.15 = (f32[16,16,128]{2,1,0:T(8,128)S(1)}, f32[16,16,128]{2,1,0:T(8,128)}, u32[]{:S(2)}) copy-start(f32[16,16,128]{2,1,0:T(8,128)} %param.9) | copy-start | bytes 393220
  116.1 7.4 %collective-permute-start.26 = (f16[16,48,128]{2,1,0:T(8,128)(2,1)S(1)}, f16[16,48,128]{2,1,0:T(8,128)(2,1)S(1)}, u32[]{:S(2)}, u32[]{:S(2)}) collective-permute-start(f16[16,48,128]{2,1,0:T(8,128)(2,1)S(1)} %bitcast.127), channel_id=1, source_target_pairs={{0,32},{32,0},{64,96},{96,64},{128,160},{160,128},{192,224},{224,1... | collective-permute-start | bytes 589832 | tf_op jit(solution)/shard_map/ppermute | solution.py:25
  117.6 11.2 %collective-permute-start.27 = (f16[16,48,128]{2,1,0:T(8,128)(2,1)S(1)}, f16[16,48,128]{2,1,0:T(8,128)(2,1)S(1)}, u32[]{:S(2)}, u32[]{:S(2)}) collective-permute-start(f16[16,48,128]{2,1,0:T(8,128)(2,1)S(1)} %bitcast.126), channel_id=1, source_target_pairs={{32,64},{64,32},{96,128},{128,96},{160,192},{192,160},{33,65},{65,... | collective-permute-start | bytes 589832 | tf_op jit(solution)/shard_map/ppermute | solution.py:25
  129.0 6.3 %collective-permute-start.28 = (f16[16,16,128]{2,1,0:T(8,128)(2,1)S(1)}, f16[16,16,128]{2,1,0:T(8,128)(2,1)S(1)}, u32[]{:S(2)}, u32[]{:S(2)}) collective-permute-start(f16[16,16,128]{2,1,0:T(8,128)(2,1)S(1)} %get-tuple-element.102), channel_id=1, source_target_pairs={{0,4},{4,0},{8,12},{12,8},{16,20},{20,16},{24,28},{28,24},{1,5},{5... | collective-permute-start | bytes 196616 | tf_op jit(solution)/shard_map/ppermute | solution.py:25
  133.0 8.6 %collective-permute-start.29 = (f16[16,16,128]{2,1,0:T(8,128)(2,1)S(1)}, f16[16,16,128]{2,1,0:T(8,128)(2,1)S(1)}, u32[]{:S(2)}, u32[]{:S(2)}) collective-permute-start(f16[16,16,128]{2,1,0:T(8,128)(2,1)S(1)} %get-tuple-element.103), channel_id=1, source_target_pairs={{4,8},{8,4},{12,16},{16,12},{20,24},{24,20},{5,9},{9,5},{13,17},{1... | collective-permute-start | bytes 196616 | tf_op jit(solution)/shard_map/ppermute | solution.py:25

commit v5 on v1

--- a/solution.py
+++ b/solution.py
@@ -59,7 +59,7 @@
         wide[part, cols:] = halo.astype(wide.dtype)
 
 
-def with_columns(value, side):
+def column_sides(value, side):
     rows, cols = value.shape
     groups = cols // side
     packed = jax.ShapeDtypeStruct((rows // groups, cols), value.dtype)
@@ -71,7 +71,12 @@
         compiler_params=pltpu.CompilerParams(vmem_limit_bytes=32 << 20),
         name="edges",
     )(value)
-    before, after = order_sides(*neighbours(last, first, "gx"), "gx")
+    return neighbours(last, first, "gx")
+
+
+def with_columns(value, first, second):
+    rows, cols = value.shape
+    before, after = order_sides(first, second, "gx")
     return pl.pallas_call(
         widen_kernel,
         out_shape=jax.ShapeDtypeStruct((rows, 2 * cols), value.dtype),
@@ -284,7 +289,8 @@
     )
     usual_table, late_cell = lax.optimization_barrier((usual_table, late_cell))
     outgoing = pack(usual_table[0], tiles)
-    outgoing, psf, own_rows = lax.optimization_barrier((outgoing, psf, own_rows))
+    outgoing, psf = lax.optimization_barrier((outgoing, psf))
+    own_rows, _ = lax.optimization_barrier((own_rows, psf))
     arrived = exchange(outgoing)
 
     kernels = psf / jnp.sum(psf, axis=-1, keepdims=True)
@@ -312,8 +318,16 @@
     )
     offset = column[:, None] - jnp.arange(cols)[None, :]
     col_taps = taps_table(kernels[:, 2], radius + offset).astype(jnp.bfloat16)
-    col_taps_back = taps_table(kernels[:, 2], radius - offset).astype(jnp.bfloat16)
-    field = with_columns(own, side)
+    first, second = column_sides(own, side)
+    arrived, first, second = lax.optimization_barrier((arrived, first, second))
+    blocks = [
+        join(c, ends, usual_table[1], late_cell, arrived, late, gz_count, chunk * positions)
+        for c in range(chunks)
+    ]
+    back_kernels, _ = lax.optimization_barrier((kernels[:, 2], blocks[-1][0]))
+    col_taps_back = taps_table(back_kernels, radius - offset).astype(jnp.bfloat16)
+    first, second, _ = lax.optimization_barrier((first, second, blocks[-1][0]))
+    field = with_columns(own, first, second)
     blurred = []
     for c in range(chunks):
         swept = lax.dot_general(
@@ -328,17 +342,13 @@
                 preferred_element_type=jnp.float32,
             )
         )
-    arrived, blurred = lax.optimization_barrier((arrived, blurred))
-    joined = []
-    for c in range(chunks):
-        blocks = join(c, ends, usual_table[1], late_cell, arrived, late, gz_count, chunk * positions)
-        joined.append(ring_sum(blocks))
+    joined = [ring_sum(blocks[c]) for c in range(chunks)]
     total = jnp.zeros((tall * wide, cols), jnp.float32)
     for c in range(chunks):
         views = slice(c * chunk, (c + 1) * chunk)
         ratio = joined[c].reshape(chunk, area, cols) / (blurred[c] + background_level)
         ratio = ratio.astype(jnp.bfloat16).reshape(chunk * area, cols)
-        ratio = with_columns(ratio, side).reshape(chunk, area, -1)
+        ratio = with_columns(ratio, *column_sides(ratio, side)).reshape(chunk, area, -1)
         spread = jnp.einsum(
             "vac,vck->vak", ratio, col_taps_back[views], preferred_element_type=jnp.float32
         )

time: 128 us -> 126 us (0.984)
  matrix products: 12.8 us -> 9.53 us
  starting transfers between devices: 65.2 us -> 63.9 us
    convert_element_type x2, other arithmetic: 1.86 us -> 5.38 us  [on_device(): sheet = (down * across).astype(jnp.bfloat16)]
    ppermute x7, starting transfers between devices: 27.9 us -> 25.4 us  [neighbours(): lax.ppermute(second, axis, pairs[1])]
    dot_general x4, matrix products: 6.41 us -> 3.96 us  [taps_table(): return jnp.einsum('eim,vm->vei', table, kernel_set, precision=highest)]
    select_n x5, other arithmetic: 1.85 us -> 0.08 us  [order_sides(): return (jnp.where(even, second, first), jnp.where(even, first, second))]
    ppermute x7, waiting for transfers between devices: 14.9 us -> 16.4 us  [neighbours(): lax.ppermute(second, axis, pairs[1])]
    all_to_all x1, starting transfers between devices: 7.22 us -> 5.77 us  [exchange(): return lax.all_to_all(value, 'gy', split_axis=0, concat_axis=0, tiled=True)]
    ppermute x7, starting transfers between devices: 4.1 us -> 5.51 us  [neighbours(): lax.ppermute(first, axis, pairs[0])]
    unnamed x44 -> x20, local copies, waits for them, and re-layouts: 2.81 us -> 3.39 us
  transfers between devices with their start and end apart: 31 -> 31, of which waited for: 12 -> 13; matrix products, arithmetic and copies ran while one was open for 18% -> 16% of each run, Pallas kernels for 4% -> 2%
where the time goes in v5:
time: 126 us; the launch traced here: 125 us
  starting transfers between devices  63.9 us (51%)
  waiting for transfers between devices  24.8 us (20%)
  other arithmetic  11.5 us (9%)
  matrix products  9.53 us (8%)
  Pallas kernels  8.59 us (7%)
  local copies, waits for them, and re-layouts  5.52 us (4%)
  between operations  1.62 us (1%)
    ppermute x16, starting transfers between devices, ring_step(): return (lax.ppermute(upward, 'gz', up), lax.ppermute(downward, 'gz', down))  27.2 us
    ppermute x7, starting transfers between devices, neighbours(): lax.ppermute(second, axis, pairs[1])  25.4 us
    ppermute x7, waiting for transfers between devices, neighbours(): lax.ppermute(second, axis, pairs[1])  16.4 us
    pallas_call x2, Pallas kernels, join(): pl.pallas_call(functools.partial(join_kernel, chunk), out_shape=[jax.Shap...  6.1 us
    all_to_all x1, starting transfers between devices, exchange(): return lax.all_to_all(value, 'gy', split_axis=0, concat_axis=0, tiled=True)  5.77 us
    ppermute x7, starting transfers between devices, neighbours(): lax.ppermute(first, axis, pairs[0])  5.51 us
    convert_element_type x2, other arithmetic, on_device(): sheet = (down * across).astype(jnp.bfloat16)  5.38 us
    ppermute x16, waiting for transfers between devices, ring_step(): return (lax.ppermute(upward, 'gz', up), lax.ppermute(downward, 'gz', down))  5.31 us
  transfers between devices with their start and end apart: 31, of which 13 were waited for; matrix products, arithmetic and copies ran while one was open for 16% of the time, Pallas kernels for 2%

profile of v5, /device:TPU:106, one launch (start us, length us, event | category | flops | bytes accessed | tf_op | source)
XLA Modules:
  0.0 125.5 jit_solution(58286360988235197)
XLA Ops:
  0.0 1.0 convert_element_type.228
  1.0 4.2 %collective-permute-start.1 = (bf16[16,16,128]{2,1,0:T(8,128)(2,1)S(1)}, bf16[16,16,128]{2,1,0:T(8,128)(2,1)S(1)}, u32[]{:S(2)}, u32[]{:S(2)}) collective-permute-start(bf16[16,16,128]{2,1,0:T(8,128)(2,1)S(1)} %convert_element_type.228), channel_id=1, source_target_pairs={{4,8},{8,4},{12,16},{16,12},{20,24},{24,20},{5,9},{9,5},{13,17},{1... | collective-permute-start | bytes 196616 | tf_op jit(solution)/shard_map/ppermute | solution.py:25
  5.2 2.3 %collective-permute-start = (bf16[16,16,128]{2,1,0:T(8,128)(2,1)S(1)}, bf16[16,16,128]{2,1,0:T(8,128)(2,1)S(1)}, u32[]{:S(2)}, u32[]{:S(2)}) collective-permute-start(bf16[16,16,128]{2,1,0:T(8,128)(2,1)S(1)} %convert_element_type.228), channel_id=1, source_target_pairs={{0,4},{4,0},{8,12},{12,8},{16,20},{20,16},{24,28},{28,24},{1,5},{5... | collective-permute-start | bytes 196616 | tf_op jit(solution)/shard_map/ppermute | solution.py:25
  7.5 1.0 add_select_fusion
  8.5 1.0 reshape.561
  9.9 0.2 convert_reduce_fusion
  10.1 0.6 reduce_max.9
  11.7 0.4 select_reduce_fusion.1
  12.1 1.1 copy-done.3
  13.2 1.1 pack.3
  14.3 1.3 %copy-done = bf16[8,56,16,128]{3,2,1,0:T(8,128)(2,1)} copy-done((bf16[8,56,16,128]{3,2,1,0:T(8,128)(2,1)}, bf16[8,56,16,128]{3,2,1,0:T(8,128)(2,1)S(1)}, u32[]{:S(2)}) %copy-start) | copy-done | bytes 1835032
  15.6 5.8 %all-to-all-start.1 = ((bf16[8,56,16,128]{3,2,1,0:T(8,128)(2,1)}), bf16[8,56,16,128]{3,2,1,0:T(8,128)(2,1)S(1)}, u32[]{:S(2)}, u32[]{:S(2)}) async-start(bf16[8,56,16,128]{3,2,1,0:T(8,128)(2,1)} %copy-done), calls=%async_computation.1 | async-start | bytes 3670016 | tf_op jit(solution)/shard_map/all_to_all | solution.py:221
  22.0 0.6 fusion.5
  22.7 0.6 fusion.4
  23.5 1.4 %fusion.7 = bf16[6,256,128]{2,0,1:T(8,128)(2,1)S(1)} fusion(s32[256,128]{1,0:T(8,128)S(1)} %get-tuple-element.125, f32[6,3,31]{2,0,1:T(8,128)S(1)} %copy_divide_fusion), kind=kOutput, calls=%fused_computation.20 | convolution fusion | flops 74350592 | bytes 528384 | tf_op jit(solution)/shard_map/eim,vm->vei/dot_general | solution.py:93
  24.9 0.2 fusion.64
  25.1 2.7 %multiply_convert_fusion.1 = bf16[48,48,768]{2,1,0:T(8,128)(2,1)} fusion(f32[48,768]{1,0:T(8,128)S(1)} %bitcast.110, f32[48,768]{1,0:T(8,128)S(1)} %bitcast.112), kind=kLoop, calls=%fused_computation.5 | loop fusion | flops 3538944 | bytes 3833856 | tf_op jit(solution)/shard_map/convert_element_type | solution.py:308
  27.7 2.7 %multiply_convert_fusion = bf16[48,48,768]{2,1,0:T(8,128)(2,1)} fusion(f32[48,768]{1,0:T(8,128)S(1)} %bitcast.109, f32[48,768]{1,0:T(8,128)S(1)} %bitcast.111), kind=kLoop, calls=%fused_computation.4 | loop fusion | flops 3538944 | bytes 3833856 | tf_op jit(solution)/shard_map/convert_element_type | solution.py:308
  30.5 0.3 convert_reduce_fusion.1
  30.9 0.2 collective-permute-start.3
  31.1 5.9 %collective-permute-start.2 = (bf16[16,48,128]{2,1,0:T(8,128)(2,1)S(1)}, bf16[16,48,128]{2,1,0:T(8,128)(2,1)S(1)}, u32[]{:S(2)}, u32[]{:S(2)}) collective-permute-start(bf16[16,48,128]{2,1,0:T(8,128)(2,1)S(1)} %pad_maximum_fusion.1), channel_id=1, source_target_pairs={{32,64},{64,32},{96,128},{128,96},{160,192},{192,160},{33,65},{65,... | collective-permute-start | bytes 589832 | tf_op jit(solution)/shard_map/ppermute | solution.py:25
  37.1 3.6 %collective-permute-done.2 = bf16[16,48,128]{2,1,0:T(8,128)(2,1)S(1)} collective-permute-done((bf16[16,48,128]{2,1,0:T(8,128)(2,1)S(1)}, bf16[16,48,128]{2,1,0:T(8,128)(2,1)S(1)}, u32[]{:S(2)}, u32[]{:S(2)}) %collective-permute-start.2) | collective-permute-done | bytes 196640 | tf_op jit(solution)/shard_map/ppermute | solution.py:25
  40.8 0.3 edges.3
  41.1 1.9 %collective-permute-start.5 = (bf16[288,128]{1,0:T(8,128)(2,1)S(1)}, bf16[288,128]{1,0:T(8,128)(2,1)S(1)}, u32[]{:S(2)}, u32[]{:S(2)}) collective-permute-start(bf16[288,128]{1,0:T(8,128)(2,1)S(1)} %get-tuple-element.110), channel_id=1, source_target_pairs={{1,2},{2,1},{5,6},{6,5},{9,10},{10,9},{13,14},{14,13},{17,18},{18,... | collective-permute-start | bytes 221192 | tf_op jit(solution)/shard_map/ppermute | solution.py:25
  43.2 3.6 %collective-permute-done.5 = bf16[288,128]{1,0:T(8,128)(2,1)S(1)} collective-permute-done((bf16[288,128]{1,0:T(8,128)(2,1)S(1)}, bf16[288,128]{1,0:T(8,128)(2,1)S(1)}, u32[]{:S(2)}, u32[]{:S(2)}) %collective-permute-start.5) | collective-permute-done | bytes 73760 | tf_op jit(solution)/shard_map/ppermute | solution.py:25
  46.8 3.5 %join.3 = (bf16[48,16,128]{2,1,0:T(8,128)(2,1)S(1)}, bf16[48,16,128]{2,1,0:T(8,128)(2,1)S(1)}, bf16[48,16,128]{2,1,0:T(8,128)(2,1)S(1)}, bf16[48,16,128]{2,1,0:T...) custom-call(s32[3,8]{1,0:T(4,128)S(1)} %pad_add_fusion.1.ends, ...), custom_call_target="tpu_custom_call" | custom-call | tf_op jit(solution)/shard_map/join/pallas_call | solution.py:200
  50.3 2.6 %join.2 = (bf16[48,16,128]{2,1,0:T(8,128)(2,1)S(1)}, bf16[48,16,128]{2,1,0:T(8,128)(2,1)S(1)}, bf16[48,16,128]{2,1,0:T(8,128)(2,1)S(1)}, bf16[48,16,128]{2,1,0:T...) custom-call(s32[3,8]{1,0:T(4,128)S(1)} %pad_add_fusion.1.ends, ...), custom_call_target="tpu_custom_call" | custom-call | tf_op jit(solution)/shard_map/join/pallas_call | solution.py:200
  53.0 3.5 %collective-permute-start.16 = (bf16[24,16,128]{2,1,0:T(8,128)(2,1)S(1)}, bf16[24,16,128]{2,1,0:T(8,128)(2,1)S(1)}, u32[]{:S(2)}, u32[]{:S(2)}) collective-permute-start(bf16[24,16,128]{2,1,0:T(8,128)(2,1)S(1)} %get-tuple-element.83), channel_id=1, source_target_pairs={{0,32},{32,64},{64,96},{96,128},{128,160},{160,192},{192,224},{224... | collective-permute-start | bytes 294920 | tf_op jit(solution)/shard_map/ppermute | solution.py:232
  56.4 3.2 %collective-permute-start.6 = (bf16[24,16,128]{2,1,0:T(8,128)(2,1)S(1)}, bf16[24,16,128]{2,1,0:T(8,128)(2,1)S(1)}, u32[]{:S(2)}, u32[]{:S(2)}) collective-permute-start(bf16[24,16,128]{2,1,0:T(8,128)(2,1)S(1)} %get-tuple-element.67), channel_id=1, source_target_pairs={{0,32},{32,64},{64,96},{96,128},{128,160},{160,192},{192,224},{224... | collective-permute-start | bytes 294920 | tf_op jit(solution)/shard_map/ppermute | solution.py:232
  59.7 1.4 %fusion.6 = bf16[6,256,128]{2,0,1:T(8,128)(2,1)S(1)} fusion(s32[256,128]{1,0:T(8,128)S(1)} %get-tuple-element.124, f32[6,31]{1,0:T(8,128)S(1)} %slice_bitcast_fusion.8), kind=kOutput, calls=%fused_computation.19 | convolution fusion | flops 74350592 | bytes 525032 | tf_op jit(solution)/shard_map/eim,vm->vei/dot_general | solution.py:93
  61.1 0.2 fusion.63
  61.3 0.4 widen.3
  61.7 1.1 convolution_convert_fusion.1
  62.8 0.9 copy-done.1
  63.7 1.1 convolution_convert_fusion
  64.8 0.3 convolution_add_fusion.2
  65.1 0.3 convolution_add_fusion.1
  65.7 3.3 %collective-permute-start.7 = (bf16[48,16,128]{2,1,0:T(8,128)(2,1)S(1)}, bf16[48,16,128]{2,1,0:T(8,128)(2,1)S(1)}, u32[]{:S(2)}, u32[]{:S(2)}) collective-permute-start(bf16[48,16,128]{2,1,0:T(8,128)(2,1)S(1)} %pad_maximum_fusion.2), channel_id=1, source_target_pairs={{0,32},{32,64},{64,96},{96,128},{128,160},{160,192},{192,224},{224... | collective-permute-start | bytes 589832 | tf_op jit(solution)/shard_map/ppermute | solution.py:232
  69.2 3.3 %collective-permute-start.17 = (bf16[48,16,128]{2,1,0:T(8,128)(2,1)S(1)}, bf16[48,16,128]{2,1,0:T(8,128)(2,1)S(1)}, u32[]{:S(2)}, u32[]{:S(2)}) collective-permute-start(bf16[48,16,128]{2,1,0:T(8,128)(2,1)S(1)} %pad_maximum_fusion.4), channel_id=1, source_target_pairs={{0,32},{32,64},{64,96},{96,128},{128,160},{160,192},{192,224},{224... | collective-permute-start | bytes 589832 | tf_op jit(solution)/shard_map/ppermute | solution.py:232
  72.5 2.1 %collective-permute-done.11 = bf16[48,16,128]{2,1,0:T(8,128)(2,1)S(1)} collective-permute-done((bf16[48,16,128]{2,1,0:T(8,128)(2,1)S(1)}, bf16[48,16,128]{2,1,0:T(8,128)(2,1)S(1)}, u32[]{:S(2)}, u32[]{:S(2)}) %collective-permute-start.11) | collective-permute-done | bytes 196640 | tf_op jit(solution)/shard_map/ppermute | solution.py:232
  74.8 3.3 %collective-permute-start.8 = (bf16[48,16,128]{2,1,0:T(8,128)(2,1)S(1)}, bf16[48,16,128]{2,1,0:T(8,128)(2,1)S(1)}, u32[]{:S(2)}, u32[]{:S(2)}) collective-permute-start(bf16[48,16,128]{2,1,0:T(8,128)(2,1)S(1)} %add_convert_fusion.7), channel_id=1, source_target_pairs={{0,32},{32,64},{64,96},{96,128},{128,160},{160,192},{192,224},{224... | collective-permute-start | bytes 589832 | tf_op jit(solution)/shard_map/ppermute | solution.py:232
  78.1 0.7 collective-permute-done.21
  79.1 3.3 %collective-permute-start.18 = (bf16[48,16,128]{2,1,0:T(8,128)(2,1)S(1)}, bf16[48,16,128]{2,1,0:T(8,128)(2,1)S(1)}, u32[]{:S(2)}, u32[]{:S(2)}) collective-permute-start(bf16[48,16,128]{2,1,0:T(8,128)(2,1)S(1)} %add_convert_fusion.3), channel_id=1, source_target_pairs={{0,32},{32,64},{64,96},{96,128},{128,160},{160,192},{192,224},{224... | collective-permute-start | bytes 589832 | tf_op jit(solution)/shard_map/ppermute | solution.py:232
  82.3 0.6 collective-permute-done.12
  83.0 0.3 collective-permute-start.13
  83.4 3.3 %collective-permute-start.9 = (bf16[48,16,128]{2,1,0:T(8,128)(2,1)S(1)}, bf16[48,16,128]{2,1,0:T(8,128)(2,1)S(1)}, u32[]{:S(2)}, u32[]{:S(2)}) collective-permute-start(bf16[48,16,128]{2,1,0:T(8,128)(2,1)S(1)} %add_convert_fusion.6), channel_id=1, source_target_pairs={{0,32},{32,64},{64,96},{96,128},{128,160},{160,192},{192,224},{224... | collective-permute-start | bytes 589832 | tf_op jit(solution)/shard_map/ppermute | solution.py:232
  86.7 1.3 %collective-permute-done.22 = bf16[48,16,128]{2,1,0:T(8,128)(2,1)S(1)} collective-permute-done((bf16[48,16,128]{2,1,0:T(8,128)(2,1)S(1)}, bf16[48,16,128]{2,1,0:T(8,128)(2,1)S(1)}, u32[]{:S(2)}, u32[]{:S(2)}) %collective-permute-start.22) | collective-permute-done | bytes 196640 | tf_op jit(solution)/shard_map/ppermute | solution.py:232
  88.2 3.3 %collective-permute-start.19 = (bf16[48,16,128]{2,1,0:T(8,128)(2,1)S(1)}, bf16[48,16,128]{2,1,0:T(8,128)(2,1)S(1)}, u32[]{:S(2)}, u32[]{:S(2)}) collective-permute-start(bf16[48,16,128]{2,1,0:T(8,128)(2,1)S(1)} %add_convert_fusion.2), channel_id=1, source_target_pairs={{0,32},{32,64},{64,96},{96,128},{128,160},{160,192},{192,224},{224... | collective-permute-start | bytes 589832 | tf_op jit(solution)/shard_map/ppermute | solution.py:232
  92.0 2.6 %collective-permute-start.14 = (bf16[96,128]{1,0:T(8,128)(2,1)S(1)}, bf16[96,128]{1,0:T(8,128)(2,1)S(1)}, u32[]{:S(2)}, u32[]{:S(2)}) collective-permute-start(bf16[96,128]{1,0:T(8,128)(2,1)S(1)} %get-tuple-element.121), channel_id=1, source_target_pairs={{1,2},{2,1},{5,6},{6,5},{9,10},{10,9},{13,14},{14,13},{17,18},{18,... | collective-permute-start | bytes 73736 | tf_op jit(solution)/shard_map/ppermute | solution.py:25
  94.6 0.5 collective-permute-done.23
  95.5 2.5 %collective-permute-start.24 = (bf16[96,128]{1,0:T(8,128)(2,1)S(1)}, bf16[96,128]{1,0:T(8,128)(2,1)S(1)}, u32[]{:S(2)}, u32[]{:S(2)}) collective-permute-start(bf16[96,128]{1,0:T(8,128)(2,1)S(1)} %get-tuple-element.117), channel_id=1, source_target_pairs={{1,2},{2,1},{5,6},{6,5},{9,10},{10,9},{13,14},{14,13},{17,18},{18,... | collective-permute-start | bytes 73736 | tf_op jit(solution)/shard_map/ppermute | solution.py:25
  98.2 0.2 convolution_convert_fusion.3
  98.5 1.1 fusion.68
  99.6 1.0 collective-permute-done.24
  100.8 0.2 convolution_convert_fusion.2
  101.0 1.1 fusion.67
  102.3 5.4 %collective-permute-start.27 = (f16[16,48,128]{2,1,0:T(8,128)(2,1)S(1)}, f16[16,48,128]{2,1,0:T(8,128)(2,1)S(1)}, u32[]{:S(2)}, u32[]{:S(2)}) collective-permute-start(f16[16,48,128]{2,1,0:T(8,128)(2,1)S(1)} %bitcast.118), channel_id=1, source_target_pairs={{32,64},{64,32},{96,128},{128,96},{160,192},{192,160},{33,65},{65,... | collective-permute-start | bytes 589832 | tf_op jit(solution)/shard_map/ppermute | solution.py:25
  107.8 3.5 %collective-permute-done.27 = f16[16,48,128]{2,1,0:T(8,128)(2,1)S(1)} collective-permute-done((f16[16,48,128]{2,1,0:T(8,128)(2,1)S(1)}, f16[16,48,128]{2,1,0:T(8,128)(2,1)S(1)}, u32[]{:S(2)}, u32[]{:S(2)}) %collective-permute-start.27) | collective-permute-done | bytes 196640 | tf_op jit(solution)/shard_map/ppermute | solution.py:25
  111.3 2.1 %collective-permute-done.26 = f16[16,48,128]{2,1,0:T(8,128)(2,1)S(1)} collective-permute-done((f16[16,48,128]{2,1,0:T(8,128)(2,1)S(1)}, f16[16,48,128]{2,1,0:T(8,128)(2,1)S(1)}, u32[]{:S(2)}, u32[]{:S(2)}) %collective-permute-start.26) | collective-permute-done | bytes 196640 | tf_op jit(solution)/shard_map/ppermute | solution.py:25
  113.6 2.7 %collective-permute-start.28 = (f16[16,16,128]{2,1,0:T(8,128)(2,1)S(1)}, f16[16,16,128]{2,1,0:T(8,128)(2,1)S(1)}, u32[]{:S(2)}, u32[]{:S(2)}) collective-permute-start(f16[16,16,128]{2,1,0:T(8,128)(2,1)S(1)} %get-tuple-element.106), channel_id=1, source_target_pairs={{0,4},{4,0},{8,12},{12,8},{16,20},{20,16},{24,28},{28,24},{1,5},{5... | collective-permute-start | bytes 196616 | tf_op jit(solution)/shard_map/ppermute | solution.py:25
  116.2 2.9 %collective-permute-start.29 = (f16[16,16,128]{2,1,0:T(8,128)(2,1)S(1)}, f16[16,16,128]{2,1,0:T(8,128)(2,1)S(1)}, u32[]{:S(2)}, u32[]{:S(2)}) collective-permute-start(f16[16,16,128]{2,1,0:T(8,128)(2,1)S(1)} %get-tuple-element.107), channel_id=1, source_target_pairs={{4,8},{8,4},{12,16},{16,12},{20,24},{24,20},{5,9},{9,5},{13,17},{1... | collective-permute-start | bytes 196616 | tf_op jit(solution)/shard_map/ppermute | solution.py:25
  119.1 1.0 collective-permute-done.28
  120.1 4.7 %collective-permute-done.29 = f16[16,16,128]{2,1,0:T(8,128)(2,1)S(1)} collective-permute-done((f16[16,16,128]{2,1,0:T(8,128)(2,1)S(1)}, f16[16,16,128]{2,1,0:T(8,128)(2,1)S(1)}, u32[]{:S(2)}, u32[]{:S(2)}) %collective-permute-start.29) | collective-permute-done | bytes 65568 | tf_op jit(solution)/shard_map/ppermute | solution.py:25
  124.8 0.7 fusion.22
  (125 shorter events, 4.6 us)
Async XLA Ops:
  0.0 12.1 %copy-start.5 = (bf16[6,48,2,8,128]{4,3,2,1,0:T(8,128)(2,1)S(1)}, bf16[6,48,2,8,128]{4,3,2,1,0:T(8,128)(2,1)}, u32[]{:S(2)}) copy-start(bf16[6,48,2,8,128]{4,3,2,1,0:T(8,128)(2,1)} %param.6) | copy-start | bytes 3538948
  1.0 29.8 %collective-permute-start.1 = (bf16[16,16,128]{2,1,0:T(8,128)(2,1)S(1)}, bf16[16,16,128]{2,1,0:T(8,128)(2,1)S(1)}, u32[]{:S(2)}, u32[]{:S(2)}) collective-permute-start(bf16[16,16,128]{2,1,0:T(8,128)(2,1)S(1)} %convert_element_type.228), channel_id=1, source_target_pairs={{4,8},{8,4},{12,16},{16,12},{20,24},{24,20},{5,9},{9,5},{13,17},{1... | collective-permute-start | bytes 196616 | tf_op jit(solution)/shard_map/ppermute | solution.py:25
  5.2 25.6 %collective-permute-start = (bf16[16,16,128]{2,1,0:T(8,128)(2,1)S(1)}, bf16[16,16,128]{2,1,0:T(8,128)(2,1)S(1)}, u32[]{:S(2)}, u32[]{:S(2)}) collective-permute-start(bf16[16,16,128]{2,1,0:T(8,128)(2,1)S(1)} %convert_element_type.228), channel_id=1, source_target_pairs={{0,4},{4,0},{8,12},{12,8},{16,20},{20,16},{24,28},{28,24},{1,5},{5... | collective-permute-start | bytes 196616 | tf_op jit(solution)/shard_map/ppermute | solution.py:25
  12.1 1.1 copy-start.3
  14.3 1.3 %copy-start = (bf16[8,56,16,128]{3,2,1,0:T(8,128)(2,1)}, bf16[8,56,16,128]{3,2,1,0:T(8,128)(2,1)S(1)}, u32[]{:S(2)}) copy-start(bf16[8,56,16,128]{3,2,1,0:T(8,128)(2,1)S(1)} %pack.3) | copy-start | bytes 5505028
  15.6 6.1 %copy-start.7 = (f32[6,3,31]{2,1,0:T(4,128)S(1)}, f32[6,3,31]{2,1,0:T(4,128)}, u32[]{:S(2)}) copy-start(f32[6,3,31]{2,1,0:T(4,128)} %param.8) | copy-start | bytes 6700
  15.6 31.2 %all-to-all-start.1 = ((bf16[8,56,16,128]{3,2,1,0:T(8,128)(2,1)}), bf16[8,56,16,128]{3,2,1,0:T(8,128)(2,1)S(1)}, u32[]{:S(2)}, u32[]{:S(2)}) async-start(bf16[8,56,16,128]{3,2,1,0:T(8,128)(2,1)} %copy-done), calls=%async_computation.1 | async-start | bytes 3670016 | tf_op jit(solution)/shard_map/all_to_all | solution.py:221
  30.9 6.2 %collective-permute-start.3 = (bf16[16,48,128]{2,1,0:T(8,128)(2,1)S(1)}, bf16[16,48,128]{2,1,0:T(8,128)(2,1)S(1)}, u32[]{:S(2)}, u32[]{:S(2)}) collective-permute-start(bf16[16,48,128]{2,1,0:T(8,128)(2,1)S(1)} %pad_maximum_fusion.1), channel_id=1, source_target_pairs={{0,32},{32,0},{64,96},{96,64},{128,160},{160,128},{192,224},{224,1... | collective-permute-start | bytes 589832 | tf_op jit(solution)/shard_map/ppermute | solution.py:25
  31.1 9.6 %collective-permute-start.2 = (bf16[16,48,128]{2,1,0:T(8,128)(2,1)S(1)}, bf16[16,48,128]{2,1,0:T(8,128)(2,1)S(1)}, u32[]{:S(2)}, u32[]{:S(2)}) collective-permute-start(bf16[16,48,128]{2,1,0:T(8,128)(2,1)S(1)} %pad_maximum_fusion.1), channel_id=1, source_target_pairs={{32,64},{64,32},{96,128},{128,96},{160,192},{192,160},{33,65},{65,... | collective-permute-start | bytes 589832 | tf_op jit(solution)/shard_map/ppermute | solution.py:25
  41.1 5.7 %collective-permute-start.5 = (bf16[288,128]{1,0:T(8,128)(2,1)S(1)}, bf16[288,128]{1,0:T(8,128)(2,1)S(1)}, u32[]{:S(2)}, u32[]{:S(2)}) collective-permute-start(bf16[288,128]{1,0:T(8,128)(2,1)S(1)} %get-tuple-element.110), channel_id=1, source_target_pairs={{1,2},{2,1},{5,6},{6,5},{9,10},{10,9},{13,14},{14,13},{17,18},{18,... | collective-permute-start | bytes 221192 | tf_op jit(solution)/shard_map/ppermute | solution.py:25
  43.1 3.7 %collective-permute-start.4 = (bf16[288,128]{1,0:T(8,128)(2,1)S(1)}, bf16[288,128]{1,0:T(8,128)(2,1)S(1)}, u32[]{:S(2)}, u32[]{:S(2)}) collective-permute-start(bf16[288,128]{1,0:T(8,128)(2,1)S(1)} %get-tuple-element.111), channel_id=1, source_target_pairs={{0,1},{1,0},{2,3},{3,2},{4,5},{5,4},{6,7},{7,6},{8,9},{9,8},{10,11... | collective-permute-start | bytes 221192 | tf_op jit(solution)/shard_map/ppermute | solution.py:25
  46.8 3.5 %copy-start.4 = (bf16[8,40,16,128]{3,2,1,0:T(8,128)(2,1)S(1)}, bf16[8,40,16,128]{3,2,1,0:T(8,128)(2,1)}, u32[]{:S(2)}) copy-start(bf16[8,40,16,128]{3,2,1,0:T(8,128)(2,1)} %copy-done.3) | copy-start | bytes 3932164
  53.0 16.2 %collective-permute-start.16 = (bf16[24,16,128]{2,1,0:T(8,128)(2,1)S(1)}, bf16[24,16,128]{2,1,0:T(8,128)(2,1)S(1)}, u32[]{:S(2)}, u32[]{:S(2)}) collective-permute-start(bf16[24,16,128]{2,1,0:T(8,128)(2,1)S(1)} %get-tuple-element.83), channel_id=1, source_target_pairs={{0,32},{32,64},{64,96},{96,128},{128,160},{160,192},{192,224},{224... | collective-permute-start | bytes 294920 | tf_op jit(solution)/shard_map/ppermute | solution.py:232
  56.4 12.6 %collective-permute-start.20 = (bf16[24,16,128]{2,1,0:T(8,128)(2,1)S(1)}, bf16[24,16,128]{2,1,0:T(8,128)(2,1)S(1)}, u32[]{:S(2)}, u32[]{:S(2)}) collective-permute-start(bf16[24,16,128]{2,1,0:T(8,128)(2,1)S(1)} %get-tuple-element.87), channel_id=1, source_target_pairs={{32,0},{64,32},{96,64},{128,96},{160,128},{192,160},{224,192},{0,2... | collective-permute-start | bytes 294920 | tf_op jit(solution)/shard_map/ppermute | solution.py:232
  56.4 9.2 %collective-permute-start.6 = (bf16[24,16,128]{2,1,0:T(8,128)(2,1)S(1)}, bf16[24,16,128]{2,1,0:T(8,128)(2,1)S(1)}, u32[]{:S(2)}, u32[]{:S(2)}) collective-permute-start(bf16[24,16,128]{2,1,0:T(8,128)(2,1)S(1)} %get-tuple-element.67), channel_id=1, source_target_pairs={{0,32},{32,64},{64,96},{96,128},{128,160},{160,192},{192,224},{224... | collective-permute-start | bytes 294920 | tf_op jit(solution)/shard_map/ppermute | solution.py:232
  59.7 5.8 %collective-permute-start.10 = (bf16[24,16,128]{2,1,0:T(8,128)(2,1)S(1)}, bf16[24,16,128]{2,1,0:T(8,128)(2,1)S(1)}, u32[]{:S(2)}, u32[]{:S(2)}) collective-permute-start(bf16[24,16,128]{2,1,0:T(8,128)(2,1)S(1)} %get-tuple-element.71), channel_id=1, source_target_pairs={{32,0},{64,32},{96,64},{128,96},{160,128},{192,160},{224,192},{0,2... | collective-permute-start | bytes 294920 | tf_op jit(solution)/shard_map/ppermute | solution.py:232
  59.7 2.0 %copy-start.2 = (bf16[48,48,768]{2,1,0:T(8,128)(2,1)S(1)}, bf16[48,48,768]{2,1,0:T(8,128)(2,1)}, u32[]{:S(2)}) copy-start(bf16[48,48,768]{2,1,0:T(8,128)(2,1)} %multiply_convert_fusion.1) | copy-start | bytes 10616836
  61.7 2.0 %copy-start.1 = (bf16[48,48,768]{2,1,0:T(8,128)(2,1)S(1)}, bf16[48,48,768]{2,1,0:T(8,128)(2,1)}, u32[]{:S(2)}) copy-start(bf16[48,48,768]{2,1,0:T(8,128)(2,1)} %multiply_convert_fusion) | copy-start | bytes 10616836
  65.5 9.1 %collective-permute-start.11 = (bf16[48,16,128]{2,1,0:T(8,128)(2,1)S(1)}, bf16[48,16,128]{2,1,0:T(8,128)(2,1)S(1)}, u32[]{:S(2)}, u32[]{:S(2)}) collective-permute-start(bf16[48,16,128]{2,1,0:T(8,128)(2,1)S(1)} %pad_maximum_fusion.3), channel_id=1, source_target_pairs={{32,0},{64,32},{96,64},{128,96},{160,128},{192,160},{224,192},{0,2... | collective-permute-start | bytes 589832 | tf_op jit(solution)/shard_map/ppermute | solution.py:232
  65.7 9.1 %collective-permute-start.7 = (bf16[48,16,128]{2,1,0:T(8,128)(2,1)S(1)}, bf16[48,16,128]{2,1,0:T(8,128)(2,1)S(1)}, u32[]{:S(2)}, u32[]{:S(2)}) collective-permute-start(bf16[48,16,128]{2,1,0:T(8,128)(2,1)S(1)} %pad_maximum_fusion.2), channel_id=1, source_target_pairs={{0,32},{32,64},{64,96},{96,128},{128,160},{160,192},{192,224},{224... | collective-permute-start | bytes 589832 | tf_op jit(solution)/shard_map/ppermute | solution.py:232
  69.1 9.8 %collective-permute-start.21 = (bf16[48,16,128]{2,1,0:T(8,128)(2,1)S(1)}, bf16[48,16,128]{2,1,0:T(8,128)(2,1)S(1)}, u32[]{:S(2)}, u32[]{:S(2)}) collective-permute-start(bf16[48,16,128]{2,1,0:T(8,128)(2,1)S(1)} %pad_maximum_fusion.5), channel_id=1, source_target_pairs={{32,0},{64,32},{96,64},{128,96},{160,128},{192,160},{224,192},{0,2... | collective-permute-start | bytes 589832 | tf_op jit(solution)/shard_map/ppermute | solution.py:232
  69.2 9.8 %collective-permute-start.17 = (bf16[48,16,128]{2,1,0:T(8,128)(2,1)S(1)}, bf16[48,16,128]{2,1,0:T(8,128)(2,1)S(1)}, u32[]{:S(2)}, u32[]{:S(2)}) collective-permute-start(bf16[48,16,128]{2,1,0:T(8,128)(2,1)S(1)} %pad_maximum_fusion.4), channel_id=1, source_target_pairs={{0,32},{32,64},{64,96},{96,128},{128,160},{160,192},{192,224},{224... | collective-permute-start | bytes 589832 | tf_op jit(solution)/shard_map/ppermute | solution.py:232
  74.7 8.3 %collective-permute-start.12 = (bf16[48,16,128]{2,1,0:T(8,128)(2,1)S(1)}, bf16[48,16,128]{2,1,0:T(8,128)(2,1)S(1)}, u32[]{:S(2)}, u32[]{:S(2)}) collective-permute-start(bf16[48,16,128]{2,1,0:T(8,128)(2,1)S(1)} %add_convert_fusion.5), channel_id=1, source_target_pairs={{32,0},{64,32},{96,64},{128,96},{160,128},{192,160},{224,192},{0,2... | collective-permute-start | bytes 589832 | tf_op jit(solution)/shard_map/ppermute | solution.py:232
  74.8 8.5 %collective-permute-start.8 = (bf16[48,16,128]{2,1,0:T(8,128)(2,1)S(1)}, bf16[48,16,128]{2,1,0:T(8,128)(2,1)S(1)}, u32[]{:S(2)}, u32[]{:S(2)}) collective-permute-start(bf16[48,16,128]{2,1,0:T(8,128)(2,1)S(1)} %add_convert_fusion.7), channel_id=1, source_target_pairs={{0,32},{32,64},{64,96},{96,128},{128,160},{160,192},{192,224},{224... | collective-permute-start | bytes 589832 | tf_op jit(solution)/shard_map/ppermute | solution.py:232
  78.9 9.1 %collective-permute-start.22 = (bf16[48,16,128]{2,1,0:T(8,128)(2,1)S(1)}, bf16[48,16,128]{2,1,0:T(8,128)(2,1)S(1)}, u32[]{:S(2)}, u32[]{:S(2)}) collective-permute-start(bf16[48,16,128]{2,1,0:T(8,128)(2,1)S(1)} %add_convert_fusion.1), channel_id=1, source_target_pairs={{32,0},{64,32},{96,64},{128,96},{160,128},{192,160},{224,192},{0,2... | collective-permute-start | bytes 589832 | tf_op jit(solution)/shard_map/ppermute | solution.py:232
  79.1 9.1 %collective-permute-start.18 = (bf16[48,16,128]{2,1,0:T(8,128)(2,1)S(1)}, bf16[48,16,128]{2,1,0:T(8,128)(2,1)S(1)}, u32[]{:S(2)}, u32[]{:S(2)}) collective-permute-start(bf16[48,16,128]{2,1,0:T(8,128)(2,1)S(1)} %add_convert_fusion.3), channel_id=1, source_target_pairs={{0,32},{32,64},{64,96},{96,128},{128,160},{160,192},{192,224},{224... | collective-permute-start | bytes 589832 | tf_op jit(solution)/shard_map/ppermute | solution.py:232
  83.0 8.5 %collective-permute-start.13 = (bf16[48,16,128]{2,1,0:T(8,128)(2,1)S(1)}, bf16[48,16,128]{2,1,0:T(8,128)(2,1)S(1)}, u32[]{:S(2)}, u32[]{:S(2)}) collective-permute-start(bf16[48,16,128]{2,1,0:T(8,128)(2,1)S(1)} %add_convert_fusion.4), channel_id=1, source_target_pairs={{32,0},{64,32},{96,64},{128,96},{160,128},{192,160},{224,192},{0,2... | collective-permute-start | bytes 589832 | tf_op jit(solution)/shard_map/ppermute | solution.py:232
  83.4 8.1 %collective-permute-start.9 = (bf16[48,16,128]{2,1,0:T(8,128)(2,1)S(1)}, bf16[48,16,128]{2,1,0:T(8,128)(2,1)S(1)}, u32[]{:S(2)}, u32[]{:S(2)}) collective-permute-start(bf16[48,16,128]{2,1,0:T(8,128)(2,1)S(1)} %add_convert_fusion.6), channel_id=1, source_target_pairs={{0,32},{32,64},{64,96},{96,128},{128,160},{160,192},{192,224},{224... | collective-permute-start | bytes 589832 | tf_op jit(solution)/shard_map/ppermute | solution.py:232
  88.1 7.0 %collective-permute-start.23 = (bf16[48,16,128]{2,1,0:T(8,128)(2,1)S(1)}, bf16[48,16,128]{2,1,0:T(8,128)(2,1)S(1)}, u32[]{:S(2)}, u32[]{:S(2)}) collective-permute-start(bf16[48,16,128]{2,1,0:T(8,128)(2,1)S(1)} %add_convert_fusion), channel_id=1, source_target_pairs={{32,0},{64,32},{96,64},{128,96},{160,128},{192,160},{224,192},{0,2... | collective-permute-start | bytes 589832 | tf_op jit(solution)/shard_map/ppermute | solution.py:232
  88.2 6.8 %collective-permute-start.19 = (bf16[48,16,128]{2,1,0:T(8,128)(2,1)S(1)}, bf16[48,16,128]{2,1,0:T(8,128)(2,1)S(1)}, u32[]{:S(2)}, u32[]{:S(2)}) collective-permute-start(bf16[48,16,128]{2,1,0:T(8,128)(2,1)S(1)} %add_convert_fusion.2), channel_id=1, source_target_pairs={{0,32},{32,64},{64,96},{96,128},{128,160},{160,192},{192,224},{224... | collective-permute-start | bytes 589832 | tf_op jit(solution)/shard_map/ppermute | solution.py:232
  91.9 6.1 %collective-permute-start.15 = (bf16[96,128]{1,0:T(8,128)(2,1)S(1)}, bf16[96,128]{1,0:T(8,128)(2,1)S(1)}, u32[]{:S(2)}, u32[]{:S(2)}) collective-permute-start(bf16[96,128]{1,0:T(8,128)(2,1)S(1)} %get-tuple-element.120), channel_id=1, source_target_pairs={{0,1},{1,0},{2,3},{3,2},{4,5},{5,4},{6,7},{7,6},{8,9},{9,8},{10,11... | collective-permute-start | bytes 73736 | tf_op jit(solution)/shard_map/ppermute | solution.py:25
  92.0 6.0 %collective-permute-start.14 = (bf16[96,128]{1,0:T(8,128)(2,1)S(1)}, bf16[96,128]{1,0:T(8,128)(2,1)S(1)}, u32[]{:S(2)}, u32[]{:S(2)}) collective-permute-start(bf16[96,128]{1,0:T(8,128)(2,1)S(1)} %get-tuple-element.121), channel_id=1, source_target_pairs={{1,2},{2,1},{5,6},{6,5},{9,10},{10,9},{13,14},{14,13},{17,18},{18,... | collective-permute-start | bytes 73736 | tf_op jit(solution)/shard_map/ppermute | solution.py:25
  95.4 4.2 %collective-permute-start.25 = (bf16[96,128]{1,0:T(8,128)(2,1)S(1)}, bf16[96,128]{1,0:T(8,128)(2,1)S(1)}, u32[]{:S(2)}, u32[]{:S(2)}) collective-permute-start(bf16[96,128]{1,0:T(8,128)(2,1)S(1)} %get-tuple-element.116), channel_id=1, source_target_pairs={{0,1},{1,0},{2,3},{3,2},{4,5},{5,4},{6,7},{7,6},{8,9},{9,8},{10,11... | collective-permute-start | bytes 73736 | tf_op jit(solution)/shard_map/ppermute | solution.py:25
  95.5 5.1 %collective-permute-start.24 = (bf16[96,128]{1,0:T(8,128)(2,1)S(1)}, bf16[96,128]{1,0:T(8,128)(2,1)S(1)}, u32[]{:S(2)}, u32[]{:S(2)}) collective-permute-start(bf16[96,128]{1,0:T(8,128)(2,1)S(1)} %get-tuple-element.117), channel_id=1, source_target_pairs={{1,2},{2,1},{5,6},{6,5},{9,10},{10,9},{13,14},{14,13},{17,18},{18,... | collective-permute-start | bytes 73736 | tf_op jit(solution)/shard_map/ppermute | solution.py:25
  102.2 22.6 %copy-start.6 = (f32[16,16,128]{2,1,0:T(8,128)S(1)}, f32[16,16,128]{2,1,0:T(8,128)}, u32[]{:S(2)}) copy-start(f32[16,16,128]{2,1,0:T(8,128)} %param.9) | copy-start | bytes 393220
  102.3 9.1 %collective-permute-start.27 = (f16[16,48,128]{2,1,0:T(8,128)(2,1)S(1)}, f16[16,48,128]{2,1,0:T(8,128)(2,1)S(1)}, u32[]{:S(2)}, u32[]{:S(2)}) collective-permute-start(f16[16,48,128]{2,1,0:T(8,128)(2,1)S(1)} %bitcast.118), channel_id=1, source_target_pairs={{32,64},{64,32},{96,128},{128,96},{160,192},{192,160},{33,65},{65,... | collective-permute-start | bytes 589832 | tf_op jit(solution)/shard_map/ppermute | solution.py:25
  107.7 5.8 %collective-permute-start.26 = (f16[16,48,128]{2,1,0:T(8,128)(2,1)S(1)}, f16[16,48,128]{2,1,0:T(8,128)(2,1)S(1)}, u32[]{:S(2)}, u32[]{:S(2)}) collective-permute-start(f16[16,48,128]{2,1,0:T(8,128)(2,1)S(1)} %bitcast.117), channel_id=1, source_target_pairs={{0,32},{32,0},{64,96},{96,64},{128,160},{160,128},{192,224},{224,1... | collective-permute-start | bytes 589832 | tf_op jit(solution)/shard_map/ppermute | solution.py:25
  113.6 6.6 %collective-permute-start.28 = (f16[16,16,128]{2,1,0:T(8,128)(2,1)S(1)}, f16[16,16,128]{2,1,0:T(8,128)(2,1)S(1)}, u32[]{:S(2)}, u32[]{:S(2)}) collective-permute-start(f16[16,16,128]{2,1,0:T(8,128)(2,1)S(1)} %get-tuple-element.106), channel_id=1, source_target_pairs={{0,4},{4,0},{8,12},{12,8},{16,20},{20,16},{24,28},{28,24},{1,5},{5... | collective-permute-start | bytes 196616 | tf_op jit(solution)/shard_map/ppermute | solution.py:25
  116.2 8.6 %collective-permute-start.29 = (f16[16,16,128]{2,1,0:T(8,128)(2,1)S(1)}, f16[16,16,128]{2,1,0:T(8,128)(2,1)S(1)}, u32[]{:S(2)}, u32[]{:S(2)}) collective-permute-start(f16[16,16,128]{2,1,0:T(8,128)(2,1)S(1)} %get-tuple-element.107), channel_id=1, source_target_pairs={{4,8},{8,4},{12,16},{16,12},{20,24},{24,20},{5,9},{9,5},{13,17},{1... | collective-permute-start | bytes 196616 | tf_op jit(solution)/shard_map/ppermute | solution.py:25
